TPU v7x, 512 devices: a whole 4x8x8 slice. The times are simulated.
512 devices in a mesh: seq: 128 (over z, y, core), chan: 4 (over x).
Axes of the slice: x: 4, y: 8, z: 8, core: 2. Of those that a mesh axis runs over, the one named last changes fastest.
Arguments:
- values: bfloat16 [160, 128, 4096], P(None, 'seq', 'chan'), may hold values from -6 to 6
- gates: bfloat16 [160, 128, 4096], P(None, 'seq', 'chan'), may hold values from -6 to 6
- filters: bfloat16 [256, 4096], P(None, 'chan'), may hold values from -1.1 to 1.1
- skip: float32 [4096], P('chan'), may hold values from -1 to 1
- weights: bfloat16 [4096, 4096], P(None, ('chan', 'seq')), may hold values from -0.09375 to 0.09375
- doc_lengths: int32 [128], replicated, may hold values from 1 to 256, 20480 in all
Outputs:
- mixed: bfloat16 [160, 128, 4096], P(None, 'seq', 'chan')
Inputs may be any that keep to these rules, and one draw needn't show every extreme that they name: `doc_lengths`: the 128 documents lie in order and together fill the 20480 rows of the window; the longest has exactly 256 rows.
All inputs are finite; a program needn't handle non-finite values.
Results may differ from a plain program's by a relative error of at most 0.0057.
Values may be sent and summed in bfloat16 or wider, within the bound.
No kernel may reach another device: no remote copies, remote signals or barrier semaphores. Data moves between devices by JAX's collectives and lax.ppermute only.
A program may use at most 64 MiB of HBM per device.

v0:
```python
import functools

import jax
import jax.numpy as jnp
from jax import lax
from jax.experimental import pallas as pl
from jax.experimental.pallas import tpu as pltpu
from jax.sharding import Mesh
from jax.sharding import PartitionSpec as P

F32 = jnp.float32
BF16 = jnp.bfloat16
LANES = 128
CH = 8
ROWS = 160
HEAD = 128
TAIL = ROWS - HEAD
FOLD = LANES // TAIL
PER = CH + CH // FOLD
PEERS = 128
MSG = PEERS * PER
VMEM_LIMIT = 48 * 1024 * 1024
SEQ = ("z", "y", "core")


def full(shape):
    return pl.BlockSpec(shape, lambda: (0,) * len(shape))


def call(kernel, out, ins, scratch, flops=0, smem=0):
    args = ins
    in_specs = [pl.BlockSpec(memory_space=pltpu.SMEM)] * smem
    in_specs += [full(a.shape) for a in args[smem:]]
    nbytes = sum(a.size * a.dtype.itemsize for a in args)
    nbytes += out.size * out.dtype.itemsize
    return pl.pallas_call(
        kernel,
        out_shape=out,
        in_specs=in_specs,
        out_specs=full(out.shape),
        scratch_shapes=scratch,
        compiler_params=pltpu.CompilerParams(vmem_limit_bytes=VMEM_LIMIT),
        cost_estimate=pl.CostEstimate(flops=flops, bytes_accessed=nbytes, transcendentals=0),
    )(*args)


def pack_kernel(v_ref, out_ref, msg, low):
    for j in range(8):
        cols = slice(j * LANES, (j + 1) * LANES)
        block = v_ref[:, cols].astype(F32)
        head = block[:HEAD].T
        for g in range(16):
            msg[pl.ds((16 * j + g) * PER, CH), :] = head[g * CH : (g + 1) * CH]
        low[cols, :TAIL] = block[HEAD:].T
    for i in range(CH // FOLD):
        parts = [low[pl.ds(FOLD * i + k, PEERS, stride=CH), :][:, :TAIL] for k in range(FOLD)]
        msg[pl.ds(CH + i, PEERS, stride=PER), :] = jnp.concatenate(parts, axis=1)
    out_ref[...] = msg[...].astype(BF16)


def toeplitz_kernel(index_ref, f_ref, out_ref, taps):
    group = index_ref[0]
    tile = pl.multiple_of(lax.div(group, 16) * LANES, LANES)
    taps[...] = f_ref[:, pl.ds(tile, LANES)].astype(F32).T
    mine = taps[pl.ds(pl.multiple_of(lax.rem(group, 16) * CH, CH), CH), :]
    row = lax.broadcasted_iota(jnp.int32, (LANES, LANES), 0)
    lane = lax.broadcasted_iota(jnp.int32, (LANES, LANES), 1)
    for c in range(CH):
        spread = jnp.broadcast_to(mine[c : c + 1, :], (LANES, 2 * LANES))
        turned = pltpu.roll(spread, 0, 1, stride=1, stride_axis=0)
        near = jnp.where(lane >= row, turned[:, :LANES], 0.0).astype(BF16)
        out_ref[c, :LANES, :LANES] = near
        out_ref[c, LANES:, LANES:] = near
        out_ref[c, :LANES, LANES:] = turned[:, LANES:].astype(BF16)
        out_ref[c, LANES:, :LANES] = jnp.zeros((LANES, LANES), BF16)


def conv_kernel(start_ref, length_ref, skip_ref, in_ref, toep_ref, out_ref, msg, seq, result, first, second):
    msg[...] = in_ref[...].astype(F32)
    for c in range(CH):
        seq[pl.ds(c, HEAD, stride=CH), :] = msg[pl.ds(c, PEERS, stride=PER), :].T
    for i in range(CH // FOLD):
        tail = msg[pl.ds(CH + i, PEERS, stride=PER), :].T
        for k in range(FOLD):
            seq[pl.ds(HEAD * CH + FOLD * i + k, TAIL, stride=CH), :] = tail[k * TAIL : (k + 1) * TAIL]
    result[...] = jnp.zeros_like(result)
    lane = lax.broadcasted_iota(jnp.int32, (CH, LANES), 1)

    def take(d, carry):
        begin, length = start_ref[d], length_ref[d]
        row = pl.multiple_of(lax.shift_right_logical(begin, 7) * CH, CH)
        turn = begin & (LANES - 1)
        back = (LANES - turn) & (LANES - 1)
        pieces = [pltpu.roll(seq[pl.ds(row + CH * i, CH), :], back, 1) for i in range(3)]
        whole = lane < LANES - turn
        near = jnp.where(whole, pieces[0], pieces[1])
        far = jnp.where(whole, pieces[1], pieces[2])
        first[pl.ds(d, CH, stride=PEERS), :] = jnp.where(lane < length, near, 0.0)
        second[pl.ds(d, CH, stride=PEERS), :] = jnp.where(lane < length - LANES, far, 0.0)
        return carry

    lax.fori_loop(0, PEERS, take, 0, unroll=8)
    for c in range(CH):
        rows = slice(c * PEERS, (c + 1) * PEERS)
        near, far = first[rows, :], second[rows, :]
        both = jnp.concatenate([near, far], axis=1).astype(BF16)
        done = jnp.dot(both, toep_ref[c], preferred_element_type=F32)
        gain = skip_ref[c]
        first[rows, :] = (done[:, :LANES] + gain * near).astype(BF16).astype(F32)
        second[rows, :] = (done[:, LANES:] + gain * far).astype(BF16).astype(F32)

    def give(d, carry):
        begin, length = start_ref[d], length_ref[d]
        row = pl.multiple_of(lax.shift_right_logical(begin, 7) * CH, CH)
        turn = begin & (LANES - 1)
        near = jnp.where(lane < length, first[pl.ds(d, CH, stride=PEERS), :], 0.0)
        far = jnp.where(lane < length - LANES, second[pl.ds(d, CH, stride=PEERS), :], 0.0)
        near = pltpu.roll(near, turn, 1)
        far = pltpu.roll(far, turn, 1)
        whole = lane >= turn
        result[pl.ds(row, CH), :] += jnp.where(whole, near, 0.0)
        result[pl.ds(row + CH, CH), :] += jnp.where(whole, far, near)
        result[pl.ds(row + 2 * CH, CH), :] += jnp.where(whole, 0.0, far)
        return carry

    lax.fori_loop(0, PEERS, give, 0, unroll=8)
    for c in range(CH):
        msg[pl.ds(c, PEERS, stride=PER), :] = result[pl.ds(c, HEAD, stride=CH), :].T
    for i in range(CH // FOLD):
        parts = [result[pl.ds(HEAD * CH + FOLD * i + k, TAIL, stride=CH), :] for k in range(FOLD)]
        msg[pl.ds(CH + i, PEERS, stride=PER), :] = jnp.concatenate(parts, axis=0).T
    out_ref[...] = msg[...].astype(BF16)


def gate_kernel(in_ref, g_ref, out_ref, msg, low):
    msg[...] = in_ref[...].astype(F32)
    for i in range(CH // FOLD):
        tail = msg[pl.ds(CH + i, PEERS, stride=PER), :]
        for k in range(FOLD):
            low[pl.ds(FOLD * i + k, PEERS, stride=CH), :TAIL] = tail[:, k * TAIL : (k + 1) * TAIL]
    for j in range(8):
        cols = slice(j * LANES, (j + 1) * LANES)
        head = [msg[pl.ds((16 * j + g) * PER, CH), :] for g in range(16)]
        head = jnp.concatenate(head, axis=0).T
        out_ref[:HEAD, cols] = (head * g_ref[:HEAD, cols].astype(F32)).astype(BF16)
        tail = low[cols, :].T[:TAIL]
        out_ref[HEAD:, cols] = (tail * g_ref[HEAD:, cols].astype(F32)).astype(BF16)


def exchange(message):
    sent = message.reshape(PEERS, PER // 2, 2, LANES)
    got = lax.all_to_all(sent, SEQ, split_axis=0, concat_axis=0, tiled=True)
    return got.reshape(MSG, LANES)


def local(values, gates, filters, skip, weights, doc_lengths):
    index = lax.axis_index(SEQ).astype(jnp.int32)
    width = values.shape[2]
    msg = jax.ShapeDtypeStruct((MSG, LANES), BF16)
    buf = pltpu.VMEM((MSG, LANES), F32)
    low = pltpu.VMEM((width, LANES), F32)
    packed = call(pack_kernel, msg, [values.reshape(ROWS, width)], [buf, low])
    toep = call(
        toeplitz_kernel,
        jax.ShapeDtypeStruct((CH, 2 * LANES, 2 * LANES), BF16),
        [index[None], filters],
        [pltpu.VMEM((LANES, 2 * LANES), F32)],
        smem=1,
    )
    starts = jnp.cumsum(doc_lengths) - doc_lengths
    own_skip = lax.dynamic_slice(skip, (index * CH,), (CH,))
    got = exchange(packed)
    convolved = call(
        conv_kernel,
        msg,
        [starts, doc_lengths, own_skip, got, toep],
        [
            buf,
            pltpu.VMEM((MSG + 3 * CH, LANES), F32),
            pltpu.VMEM((MSG + 3 * CH, LANES), F32),
            pltpu.VMEM((CH * PEERS, LANES), F32),
            pltpu.VMEM((CH * PEERS, LANES), F32),
        ],
        flops=2 * CH * PEERS * 256 * 256,
        smem=3,
    )
    back = exchange(convolved)
    gated = call(
        gate_kernel,
        jax.ShapeDtypeStruct((ROWS, width), BF16),
        [back, gates.reshape(ROWS, width)],
        [buf, low],
    )
    return project(gated, weights, index)


def project(gated, weights, index):
    half = gated.shape[1] // 2
    parts = [lax.all_gather(gated[:, a : a + half], "chan", axis=0) for a in (0, half)]
    rows = jnp.concatenate(parts, axis=2)
    rows = jnp.swapaxes(rows, 0, 1).reshape(ROWS, -1)
    table = lax.all_gather(weights.T, SEQ, axis=0, tiled=True)
    mixed = lax.dot_general(rows, table, (((1,), (1,)), ((), ())), preferred_element_type=F32)
    return mixed.astype(BF16)[:, None, :]


def solution(mesh):
    shape = dict(z=8, y=8, core=2, chan=4)
    fine = Mesh(mesh.devices.reshape(tuple(shape.values())), tuple(shape))
    placed = (
        P(None, SEQ, "chan"),
        P(None, SEQ, "chan"),
        P(None, "chan"),
        P("chan"),
        P(None, ("chan",) + SEQ),
        P(),
    )
    return jax.shard_map(
        local, mesh=fine, in_specs=placed, out_specs=P(None, SEQ, "chan"), check_vma=False
    )
```

profile of v0, /device:TPU:1, one launch (start us, length us, event | category | flops | bytes accessed | tf_op | source)
XLA Modules:
  0.0 123.8 jit_solution(1353072602384279303)
XLA Ops:
  6.5 0.0 copy-start
  6.5 0.0 all-gather.4.cloned.1.call-start
  6.5 0.7 all-gather.4.cloned.1.call-update
  7.3 0.0 copy-start.1
  7.3 1.0 copy-done.1
  8.2 0.0 copy-start.3
  8.2 1.1 shard_map.64
  9.4 18.4 %all-to-all-start = ((bf16[128,5,2,128]{3,2,1,0:T(2,128)(2,1)}), bf16[128,5,2,128]{3,2,1,0:T(2,128)(2,1)S(1)}, u32[]{:S(2)}, u32[]{:S(2)}) async-start(bf16[128,5,2,128]{3,2,1,0:T(2,128)(2,1)} %bitcast.2), calls=%async_computation | async-start | bytes 655360 | tf_op jit(solution)/shard_map/all_to_all | solution.py:152
  27.8 0.0 copy-done.3
  27.8 0.1 copy.8
  27.9 0.2 reduce-window.9
  28.1 0.1 reduce
  28.2 0.8 dynamic_slice.3.skip_ref
  29.0 0.0 copy-done
  29.0 0.4 shard_map.65.toep_ref
  29.4 0.0 copy-start.2
  29.4 15.4 %all-to-all-done = bf16[128,5,2,128]{3,2,1,0:T(2,128)(2,1)S(1)} async-done(((bf16[128,5,2,128]{3,2,1,0:T(2,128)(2,1)}), bf16[128,5,2,128]{3,2,1,0:T(2,128)(2,1)S(1)}, u32[]{:S(2)}, u32[]{:S(2)}) %all-to-all-start) | async-done | bytes 327712 | tf_op jit(solution)/shard_map/all_to_all | solution.py:152
  44.7 5.4 %shard_map.66 = bf16[1280,128]{1,0:T(8,128)(2,1)S(1)} custom-call(s32[128]{0:T(128)S(1)} %sub.3.start_ref, s32[128]{0:T(128)S(1)} %copy-done.3, f32[8]{0:T(128)S(1)} %dynamic_slice.3.skip_ref, bf16[1280,128]{1,0:T(8,128)(2,1)S(1)} %bitcast.18, bf16[8,256,256]{2,1,0:T(8,128)(2,1)S(1)} %shard_map.65.toep_ref), custom_call_target="tpu_custom_call" | custom-call | flops 134217728 | bytes 1704992 | tf_op jit(solution)/shard_map/pallas_call | solution.py:36
  50.1 21.6 %all_to_all.10 = bf16[128,5,2,128]{3,2,1,0:T(2,128)(2,1)S(1)} all-to-all(bf16[128,5,2,128]{3,2,1,0:T(2,128)(2,1)S(1)} %bitcast.19), channel_id=1, replica_groups=mesh['z'=8,'y'=8,'core'=2,'chan'=4] {'z','y','core'}, dimensions={0} | all-to-all | bytes 655360 | tf_op jit(solution)/shard_map/all_to_all | solution.py:152
  71.7 0.0 copy-done.2
  71.7 0.4 shard_map.67
  72.1 11.5 %all-gather.1 = bf16[640,512]{1,0:T(8,128)(2,1)S(1)} all-gather(bf16[160,512]{1,0:T(8,128)(2,1)S(1)} %get-tuple-element.6), channel_id=3, replica_groups=mesh['z'=8,'y'=8,'core'=2,'chan'=4] {'chan'}, dimensions={0}, use_global_device_ids=true | all-gather | bytes 819200 | tf_op jit(solution)/shard_map/all_gather | solution.py:199
  83.6 0.5 copy.10
  84.1 11.2 %all-gather = bf16[640,512]{1,0:T(8,128)(2,1)S(1)} all-gather(bf16[160,512]{1,0:T(8,128)(2,1)S(1)} %get-tuple-element.5), channel_id=2, replica_groups=mesh['z'=8,'y'=8,'core'=2,'chan'=4] {'chan'}, dimensions={0}, use_global_device_ids=true | all-gather | bytes 819200 | tf_op jit(solution)/shard_map/all_gather | solution.py:199
  95.3 0.5 copy.9
  95.8 0.6 pad_maximum_fusion
  96.4 0.5 copy.11
  96.9 13.1 %all-gather.4.cloned.1.call-done = bf16[1024,4096]{1,0:T(8,128)(2,1)} async-done(((bf16[8,4096]{1,0:T(8,128)(2,1)}), bf16[1024,4096]{1,0:T(8,128)(2,1)}) %all-gather.4.cloned.1.call-update) | async-done | bytes 8388624 | tf_op jit(solution)/shard_map/all_gather | solution.py:202
  110.0 7.0 %fusion = bf16[160,1,1024]{2,0,1:T(8,128)(2,1)} fusion(bf16[160,4096]{1,0:T(8,128)(2,1)S(1)} %bitcast.24, bf16[1024,4096]{1,0:T(8,128)(2,1)} %all-gather.4.cloned.1.call-done), kind=kOutput, calls=%fused_computation.2 | convolution fusion | flops 1342341120 | bytes 10027008 | tf_op jit(solution)/shard_map/dot_general | solution.py:203
  (2 shorter events, 0.0 us)
Async XLA Ops:
  6.5 22.5 %copy-start = (bf16[256,1024]{1,0:T(8,128)(2,1)S(1)}, bf16[256,1024]{1,0:T(8,128)(2,1)}, u32[]{:S(2)}) copy-start(bf16[256,1024]{1,0:T(8,128)(2,1)} %f_ref.1) | copy-start | bytes 1572868
  6.5 103.4 %all-gather.4.cloned.1.call-start = ((), (), s32[]{:S(2)}) async-start(), calls=%async_computation.2 | async-start | bytes 8454144 | tf_op jit(solution)/shard_map/all_gather | solution.py:202
  7.3 1.0 copy-start.1
  8.2 19.6 %copy-start.3 = (s32[128]{0:T(128)S(1)}, s32[128]{0:T(128)}, u32[]{:S(2)}) copy-start(s32[128]{0:T(128)} %length_ref.1) | copy-start | bytes 1540
  9.4 35.4 %all-to-all-start = ((bf16[128,5,2,128]{3,2,1,0:T(2,128)(2,1)}), bf16[128,5,2,128]{3,2,1,0:T(2,128)(2,1)S(1)}, u32[]{:S(2)}, u32[]{:S(2)}) async-start(bf16[128,5,2,128]{3,2,1,0:T(2,128)(2,1)} %bitcast.2), calls=%async_computation | async-start | bytes 655360 | tf_op jit(solution)/shard_map/all_to_all | solution.py:152
  29.4 42.4 %copy-start.2 = (bf16[160,1,1024]{2,0,1:T(8,128)(2,1)S(1)}, bf16[160,1,1024]{2,0,1:T(8,128)(2,1)}, u32[]{:S(2)}) copy-start(bf16[160,1,1024]{2,0,1:T(8,128)(2,1)} %param.7) | copy-start | bytes 983044
Sparse Core Ops, SparseCore 0:
  10.5 99.4 all-gather.3
where the time goes:
time: 124 us
  blocking collectives  44.2 us (36%)
  waiting for transfers between devices  29.1 us (23%)
  starting transfers between devices  18.4 us (15%)
  between operations  13.5 us (11%)
  Pallas kernels  7.28 us (6%)
  matrix products  7.01 us (6%)
  local copies, waits for them, and re-layouts  3.41 us (3%)
    all_gather x2, blocking collectives, project(): lax.all_gather(gated[:, a:a + half], 'chan', axis=0)  22.6 us
    all_to_all x1, blocking collectives, exchange(): got = lax.all_to_all(sent, SEQ, split_axis=0, concat_axis=0, tiled=True)  21.6 us
    all_to_all x1, starting transfers between devices, exchange(): got = lax.all_to_all(sent, SEQ, split_axis=0, concat_axis=0, tiled=True)  18.4 us
    all_to_all x1, waiting for transfers between devices, exchange(): got = lax.all_to_all(sent, SEQ, split_axis=0, concat_axis=0, tiled=True)  15.4 us
    all_gather x1, waiting for transfers between devices, project(): table = lax.all_gather(weights.T, SEQ, axis=0, tiled=True)  13.1 us
    pallas_call x4, Pallas kernels, call(): pl.pallas_call(kernel, out_shape=out, in_specs=in_specs, out_specs=full(o...  7.28 us
    dot_general x1, matrix products, project(): lax.dot_general(rows, table, (((1,), (1,)), ((), ())), preferred_element_...  7.01 us
  transfers between devices with their start and end apart: 2, of which 2 were waited for; matrix products, arithmetic and copies ran while one was open for 3% of the time, Pallas kernels for 6%

commit v1 on v0

--- a/solution.py
+++ b/solution.py
@@ -5,7 +5,6 @@
 from jax import lax
 from jax.experimental import pallas as pl
 from jax.experimental.pallas import tpu as pltpu
-from jax.sharding import Mesh
 from jax.sharding import PartitionSpec as P
 
 F32 = jnp.float32
@@ -20,7 +19,7 @@
 PEERS = 128
 MSG = PEERS * PER
 VMEM_LIMIT = 48 * 1024 * 1024
-SEQ = ("z", "y", "core")
+SEQ = "seq"
 
 
 def full(shape):
@@ -142,9 +141,40 @@
         cols = slice(j * LANES, (j + 1) * LANES)
         head = [msg[pl.ds((16 * j + g) * PER, CH), :] for g in range(16)]
         head = jnp.concatenate(head, axis=0).T
-        out_ref[:HEAD, cols] = (head * g_ref[:HEAD, cols].astype(F32)).astype(BF16)
+        head = (head * g_ref[:HEAD, cols].astype(F32)).astype(BF16)
         tail = low[cols, :].T[:TAIL]
-        out_ref[HEAD:, cols] = (tail * g_ref[HEAD:, cols].astype(F32)).astype(BF16)
+        tail = (tail * g_ref[HEAD:, cols].astype(F32)).astype(BF16)
+        for q in range(out_ref.shape[0]):
+            out_ref[q, :HEAD, cols] = head
+            out_ref[q, HEAD:, cols] = tail
+
+
+def multiply(rows_ref, w_ref):
+    groups, _, width = rows_ref.shape
+    total = jnp.zeros((w_ref.shape[0], ROWS), F32)
+    for q in range(groups):
+        part = w_ref[:, q * width : (q + 1) * width]
+        total += lax.dot_general(part, rows_ref[q], (((1,), (1,)), ((), ())), preferred_element_type=F32)
+    return total
+
+
+def own_kernel(rows_ref, w_ref, out_ref):
+    out_ref[...] = multiply(rows_ref, w_ref)
+
+
+def other_kernel(core_ref, rows_ref, w_ref, own_ref, out_ref, zy, yz):
+    other = multiply(rows_ref, w_ref)
+    own_first = core_ref[0] == 0
+    own = own_ref[...]
+    zy[...] = jnp.where(own_first, own, other)
+    yz[...] = jnp.where(own_first, other, own)
+    for z in range(8):
+        parts = []
+        for y in range(8):
+            parts.append(zy[(8 * z + y) * 8 : (8 * z + y + 1) * 8, :])
+            parts.append(yz[(8 * y + z) * 8 : (8 * y + z + 1) * 8, :])
+        block = jnp.concatenate(parts, axis=0)
+        out_ref[:, z * LANES : (z + 1) * LANES] = block.T.astype(BF16)
 
 
 def exchange(message):
@@ -159,7 +189,9 @@
     msg = jax.ShapeDtypeStruct((MSG, LANES), BF16)
     buf = pltpu.VMEM((MSG, LANES), F32)
     low = pltpu.VMEM((width, LANES), F32)
+    line = gather_line(weights.T)
     packed = call(pack_kernel, msg, [values.reshape(ROWS, width)], [buf, low])
+    packed, filters, doc_lengths, skip = lax.optimization_barrier((packed, filters, doc_lengths, skip))
     toep = call(
         toeplitz_kernel,
         jax.ShapeDtypeStruct((CH, 2 * LANES, 2 * LANES), BF16),
@@ -169,7 +201,10 @@
     )
     starts = jnp.cumsum(doc_lengths) - doc_lengths
     own_skip = lax.dynamic_slice(skip, (index * CH,), (CH,))
-    got = exchange(packed)
+    got, line, toep, starts, own_skip = lax.optimization_barrier(
+        (exchange(packed), line, toep, starts, own_skip)
+    )
+    own = lax.all_gather(line, "seq", axis=0, axis_index_groups=lines("z"), tiled=True)
     convolved = call(
         conv_kernel,
         msg,
@@ -184,37 +219,56 @@
         flops=2 * CH * PEERS * 256 * 256,
         smem=3,
     )
-    back = exchange(convolved)
-    gated = call(
+    back, own = lax.optimization_barrier((exchange(convolved), own))
+    other = lax.ppermute(own, "seq", [(i, i ^ 1) for i in range(PEERS)])
+    groups = lax.axis_size("chan")
+    copies = call(
         gate_kernel,
-        jax.ShapeDtypeStruct((ROWS, width), BF16),
+        jax.ShapeDtypeStruct((groups, ROWS, width), BF16),
         [back, gates.reshape(ROWS, width)],
         [buf, low],
     )
-    return project(gated, weights, index)
-
-
-def project(gated, weights, index):
-    half = gated.shape[1] // 2
-    parts = [lax.all_gather(gated[:, a : a + half], "chan", axis=0) for a in (0, half)]
-    rows = jnp.concatenate(parts, axis=2)
-    rows = jnp.swapaxes(rows, 0, 1).reshape(ROWS, -1)
-    table = lax.all_gather(weights.T, SEQ, axis=0, tiled=True)
-    mixed = lax.dot_general(rows, table, (((1,), (1,)), ((), ())), preferred_element_type=F32)
-    return mixed.astype(BF16)[:, None, :]
+    rows = lax.all_to_all(copies, "chan", split_axis=0, concat_axis=0, tiled=True)
+    half = jax.ShapeDtypeStruct((own.shape[0], ROWS), F32)
+    place = pltpu.VMEM(half.shape, F32)
+    flops = 2 * ROWS * own.size
+    first = call(own_kernel, half, [rows, own], [], flops=flops)
+    core = lax.rem(index, 2)[None]
+    mixed = call(
+        other_kernel,
+        jax.ShapeDtypeStruct((ROWS, width), BF16),
+        [core, rows, other, first],
+        [place, place],
+        flops=flops,
+        smem=1,
+    )
+    return mixed[:, None, :]
+
+
+def lines(first):
+    along = {"y": [], "z": []}
+    for core in range(2):
+        axis = first if core == 0 else ("z" if first == "y" else "y")
+        for fixed in range(8):
+            along[axis].append([(fixed * 16 + i * 2 if axis == "y" else i * 16 + fixed * 2) + core for i in range(8)])
+    return along["y"] + along["z"]
+
+
+def gather_line(shard):
+    twice = jnp.concatenate([shard, shard], axis=0)
+    got = lax.all_gather(twice, "seq", axis=0, axis_index_groups=lines("y"))
+    return got[:, : shard.shape[0]].reshape(-1, shard.shape[1])
 
 
 def solution(mesh):
-    shape = dict(z=8, y=8, core=2, chan=4)
-    fine = Mesh(mesh.devices.reshape(tuple(shape.values())), tuple(shape))
     placed = (
-        P(None, SEQ, "chan"),
-        P(None, SEQ, "chan"),
+        P(None, "seq", "chan"),
+        P(None, "seq", "chan"),
         P(None, "chan"),
         P("chan"),
-        P(None, ("chan",) + SEQ),
+        P(None, ("chan", "seq")),
         P(),
     )
     return jax.shard_map(
-        local, mesh=fine, in_specs=placed, out_specs=P(None, SEQ, "chan"), check_vma=False
-    )
+        local, mesh=mesh, in_specs=placed, out_specs=P(None, "seq", "chan"), check_vma=False
+    )

time: 124 us -> 151 us (1.22)
  waiting for transfers between devices: 29.1 us -> 50 us
  starting transfers between devices: 18.4 us -> 28.4 us
  blocking collectives: 44.2 us -> 34.5 us
  matrix products: 7.01 us -> 0 us
  Pallas kernels: 7.28 us -> 14.1 us
  local copies, waits for them, and re-layouts: 3.41 us -> 7.61 us
  other arithmetic: 0.84 us -> 2.52 us
    all_gather x2 -> x0, blocking collectives: 22.6 us -> none  [project(): lax.all_gather(gated[:, a:a + half], 'chan', axis=0)]
    all_gather x1 -> x2, waiting for transfers between devices: 13.1 us -> 32.2 us  [the longest x1 21.3 us: gather_line(): got = lax.all_gather(twice, 'seq', axis=0, axis_index_groups=lines('y'))]
    all_to_all x0 -> x1, waiting for transfers between devices: none -> 17.7 us  [local(): lax.all_to_all(copies, 'chan', split_axis=0, concat_axis=0, tiled=True)]
    all_to_all x1, waiting for transfers between devices: 15.4 us -> 0.01 us  [exchange(): got = lax.all_to_all(sent, SEQ, split_axis=0, concat_axis=0, tiled=True)]
    all_to_all x1, blocking collectives: 21.6 us -> 34.5 us  [exchange(): got = lax.all_to_all(sent, SEQ, split_axis=0, concat_axis=0, tiled=True)]
    dot_general x1 -> x0, matrix products: 7.01 us -> none  [project(): lax.dot_general(rows, table, (((1,), (1,)), ((), ())), preferred_element_...]
    pallas_call x4 -> x6, Pallas kernels: 7.28 us -> 14.1 us  [call(): pl.pallas_call(kernel, out_shape=out, in_specs=in_specs, out_specs=full(o...]
    ppermute x0 -> x1, starting transfers between devices: none -> 5.95 us  [local(): other = lax.ppermute(own, 'seq', [(i, i ^ 1) for i in range(PEERS)])]
  transfers between devices with their start and end apart: 2 -> 5, of which waited for: 2 -> 3; matrix products, arithmetic and copies ran while one was open for 3% -> 3% of each run, Pallas kernels for 6% -> 6%
where the time goes in v1:
time: 151 us
  waiting for transfers between devices  50 us (33%)
  blocking collectives  34.5 us (23%)
  starting transfers between devices  28.4 us (19%)
  Pallas kernels  14.1 us (9%)
  between operations  13.5 us (9%)
  local copies, waits for them, and re-layouts  7.61 us (5%)
  other arithmetic  2.52 us (2%)
    all_to_all x1, blocking collectives, exchange(): got = lax.all_to_all(sent, SEQ, split_axis=0, concat_axis=0, tiled=True)  34.5 us
    all_gather x1, waiting for transfers between devices, gather_line(): got = lax.all_gather(twice, 'seq', axis=0, axis_index_groups=lines('y'))  21.3 us
    all_to_all x1, starting transfers between devices, exchange(): got = lax.all_to_all(sent, SEQ, split_axis=0, concat_axis=0, tiled=True)  18.4 us
    all_to_all x1, waiting for transfers between devices, local(): lax.all_to_all(copies, 'chan', split_axis=0, concat_axis=0, tiled=True)  17.7 us
    pallas_call x6, Pallas kernels, call(): pl.pallas_call(kernel, out_shape=out, in_specs=in_specs, out_specs=full(o...  14.1 us
    all_gather x1, waiting for transfers between devices, local(): lax.all_gather(line, 'seq', axis=0, axis_index_groups=lines('z'), tiled=T...  10.9 us
    ppermute x1, starting transfers between devices, local(): other = lax.ppermute(own, 'seq', [(i, i ^ 1) for i in range(PEERS)])  5.95 us
    unnamed x10, local copies, waits for them, and re-layouts  4.2 us
  transfers between devices with their start and end apart: 5, of which 3 were waited for; matrix products, arithmetic and copies ran while one was open for 3% of the time, Pallas kernels for 6%

profile of v1, /device:TPU:1, one launch (start us, length us, event | category | flops | bytes accessed | tf_op | source)
XLA Modules:
  0.0 150.5 jit_solution(1960884235301343490)
XLA Ops:
  6.5 0.0 copy-start.4
  6.5 0.0 copy-start.3
  6.5 0.0 all-gather.6.cloned.1.call-start
  6.5 1.6 %pad_maximum_fusion = bf16[16,4096]{1,0:T(8,128)(2,1)} fusion(bf16[8,4096]{1,0:T(8,128)(2,1)} %bitcast.21), kind=kLoop, calls=%fused_computation.1 | loop fusion | flops 262144 | bytes 196608 | tf_op jit(solution)/shard_map/concatenate | solution.py:258
  8.1 0.0 all-gather.6.cloned.1.call-update
  8.1 0.0 copy-start.2
  8.2 1.0 copy-done.2
  9.1 1.1 shard_map.64
  10.3 18.4 %all-to-all-start = ((bf16[128,5,2,128]{3,2,1,0:T(2,128)(2,1)}), bf16[128,5,2,128]{3,2,1,0:T(2,128)(2,1)S(1)}, u32[]{:S(2)}, u32[]{:S(2)}) async-start(bf16[128,5,2,128]{3,2,1,0:T(2,128)(2,1)} %bitcast.2), calls=%async_computation | async-start | bytes 655360 | tf_op jit(solution)/shard_map/all_to_all | solution.py:182
  28.7 0.0 all-gather.4.cloned.1.call-start
  28.7 0.8 copy.8
  29.5 0.2 reduce-window.9
  29.7 0.1 reduce
  29.8 0.7 sub.3.start_ref
  30.5 0.0 copy-start.1
  30.5 1.0 copy-done.1
  31.5 0.4 shard_map.65.toep_ref
  31.9 0.8 dynamic_slice.3.skip_ref
  32.6 21.3 %all-gather.6.cloned.1.call-done = bf16[128,4096]{1,0:T(8,128)(2,1)} async-done(((bf16[16,4096]{1,0:T(8,128)(2,1)}), bf16[128,4096]{1,0:T(8,128)(2,1)}) %all-gather.6.cloned.1.call-update) | async-done | bytes 1048592 | tf_op jit(solution)/shard_map/all_gather | solution.py:259
  53.9 1.9 %slice_bitcast_fusion = bf16[64,4096]{1,0:T(8,128)(2,1)} fusion(bf16[8,16,4096]{2,1,0:T(8,128)(2,1)} %bitcast.20), kind=kLoop, calls=%fused_computation | loop fusion | bytes 1048576 | tf_op jit(solution)/shard_map/reshape | solution.py:260
  55.8 0.0 all-to-all-done
  55.8 0.0 all-gather.4.cloned.1.call-update
  55.8 0.0 copy-done.4
  55.8 5.4 %shard_map.66 = bf16[1280,128]{1,0:T(8,128)(2,1)S(1)} custom-call(s32[128]{0:T(128)S(1)} %sub.3.start_ref, s32[128]{0:T(128)S(1)} %copy-done.4, f32[8]{0:T(128)S(1)} %dynamic_slice.3.skip_ref, bf16[1280,128]{1,0:T(8,128)(2,1)S(1)} %bitcast.14, bf16[8,256,256]{2,1,0:T(8,128)(2,1)S(1)} %shard_map.65.toep_ref), custom_call_target="tpu_custom_call" | custom-call | flops 134217728 | bytes 1704992 | tf_op jit(solution)/shard_map/pallas_call | solution.py:35
  61.2 34.5 %all_to_all.15 = bf16[128,5,2,128]{3,2,1,0:T(2,128)(2,1)S(1)} all-to-all(bf16[128,5,2,128]{3,2,1,0:T(2,128)(2,1)S(1)} %bitcast.15), channel_id=1, replica_groups=mesh['seq'=128,'chan'=4] {'seq'}, dimensions={0} | all-to-all | bytes 655360 | tf_op jit(solution)/shard_map/all_to_all | solution.py:182
  95.7 10.9 %all-gather.4.cloned.1.call-done.w_ref = bf16[512,4096]{1,0:T(8,128)(2,1)} async-done(((bf16[64,4096]{1,0:T(8,128)(2,1)}), bf16[512,4096]{1,0:T(8,128)(2,1)}) %all-gather.4.cloned.1.call-update) | async-done | bytes 4194320 | tf_op jit(solution)/shard_map/all_gather | solution.py:207
  106.6 6.0 %collective-permute-start = (bf16[512,4096]{1,0:T(8,128)(2,1)}, bf16[512,4096]{1,0:T(8,128)(2,1)}, u32[]{:S(2)}, u32[]{:S(2)}) collective-permute-start(bf16[512,4096]{1,0:T(8,128)(2,1)} %all-gather.4.cloned.1.call-done.w_ref), channel_id=1, source_target_pairs={{0,4},{4,0},{8,12},{12,8},{16,20},{20,16},{24,28},{28,24},{32,36},... | collective-permute-start | bytes 12582920 | tf_op jit(solution)/shard_map/ppermute | solution.py:223
  112.6 0.0 copy-done.3
  112.6 1.6 %shard_map.67 = bf16[4,160,1024]{2,1,0:T(8,128)(2,1)} custom-call(bf16[1280,128]{1,0:T(8,128)(2,1)S(1)} %bitcast.16, bf16[160,1024]{1,0:T(8,128)(2,1)S(1)} %bitcast.18), custom_call_target="tpu_custom_call" | custom-call | bytes 1966080 | tf_op jit(solution)/shard_map/pallas_call | solution.py:35
  114.2 3.9 %all-to-all-start.2 = ((bf16[4,160,1024]{2,1,0:T(8,128)(2,1)}), bf16[4,160,1024]{2,1,0:T(8,128)(2,1)S(1)}, u32[]{:S(2)}, u32[]{:S(2)}) async-start(bf16[4,160,1024]{2,1,0:T(8,128)(2,1)} %shard_map.67), calls=%async_computation.2 | async-start | bytes 2621440 | tf_op jit(solution)/shard_map/all_to_all | solution.py:231
  118.1 17.7 %all-to-all-done.2.rows_ref = bf16[4,160,1024]{2,1,0:T(8,128)(2,1)S(1)} async-done(((bf16[4,160,1024]{2,1,0:T(8,128)(2,1)}), bf16[4,160,1024]{2,1,0:T(8,128)(2,1)S(1)}, u32[]{:S(2)}, u32[]{:S(2)}) %all-to-all-start.2) | async-done | bytes 1310752 | tf_op jit(solution)/shard_map/all_to_all | solution.py:231
  135.9 0.0 copy-start
  135.9 2.2 %copy-done = bf16[512,4096]{1,0:T(8,128)(2,1)S(1)} copy-done((bf16[512,4096]{1,0:T(8,128)(2,1)S(1)}, bf16[512,4096]{1,0:T(8,128)(2,1)}, u32[]{:S(2)}) %copy-start) | copy-done | bytes 4194328
  138.1 1.3 shard_map.68.own_ref
  139.3 0.0 collective-permute-done.w_ref
  139.3 4.4 %shard_map.69 = bf16[160,1024]{1,0:T(8,128)(2,1)} custom-call(s32[1]{0:T(128)} %bitcast.core_ref, bf16[4,160,1024]{2,1,0:T(8,128)(2,1)S(1)} %all-to-all-done.2.rows_ref, bf16[512,4096]{1,0:T(8,128)(2,1)} %collective-permute-done.w_ref, f32[512,160]{1,0:T(8,128)S(1)} %shard_map.68.own_ref), custom_call_target="tpu_custom_call" | custom-call | flops 671088640 | bytes 6160388 | tf_op jit(solution)/shard_map/pallas_call | solution.py:35
Async XLA Ops:
  6.5 49.3 %copy-start.4 = (s32[128]{0:T(128)S(1)}, s32[128]{0:T(128)}, u32[]{:S(2)}) copy-start(s32[128]{0:T(128)} %length_ref) | copy-start | bytes 1540
  6.5 106.1 %copy-start.3 = (bf16[160,1,1024]{2,0,1:T(8,128)(2,1)S(1)}, bf16[160,1,1024]{2,0,1:T(8,128)(2,1)}, u32[]{:S(2)}) copy-start(bf16[160,1,1024]{2,0,1:T(8,128)(2,1)} %param.7) | copy-start | bytes 983044
  6.5 47.4 %all-gather.6.cloned.1.call-start = ((), (), s32[]{:S(2)}) async-start(), calls=%async_computation.4 | async-start | bytes 1179648 | tf_op jit(solution)/shard_map/all_gather | solution.py:259
  8.1 1.0 copy-start.2
  10.3 45.5 %all-to-all-start = ((bf16[128,5,2,128]{3,2,1,0:T(2,128)(2,1)}), bf16[128,5,2,128]{3,2,1,0:T(2,128)(2,1)S(1)}, u32[]{:S(2)}, u32[]{:S(2)}) async-start(bf16[128,5,2,128]{3,2,1,0:T(2,128)(2,1)} %bitcast.2), calls=%async_computation | async-start | bytes 655360 | tf_op jit(solution)/shard_map/all_to_all | solution.py:182
  28.7 77.9 %all-gather.4.cloned.1.call-start = ((), (), s32[]{:S(2)}) async-start(), calls=%async_computation.3 | async-start | bytes 4718592 | tf_op jit(solution)/shard_map/all_gather | solution.py:207
  30.5 1.0 copy-start.1
  106.6 32.7 %collective-permute-start = (bf16[512,4096]{1,0:T(8,128)(2,1)}, bf16[512,4096]{1,0:T(8,128)(2,1)}, u32[]{:S(2)}, u32[]{:S(2)}) collective-permute-start(bf16[512,4096]{1,0:T(8,128)(2,1)} %all-gather.4.cloned.1.call-done.w_ref), channel_id=1, source_target_pairs={{0,4},{4,0},{8,12},{12,8},{16,20},{20,16},{24,28},{28,24},{32,36},... | collective-permute-start | bytes 12582920 | tf_op jit(solution)/shard_map/ppermute | solution.py:223
  114.2 21.7 %all-to-all-start.2 = ((bf16[4,160,1024]{2,1,0:T(8,128)(2,1)}), bf16[4,160,1024]{2,1,0:T(8,128)(2,1)S(1)}, u32[]{:S(2)}, u32[]{:S(2)}) async-start(bf16[4,160,1024]{2,1,0:T(8,128)(2,1)} %shard_map.67), calls=%async_computation.2 | async-start | bytes 2621440 | tf_op jit(solution)/shard_map/all_to_all | solution.py:231
  135.9 2.2 %copy-start = (bf16[512,4096]{1,0:T(8,128)(2,1)S(1)}, bf16[512,4096]{1,0:T(8,128)(2,1)}, u32[]{:S(2)}) copy-start(bf16[512,4096]{1,0:T(8,128)(2,1)} %all-gather.4.cloned.1.call-done.w_ref) | copy-start | bytes 12582916
Sparse Core Ops, SparseCore 0:
  9.4 44.4 all-gather.5
  56.0 50.5 all-gather.3

commit v2 on v1

--- a/solution.py
+++ b/solution.py
@@ -20,6 +20,8 @@
 MSG = PEERS * PER
 VMEM_LIMIT = 48 * 1024 * 1024
 SEQ = "seq"
+LINE = 8
+AWAY = (0, 4, 2, -2, 1, 3, -1, -3)
 
 
 def full(shape):
@@ -158,23 +160,32 @@
     return total
 
 
-def own_kernel(rows_ref, w_ref, out_ref):
-    out_ref[...] = multiply(rows_ref, w_ref)
-
-
-def other_kernel(core_ref, rows_ref, w_ref, own_ref, out_ref, zy, yz):
-    other = multiply(rows_ref, w_ref)
-    own_first = core_ref[0] == 0
-    own = own_ref[...]
-    zy[...] = jnp.where(own_first, own, other)
-    yz[...] = jnp.where(own_first, other, own)
-    for z in range(8):
-        parts = []
-        for y in range(8):
-            parts.append(zy[(8 * z + y) * 8 : (8 * z + y + 1) * 8, :])
-            parts.append(yz[(8 * y + z) * 8 : (8 * y + z + 1) * 8, :])
-        block = jnp.concatenate(parts, axis=0)
-        out_ref[:, z * LANES : (z + 1) * LANES] = block.T.astype(BF16)
+def own_kernel(rows_ref, near_ref, far_ref, out_ref):
+    half = near_ref.shape[0]
+    out_ref[:half] = multiply(rows_ref, near_ref)
+    out_ref[half:] = multiply(rows_ref, far_ref)
+
+
+def other_kernel(index_ref, rows_ref, near_ref, far_ref, own_ref, out_ref, other, columns):
+    half = near_ref.shape[0]
+    other[:half] = multiply(rows_ref, near_ref)
+    other[half:] = multiply(rows_ref, far_ref)
+    index = index_ref[0]
+    z, y, core = lax.shift_right_logical(index, 4), lax.shift_right_logical(index, 1) & 7, index & 1
+    for source, origin in ((own_ref, core), (other, 1 - core)):
+        straight = origin == 0
+        outer, outer_step = jnp.where(straight, z, y), jnp.where(straight, 16, 2)
+        inner, inner_step = jnp.where(straight, y, z), jnp.where(straight, 2, 16)
+        inners = [((inner + AWAY[a]) & 7) * inner_step + origin for a in range(LINE)]
+        for b in range(LINE):
+            base = ((outer + AWAY[b]) & 7) * outer_step
+            for a in range(LINE):
+                group = base + inners[a]
+                rows = slice((LINE * b + a) * CH, (LINE * b + a + 1) * CH)
+                columns[pl.ds(pl.multiple_of(group * CH, CH), CH), :] = source[rows, :]
+    for j in range(8):
+        cols = slice(j * LANES, (j + 1) * LANES)
+        out_ref[:, cols] = columns[cols, :].T.astype(BF16)
 
 
 def exchange(message):
@@ -189,9 +200,11 @@
     msg = jax.ShapeDtypeStruct((MSG, LANES), BF16)
     buf = pltpu.VMEM((MSG, LANES), F32)
     low = pltpu.VMEM((width, LANES), F32)
-    line = gather_line(weights.T)
     packed = call(pack_kernel, msg, [values.reshape(ROWS, width)], [buf, low])
-    packed, filters, doc_lengths, skip = lax.optimization_barrier((packed, filters, doc_lengths, skip))
+    packed, filters, doc_lengths, skip, shard = lax.optimization_barrier(
+        (packed, filters, doc_lengths, skip, weights.T)
+    )
+    line = first_line(shard)
     toep = call(
         toeplitz_kernel,
         jax.ShapeDtypeStruct((CH, 2 * LANES, 2 * LANES), BF16),
@@ -201,10 +214,9 @@
     )
     starts = jnp.cumsum(doc_lengths) - doc_lengths
     own_skip = lax.dynamic_slice(skip, (index * CH,), (CH,))
-    got, line, toep, starts, own_skip = lax.optimization_barrier(
-        (exchange(packed), line, toep, starts, own_skip)
-    )
-    own = lax.all_gather(line, "seq", axis=0, axis_index_groups=lines("z"), tiled=True)
+    got = exchange(packed)
+    line, toep, starts, own_skip = lax.optimization_barrier((line, toep, starts, own_skip))
+    fars = direct(line, "z")
     convolved = call(
         conv_kernel,
         msg,
@@ -219,8 +231,11 @@
         flops=2 * CH * PEERS * 256 * 256,
         smem=3,
     )
-    back, own = lax.optimization_barrier((exchange(convolved), own))
-    other = lax.ppermute(own, "seq", [(i, i ^ 1) for i in range(PEERS)])
+    block, four, two, back_two, _ = lax.optimization_barrier((line, *fars, convolved))
+    near = jnp.concatenate([block, four, two, back_two], axis=0)
+    back, *sides = lax.optimization_barrier((exchange(convolved), *handed(block, two, back_two, "z")))
+    own = near, jnp.concatenate(sides, axis=0)
+    other = tuple(lax.ppermute(part, "seq", [(i, i ^ 1) for i in range(PEERS)]) for part in own)
     groups = lax.axis_size("chan")
     copies = call(
         gate_kernel,
@@ -229,16 +244,15 @@
         [buf, low],
     )
     rows = lax.all_to_all(copies, "chan", split_axis=0, concat_axis=0, tiled=True)
-    half = jax.ShapeDtypeStruct((own.shape[0], ROWS), F32)
-    place = pltpu.VMEM(half.shape, F32)
-    flops = 2 * ROWS * own.size
-    first = call(own_kernel, half, [rows, own], [], flops=flops)
-    core = lax.rem(index, 2)[None]
+    wide = own[0].shape[0] + own[1].shape[0]
+    half = jax.ShapeDtypeStruct((wide, ROWS), F32)
+    flops = 2 * ROWS * wide * own[0].shape[1]
+    first = call(own_kernel, half, [rows, *own], [], flops=flops)
     mixed = call(
         other_kernel,
         jax.ShapeDtypeStruct((ROWS, width), BF16),
-        [core, rows, other, first],
-        [place, place],
+        [index[None], rows, *other, first],
+        [pltpu.VMEM((wide, ROWS), F32), pltpu.VMEM((2 * wide, ROWS), F32)],
         flops=flops,
         smem=1,
     )
@@ -254,10 +268,23 @@
     return along["y"] + along["z"]
 
 
-def gather_line(shard):
-    twice = jnp.concatenate([shard, shard], axis=0)
-    got = lax.all_gather(twice, "seq", axis=0, axis_index_groups=lines("y"))
-    return got[:, : shard.shape[0]].reshape(-1, shard.shape[1])
+def move(array, first, places):
+    pairs = [(line[(i + places) % LINE], line[i]) for line in lines(first) for i in range(LINE)]
+    return lax.ppermute(array, "seq", pairs)
+
+
+def direct(block, first):
+    return tuple(move(block, first, places) for places in AWAY[1:4])
+
+
+def handed(block, two, back_two, first):
+    one = move(jnp.concatenate([block, two], axis=0), first, 1)
+    return one, move(jnp.concatenate([block, back_two], axis=0), first, -1)
+
+
+def first_line(shard):
+    four, two, back_two = direct(shard, "y")
+    return jnp.concatenate([shard, four, two, back_two, *handed(shard, two, back_two, "y")], axis=0)
 
 
 def solution(mesh):

time: 151 us -> 145 us (0.960)
  starting transfers between devices: 28.4 us -> 82.6 us
  waiting for transfers between devices: 50 us -> 14.6 us
  between operations: 13.5 us -> 0.34 us
  blocking collectives: 34.5 us -> 21.6 us
    ppermute x1 -> x12, starting transfers between devices: 5.95 us -> 60.4 us  [the longest x10 43 us: move(): return lax.ppermute(array, 'seq', pairs)]
    all_gather x2 -> x0, waiting for transfers between devices: 32.2 us -> none  [the longest x1 21.3 us: gather_line(): got = lax.all_gather(twice, 'seq', axis=0, axis_index_groups=lines('y'))]
    all_to_all x1 -> x0, waiting for transfers between devices: 17.7 us -> none  [local(): lax.all_to_all(copies, 'chan', split_axis=0, concat_axis=0, tiled=True)]
    ppermute x1 -> x12, waiting for transfers between devices: 0.01 us -> 14.6 us  [the longest x10 14.6 us: move(): return lax.ppermute(array, 'seq', pairs)]
    all_to_all x1, blocking collectives: 34.5 us -> 21.6 us  [local(): lax.all_to_all(copies, 'chan', split_axis=0, concat_axis=0, tiled=True)]
    all_to_all x1 -> x0, starting transfers between devices: 3.94 us -> none  [local(): lax.all_to_all(copies, 'chan', split_axis=0, concat_axis=0, tiled=True)]
    all_to_all x1 -> x2, starting transfers between devices: 18.4 us -> 22.2 us  [exchange(): got = lax.all_to_all(sent, SEQ, split_axis=0, concat_axis=0, tiled=True)]
    concatenate x0 -> x3, local copies, waits for them, and re-layouts: none -> 2.4 us  [the longest x1 1.31 us: local(): own = (near, jnp.concatenate(sides, axis=0))]
  transfers between devices with their start and end apart: 5 -> 14, of which waited for: 3 -> 5; matrix products, arithmetic and copies ran while one was open for 3% -> 7% of each run, Pallas kernels for 6% -> 6%
where the time goes in v2:
time: 145 us; the launch traced here: 144 us
  starting transfers between devices  82.6 us (57%)
  blocking collectives  21.6 us (15%)
  waiting for transfers between devices  14.6 us (10%)
  Pallas kernels  13.1 us (9%)
  local copies, waits for them, and re-layouts  8.29 us (6%)
  other arithmetic  3.61 us (2%)
    ppermute x10, starting transfers between devices, move(): return lax.ppermute(array, 'seq', pairs)  43 us
    all_to_all x2, starting transfers between devices, exchange(): got = lax.all_to_all(sent, SEQ, split_axis=0, concat_axis=0, tiled=True)  22.2 us
    all_to_all x1, blocking collectives, local(): lax.all_to_all(copies, 'chan', split_axis=0, concat_axis=0, tiled=True)  21.6 us
    ppermute x2, starting transfers between devices, local(): lax.ppermute(part, 'seq', [(i, i ^ 1) for i in range(PEERS)])  17.4 us
    ppermute x10, waiting for transfers between devices, move(): return lax.ppermute(array, 'seq', pairs)  14.6 us
    pallas_call x6, Pallas kernels, call(): pl.pallas_call(kernel, out_shape=out, in_specs=in_specs, out_specs=full(o...  13.1 us
    unnamed x23, local copies, waits for them, and re-layouts  4.37 us
  transfers between devices with their start and end apart: 14, of which 5 were waited for; matrix products, arithmetic and copies ran while one was open for 7% of the time, Pallas kernels for 6%

profile of v2, /device:TPU:1, one launch (start us, length us, event | category | flops | bytes accessed | tf_op | source)
XLA Modules:
  0.0 144.1 jit_solution(7403720725783105227)
XLA Ops:
  0.0 0.0 copy-start.1
  0.0 1.0 copy-done.1
  1.0 0.0 copy-start.6
  1.0 1.1 shard_map.64
  2.1 0.0 copy-start.3
  2.1 11.6 %collective-permute-start = (bf16[8,4096]{1,0:T(8,128)(2,1)}, bf16[8,4096]{1,0:T(8,128)(2,1)S(1)}, u32[]{:S(2)}, u32[]{:S(2)}) collective-permute-start(bf16[8,4096]{1,0:T(8,128)(2,1)} %bitcast.15), channel_id=1, source_target_pairs={{32,0},{40,8},{48,16},{56,24},{0,32},{8,40},{16,48},{24,56},{96,64... | collective-permute-start | bytes 196616 | tf_op jit(solution)/shard_map/ppermute | solution.py:273
  13.7 1.9 %collective-permute-start.1 = (bf16[8,4096]{1,0:T(8,128)(2,1)}, bf16[8,4096]{1,0:T(8,128)(2,1)S(1)}, u32[]{:S(2)}, u32[]{:S(2)}) collective-permute-start(bf16[8,4096]{1,0:T(8,128)(2,1)} %bitcast.16), channel_id=1, source_target_pairs={{16,0},{24,8},{32,16},{40,24},{48,32},{56,40},{0,48},{8,56},{80,64... | collective-permute-start | bytes 196616 | tf_op jit(solution)/shard_map/ppermute | solution.py:273
  15.7 4.2 %collective-permute-start.2 = (bf16[8,4096]{1,0:T(8,128)(2,1)}, bf16[8,4096]{1,0:T(8,128)(2,1)S(1)}, u32[]{:S(2)}, u32[]{:S(2)}) collective-permute-start(bf16[8,4096]{1,0:T(8,128)(2,1)} %bitcast.17), channel_id=1, source_target_pairs={{48,0},{56,8},{0,16},{8,24},{16,32},{24,40},{32,48},{40,56},{112,6... | collective-permute-start | bytes 196616 | tf_op jit(solution)/shard_map/ppermute | solution.py:273
  19.9 12.5 %all-to-all-start = ((bf16[128,5,2,128]{3,2,1,0:T(2,128)(2,1)}), bf16[128,5,2,128]{3,2,1,0:T(2,128)(2,1)S(1)}, u32[]{:S(2)}, u32[]{:S(2)}) async-start(bf16[128,5,2,128]{3,2,1,0:T(2,128)(2,1)} %bitcast.4), calls=%async_computation | async-start | bytes 655360 | tf_op jit(solution)/shard_map/all_to_all | solution.py:193
  32.4 0.8 constant_dynamic-update-slice_fusion.5
  33.3 0.8 copy.8
  34.0 0.2 reduce-window.9
  34.2 0.1 reduce
  34.3 0.7 sub.3.start_ref
  35.0 0.8 dynamic_slice.3.skip_ref
  35.7 0.0 copy-start
  35.7 1.0 copy-done
  36.8 0.4 shard_map.65.toep_ref
  37.1 0.0 collective-permute-done.1
  37.2 0.0 collective-permute-done.2
  37.2 0.0 copy-done.6
  37.2 5.2 %collective-permute-start.3 = (bf16[16,4096]{1,0:T(8,128)(2,1)S(1)}, bf16[16,4096]{1,0:T(8,128)(2,1)S(1)}, u32[]{:S(2)}, u32[]{:S(2)}) collective-permute-start(bf16[16,4096]{1,0:T(8,128)(2,1)S(1)} %get-tuple-element.40), channel_id=1, source_target_pairs={{8,0},{16,8},{24,16},{32,24},{40,32},{48,40},{56,48},{0,56},{72,64... | collective-permute-start | bytes 393224 | tf_op jit(solution)/shard_map/ppermute | solution.py:273
  42.4 1.9 %collective-permute-start.4 = (bf16[16,4096]{1,0:T(8,128)(2,1)S(1)}, bf16[16,4096]{1,0:T(8,128)(2,1)S(1)}, u32[]{:S(2)}, u32[]{:S(2)}) collective-permute-start(bf16[16,4096]{1,0:T(8,128)(2,1)S(1)} %get-tuple-element.39), channel_id=1, source_target_pairs={{56,0},{0,8},{8,16},{16,24},{24,32},{32,40},{40,48},{48,56},{120,6... | collective-permute-start | bytes 393224 | tf_op jit(solution)/shard_map/ppermute | solution.py:273
  44.3 0.0 collective-permute-done
  44.4 0.7 collective-permute-done.3
  45.1 4.6 %collective-permute-done.4 = bf16[16,4096]{1,0:T(8,128)(2,1)S(1)} collective-permute-done((bf16[16,4096]{1,0:T(8,128)(2,1)S(1)}, bf16[16,4096]{1,0:T(8,128)(2,1)S(1)}, u32[]{:S(2)}, u32[]{:S(2)}) %collective-permute-start.4) | collective-permute-done | bytes 131104 | tf_op jit(solution)/shard_map/ppermute | solution.py:273
  49.7 6.7 %collective-permute-start.5 = (bf16[64,4096]{1,0:T(8,128)(2,1)S(1)}, bf16[64,4096]{1,0:T(8,128)(2,1)S(1)}, u32[]{:S(2)}, u32[]{:S(2)}) collective-permute-start(bf16[64,4096]{1,0:T(8,128)(2,1)S(1)} %constant_dynamic-update-slice_fusion), channel_id=1, source_target_pairs={{36,4},{44,12},{52,20},{60,28},{4,36},{12,44},{20,52},{28,60},{100... | collective-permute-start | bytes 1572872 | tf_op jit(solution)/shard_map/ppermute | solution.py:273
  56.4 2.2 %collective-permute-start.6 = (bf16[64,4096]{1,0:T(8,128)(2,1)S(1)}, bf16[64,4096]{1,0:T(8,128)(2,1)S(1)}, u32[]{:S(2)}, u32[]{:S(2)}) collective-permute-start(bf16[64,4096]{1,0:T(8,128)(2,1)S(1)} %constant_dynamic-update-slice_fusion), channel_id=1, source_target_pairs={{20,4},{28,12},{36,20},{44,28},{52,36},{60,44},{4,52},{12,60},{84,... | collective-permute-start | bytes 1572872 | tf_op jit(solution)/shard_map/ppermute | solution.py:273
  58.5 4.0 %collective-permute-start.7 = (bf16[64,4096]{1,0:T(8,128)(2,1)S(1)}, bf16[64,4096]{1,0:T(8,128)(2,1)}, u32[]{:S(2)}, u32[]{:S(2)}) collective-permute-start(bf16[64,4096]{1,0:T(8,128)(2,1)S(1)} %constant_dynamic-update-slice_fusion), channel_id=1, source_target_pairs={{52,4},{60,12},{4,20},{12,28},{20,36},{28,44},{36,52},{44,60},{116... | collective-permute-start | bytes 1572872 | tf_op jit(solution)/shard_map/ppermute | solution.py:273
  62.6 0.0 all-to-all-done
  62.6 0.0 copy-done.3
  62.6 6.1 %shard_map.66 = bf16[1280,128]{1,0:T(8,128)(2,1)} custom-call(s32[128]{0:T(128)S(1)} %sub.3.start_ref, s32[128]{0:T(128)S(1)} %copy-done.3, f32[8]{0:T(128)S(1)} %dynamic_slice.3.skip_ref, bf16[1280,128]{1,0:T(8,128)(2,1)S(1)} %bitcast.10, bf16[8,256,256]{2,1,0:T(8,128)(2,1)S(1)} %shard_map.65.toep_ref), custom_call_target="tpu_custom_call" | custom-call | flops 134217728 | bytes 1704992 | tf_op jit(solution)/shard_map/pallas_call | solution.py:37
  68.7 9.7 %all-to-all-start.1 = ((bf16[128,5,2,128]{3,2,1,0:T(2,128)(2,1)}), bf16[128,5,2,128]{3,2,1,0:T(2,128)(2,1)S(1)}, u32[]{:S(2)}, u32[]{:S(2)}) async-start(bf16[128,5,2,128]{3,2,1,0:T(2,128)(2,1)} %bitcast.6), calls=%async_computation.1 | async-start | bytes 655360 | tf_op jit(solution)/shard_map/all_to_all | solution.py:193
  78.4 0.0 collective-permute-done.5
  78.4 0.0 copy-start.4
  78.4 2.1 %collective-permute-done.6 = bf16[64,4096]{1,0:T(8,128)(2,1)S(1)} collective-permute-done((bf16[64,4096]{1,0:T(8,128)(2,1)S(1)}, bf16[64,4096]{1,0:T(8,128)(2,1)S(1)}, u32[]{:S(2)}, u32[]{:S(2)}) %collective-permute-start.6) | collective-permute-done | bytes 524320 | tf_op jit(solution)/shard_map/ppermute | solution.py:273
  80.5 0.0 copy-done.4
  80.5 0.0 collective-permute-done.7
  80.6 0.0 copy-start.5
  80.6 2.7 %pad_maximum_fusion = (bf16[128,4096]{1,0:T(8,128)(2,1)}, bf16[128,4096]{1,0:T(8,128)(2,1)}) fusion(bf16[64,4096]{1,0:T(8,128)(2,1)S(1)} %constant_dynamic-update-slice_fusion, bf16[64,4096]{1,0:T(8,128)(2,1)} %collective-permute-done.7, bf16[64,4096]{1,0:T(8,128)(2,1)S(1)} %collective-permute-done.6), kind=kLoop, calls=%fused_computation | loop fusion | flops 3670016 | bytes 3670016 | tf_op jit(solution)/shard_map/concatenate | solution.py:282
  83.3 3.2 %collective-permute-start.8 = (bf16[128,4096]{1,0:T(8,128)(2,1)}, bf16[128,4096]{1,0:T(8,128)(2,1)}, u32[]{:S(2)}, u32[]{:S(2)}) collective-permute-start(bf16[128,4096]{1,0:T(8,128)(2,1)} %get-tuple-element.38), channel_id=1, source_target_pairs={{12,4},{20,12},{28,20},{36,28},{44,36},{52,44},{60,52},{4,60},{76,... | collective-permute-start | bytes 3145736 | tf_op jit(solution)/shard_map/ppermute | solution.py:273
  86.4 2.1 %collective-permute-start.9 = (bf16[128,4096]{1,0:T(8,128)(2,1)}, bf16[128,4096]{1,0:T(8,128)(2,1)}, u32[]{:S(2)}, u32[]{:S(2)}) collective-permute-start(bf16[128,4096]{1,0:T(8,128)(2,1)} %get-tuple-element.37), channel_id=1, source_target_pairs={{60,4},{4,12},{12,20},{20,28},{28,36},{36,44},{44,52},{52,60},{124... | collective-permute-start | bytes 3145736 | tf_op jit(solution)/shard_map/ppermute | solution.py:273
  88.5 0.0 copy-done.5
  88.6 1.1 constant_dynamic-update-slice_fusion.6.near_ref
  89.7 6.9 %collective-permute-start.10 = (bf16[256,4096]{1,0:T(8,128)(2,1)S(1)}, bf16[256,4096]{1,0:T(8,128)(2,1)}, u32[]{:S(2)}, u32[]{:S(2)}) collective-permute-start(bf16[256,4096]{1,0:T(8,128)(2,1)S(1)} %constant_dynamic-update-slice_fusion.6.near_ref), channel_id=1, source_target_pairs={{0,4},{4,0},{8,12},{12,8},{16,20},{20,16},{24,28},{28,24},{32,36},... | collective-permute-start | bytes 6291464 | tf_op jit(solution)/shard_map/ppermute | solution.py:238
  96.6 0.0 all-to-all-done.1
  96.6 2.8 %collective-permute-done.8 = bf16[128,4096]{1,0:T(8,128)(2,1)} collective-permute-done((bf16[128,4096]{1,0:T(8,128)(2,1)}, bf16[128,4096]{1,0:T(8,128)(2,1)}, u32[]{:S(2)}, u32[]{:S(2)}) %collective-permute-start.8) | collective-permute-done | bytes 1048608 | tf_op jit(solution)/shard_map/ppermute | solution.py:273
  99.4 4.4 %collective-permute-done.9 = bf16[128,4096]{1,0:T(8,128)(2,1)} collective-permute-done((bf16[128,4096]{1,0:T(8,128)(2,1)}, bf16[128,4096]{1,0:T(8,128)(2,1)}, u32[]{:S(2)}, u32[]{:S(2)}) %collective-permute-start.9) | collective-permute-done | bytes 1048608 | tf_op jit(solution)/shard_map/ppermute | solution.py:273
  103.8 0.0 copy-start.2
  103.8 1.4 constant_dynamic-update-slice_fusion.11
  105.2 1.3 constant_dynamic-update-slice_fusion.10.far_ref
  106.5 10.5 %collective-permute-start.11 = (bf16[256,4096]{1,0:T(8,128)(2,1)S(1)}, bf16[256,4096]{1,0:T(8,128)(2,1)S(1)}, u32[]{:S(2)}, u32[]{:S(2)}) collective-permute-start(bf16[256,4096]{1,0:T(8,128)(2,1)S(1)} %constant_dynamic-update-slice_fusion.10.far_ref), channel_id=1, source_target_pairs={{0,4},{4,0},{8,12},{12,8},{16,20},{20,16},{24,28},{28,24},{32,36},... | collective-permute-start | bytes 6291464 | tf_op jit(solution)/shard_map/ppermute | solution.py:238
  117.0 0.0 copy-done.2
  117.0 0.4 shard_map.67
  117.4 21.6 %all_to_all.15.rows_ref = bf16[4,160,1024]{2,1,0:T(8,128)(2,1)S(1)} all-to-all(bf16[4,160,1024]{2,1,0:T(8,128)(2,1)S(1)} %shard_map.67), channel_id=1, replica_groups=mesh['seq'=128,'chan'=4] {'chan'}, dimensions={0} | all-to-all | bytes 2621440 | tf_op jit(solution)/shard_map/all_to_all | solution.py:246
  139.0 1.2 shard_map.68.own_ref
  140.3 0.0 collective-permute-done.10.near_ref
  140.3 0.0 collective-permute-done.11.far_ref
  140.3 3.8 %shard_map.69 = bf16[160,1024]{1,0:T(8,128)(2,1)} custom-call(s32[1]{0:T(128)} %bitcast.index_ref, bf16[4,160,1024]{2,1,0:T(8,128)(2,1)S(1)} %all_to_all.15.rows_ref, bf16[256,4096]{1,0:T(8,128)(2,1)} %collective-permute-done.10.near_ref, bf16[256,4096]{1,0:T(8,128)(2,1)S(1)} %collective-permute-done.11.far_ref, f32[512,160]{1,0:T(8,128)S(1)} %shard_map.68.own_ref), custom_call_target="tpu_custom_call" | custom-call | flops 671088640 | bytes 6160388 | tf_op jit(solution)/shard_map/pallas_call | solution.py:37
  (9 shorter events, 0.2 us)
Async XLA Ops:
  0.0 1.0 copy-start.1
  1.0 36.2 %copy-start.6 = (bf16[4096,8]{0,1:T(8,128)(2,1)S(1)}, bf16[4096,8]{0,1:T(8,128)(2,1)}, u32[]{:S(2)}) copy-start(bf16[4096,8]{0,1:T(8,128)(2,1)} %param.10) | copy-start | bytes 196612
  2.1 60.5 %copy-start.3 = (s32[128]{0:T(128)S(1)}, s32[128]{0:T(128)}, u32[]{:S(2)}) copy-start(s32[128]{0:T(128)} %length_ref) | copy-start | bytes 1540
  2.1 42.2 %collective-permute-start = (bf16[8,4096]{1,0:T(8,128)(2,1)}, bf16[8,4096]{1,0:T(8,128)(2,1)S(1)}, u32[]{:S(2)}, u32[]{:S(2)}) collective-permute-start(bf16[8,4096]{1,0:T(8,128)(2,1)} %bitcast.15), channel_id=1, source_target_pairs={{32,0},{40,8},{48,16},{56,24},{0,32},{8,40},{16,48},{24,56},{96,64... | collective-permute-start | bytes 196616 | tf_op jit(solution)/shard_map/ppermute | solution.py:273
  13.7 23.4 %collective-permute-start.1 = (bf16[8,4096]{1,0:T(8,128)(2,1)}, bf16[8,4096]{1,0:T(8,128)(2,1)S(1)}, u32[]{:S(2)}, u32[]{:S(2)}) collective-permute-start(bf16[8,4096]{1,0:T(8,128)(2,1)} %bitcast.16), channel_id=1, source_target_pairs={{16,0},{24,8},{32,16},{40,24},{48,32},{56,40},{0,48},{8,56},{80,64... | collective-permute-start | bytes 196616 | tf_op jit(solution)/shard_map/ppermute | solution.py:273
  15.7 21.5 %collective-permute-start.2 = (bf16[8,4096]{1,0:T(8,128)(2,1)}, bf16[8,4096]{1,0:T(8,128)(2,1)S(1)}, u32[]{:S(2)}, u32[]{:S(2)}) collective-permute-start(bf16[8,4096]{1,0:T(8,128)(2,1)} %bitcast.17), channel_id=1, source_target_pairs={{48,0},{56,8},{0,16},{8,24},{16,32},{24,40},{32,48},{40,56},{112,6... | collective-permute-start | bytes 196616 | tf_op jit(solution)/shard_map/ppermute | solution.py:273
  19.9 42.7 %all-to-all-start = ((bf16[128,5,2,128]{3,2,1,0:T(2,128)(2,1)}), bf16[128,5,2,128]{3,2,1,0:T(2,128)(2,1)S(1)}, u32[]{:S(2)}, u32[]{:S(2)}) async-start(bf16[128,5,2,128]{3,2,1,0:T(2,128)(2,1)} %bitcast.4), calls=%async_computation | async-start | bytes 655360 | tf_op jit(solution)/shard_map/all_to_all | solution.py:193
  35.7 1.0 copy-start
  37.2 7.8 %collective-permute-start.3 = (bf16[16,4096]{1,0:T(8,128)(2,1)S(1)}, bf16[16,4096]{1,0:T(8,128)(2,1)S(1)}, u32[]{:S(2)}, u32[]{:S(2)}) collective-permute-start(bf16[16,4096]{1,0:T(8,128)(2,1)S(1)} %get-tuple-element.40), channel_id=1, source_target_pairs={{8,0},{16,8},{24,16},{32,24},{40,32},{48,40},{56,48},{0,56},{72,64... | collective-permute-start | bytes 393224 | tf_op jit(solution)/shard_map/ppermute | solution.py:273
  42.4 7.3 %collective-permute-start.4 = (bf16[16,4096]{1,0:T(8,128)(2,1)S(1)}, bf16[16,4096]{1,0:T(8,128)(2,1)S(1)}, u32[]{:S(2)}, u32[]{:S(2)}) collective-permute-start(bf16[16,4096]{1,0:T(8,128)(2,1)S(1)} %get-tuple-element.39), channel_id=1, source_target_pairs={{56,0},{0,8},{8,16},{16,24},{24,32},{32,40},{40,48},{48,56},{120,6... | collective-permute-start | bytes 393224 | tf_op jit(solution)/shard_map/ppermute | solution.py:273
  49.7 28.7 %collective-permute-start.5 = (bf16[64,4096]{1,0:T(8,128)(2,1)S(1)}, bf16[64,4096]{1,0:T(8,128)(2,1)S(1)}, u32[]{:S(2)}, u32[]{:S(2)}) collective-permute-start(bf16[64,4096]{1,0:T(8,128)(2,1)S(1)} %constant_dynamic-update-slice_fusion), channel_id=1, source_target_pairs={{36,4},{44,12},{52,20},{60,28},{4,36},{12,44},{20,52},{28,60},{100... | collective-permute-start | bytes 1572872 | tf_op jit(solution)/shard_map/ppermute | solution.py:273
  56.4 24.2 %collective-permute-start.6 = (bf16[64,4096]{1,0:T(8,128)(2,1)S(1)}, bf16[64,4096]{1,0:T(8,128)(2,1)S(1)}, u32[]{:S(2)}, u32[]{:S(2)}) collective-permute-start(bf16[64,4096]{1,0:T(8,128)(2,1)S(1)} %constant_dynamic-update-slice_fusion), channel_id=1, source_target_pairs={{20,4},{28,12},{36,20},{44,28},{52,36},{60,44},{4,52},{12,60},{84,... | collective-permute-start | bytes 1572872 | tf_op jit(solution)/shard_map/ppermute | solution.py:273
  58.5 22.0 %collective-permute-start.7 = (bf16[64,4096]{1,0:T(8,128)(2,1)S(1)}, bf16[64,4096]{1,0:T(8,128)(2,1)}, u32[]{:S(2)}, u32[]{:S(2)}) collective-permute-start(bf16[64,4096]{1,0:T(8,128)(2,1)S(1)} %constant_dynamic-update-slice_fusion), channel_id=1, source_target_pairs={{52,4},{60,12},{4,20},{12,28},{20,36},{28,44},{36,52},{44,60},{116... | collective-permute-start | bytes 1572872 | tf_op jit(solution)/shard_map/ppermute | solution.py:273
  68.7 27.9 %all-to-all-start.1 = ((bf16[128,5,2,128]{3,2,1,0:T(2,128)(2,1)}), bf16[128,5,2,128]{3,2,1,0:T(2,128)(2,1)S(1)}, u32[]{:S(2)}, u32[]{:S(2)}) async-start(bf16[128,5,2,128]{3,2,1,0:T(2,128)(2,1)} %bitcast.6), calls=%async_computation.1 | async-start | bytes 655360 | tf_op jit(solution)/shard_map/all_to_all | solution.py:193
  78.4 2.1 %copy-start.4 = (bf16[64,4096]{1,0:T(8,128)(2,1)}, bf16[64,4096]{1,0:T(8,128)(2,1)S(1)}, u32[]{:S(2)}) copy-start(bf16[64,4096]{1,0:T(8,128)(2,1)S(1)} %collective-permute-done.5) | copy-start | bytes 1572868
  80.6 8.0 %copy-start.5 = (bf16[64,4096]{1,0:T(8,128)(2,1)S(1)}, bf16[64,4096]{1,0:T(8,128)(2,1)}, u32[]{:S(2)}) copy-start(bf16[64,4096]{1,0:T(8,128)(2,1)} %copy-done.4) | copy-start | bytes 1572868
  83.3 16.1 %collective-permute-start.8 = (bf16[128,4096]{1,0:T(8,128)(2,1)}, bf16[128,4096]{1,0:T(8,128)(2,1)}, u32[]{:S(2)}, u32[]{:S(2)}) collective-permute-start(bf16[128,4096]{1,0:T(8,128)(2,1)} %get-tuple-element.38), channel_id=1, source_target_pairs={{12,4},{20,12},{28,20},{36,28},{44,36},{52,44},{60,52},{4,60},{76,... | collective-permute-start | bytes 3145736 | tf_op jit(solution)/shard_map/ppermute | solution.py:273
  86.4 17.4 %collective-permute-start.9 = (bf16[128,4096]{1,0:T(8,128)(2,1)}, bf16[128,4096]{1,0:T(8,128)(2,1)}, u32[]{:S(2)}, u32[]{:S(2)}) collective-permute-start(bf16[128,4096]{1,0:T(8,128)(2,1)} %get-tuple-element.37), channel_id=1, source_target_pairs={{60,4},{4,12},{12,20},{20,28},{28,36},{36,44},{44,52},{52,60},{124... | collective-permute-start | bytes 3145736 | tf_op jit(solution)/shard_map/ppermute | solution.py:273
  89.7 50.6 %collective-permute-start.10 = (bf16[256,4096]{1,0:T(8,128)(2,1)S(1)}, bf16[256,4096]{1,0:T(8,128)(2,1)}, u32[]{:S(2)}, u32[]{:S(2)}) collective-permute-start(bf16[256,4096]{1,0:T(8,128)(2,1)S(1)} %constant_dynamic-update-slice_fusion.6.near_ref), channel_id=1, source_target_pairs={{0,4},{4,0},{8,12},{12,8},{16,20},{20,16},{24,28},{28,24},{32,36},... | collective-permute-start | bytes 6291464 | tf_op jit(solution)/shard_map/ppermute | solution.py:238
  103.8 13.2 %copy-start.2 = (bf16[160,1,1024]{2,0,1:T(8,128)(2,1)S(1)}, bf16[160,1,1024]{2,0,1:T(8,128)(2,1)}, u32[]{:S(2)}) copy-start(bf16[160,1,1024]{2,0,1:T(8,128)(2,1)} %param.7) | copy-start | bytes 983044
  106.5 33.8 %collective-permute-start.11 = (bf16[256,4096]{1,0:T(8,128)(2,1)S(1)}, bf16[256,4096]{1,0:T(8,128)(2,1)S(1)}, u32[]{:S(2)}, u32[]{:S(2)}) collective-permute-start(bf16[256,4096]{1,0:T(8,128)(2,1)S(1)} %constant_dynamic-update-slice_fusion.10.far_ref), channel_id=1, source_target_pairs={{0,4},{4,0},{8,12},{12,8},{16,20},{20,16},{24,28},{28,24},{32,36},... | collective-permute-start | bytes 6291464 | tf_op jit(solution)/shard_map/ppermute | solution.py:238

commit v3 on v1

--- a/solution.py
+++ b/solution.py
@@ -158,12 +158,12 @@
     return total
 
 
-def own_kernel(rows_ref, w_ref, out_ref):
-    out_ref[...] = multiply(rows_ref, w_ref)
-
-
-def other_kernel(core_ref, rows_ref, w_ref, own_ref, out_ref, zy, yz):
-    other = multiply(rows_ref, w_ref)
+def product_kernel(rows_ref, w_ref, out_ref):
+    out_ref[...] = multiply(rows_ref, w_ref).astype(out_ref.dtype)
+
+
+def join_kernel(core_ref, own_ref, other_ref, out_ref, zy, yz):
+    other = other_ref[...].astype(F32)
     own_first = core_ref[0] == 0
     own = own_ref[...]
     zy[...] = jnp.where(own_first, own, other)
@@ -189,9 +189,11 @@
     msg = jax.ShapeDtypeStruct((MSG, LANES), BF16)
     buf = pltpu.VMEM((MSG, LANES), F32)
     low = pltpu.VMEM((width, LANES), F32)
-    line = gather_line(weights.T)
     packed = call(pack_kernel, msg, [values.reshape(ROWS, width)], [buf, low])
-    packed, filters, doc_lengths, skip = lax.optimization_barrier((packed, filters, doc_lengths, skip))
+    packed, filters, doc_lengths, skip, shard = lax.optimization_barrier(
+        (packed, filters, doc_lengths, skip, weights.T)
+    )
+    line = gather_line(shard)
     toep = call(
         toeplitz_kernel,
         jax.ShapeDtypeStruct((CH, 2 * LANES, 2 * LANES), BF16),
@@ -219,8 +221,7 @@
         flops=2 * CH * PEERS * 256 * 256,
         smem=3,
     )
-    back, own = lax.optimization_barrier((exchange(convolved), own))
-    other = lax.ppermute(own, "seq", [(i, i ^ 1) for i in range(PEERS)])
+    back = exchange(convolved)
     groups = lax.axis_size("chan")
     copies = call(
         gate_kernel,
@@ -229,17 +230,17 @@
         [buf, low],
     )
     rows = lax.all_to_all(copies, "chan", split_axis=0, concat_axis=0, tiled=True)
-    half = jax.ShapeDtypeStruct((own.shape[0], ROWS), F32)
-    place = pltpu.VMEM(half.shape, F32)
+    swap = [(i, i ^ 1) for i in range(PEERS)]
+    half = (own.shape[0], ROWS)
     flops = 2 * ROWS * own.size
-    first = call(own_kernel, half, [rows, own], [], flops=flops)
-    core = lax.rem(index, 2)[None]
+    twin_rows = lax.ppermute(rows, "seq", swap)
+    mine = call(product_kernel, jax.ShapeDtypeStruct(half, F32), [rows, own], [], flops=flops)
+    theirs = call(product_kernel, jax.ShapeDtypeStruct(half, BF16), [twin_rows, own], [], flops=flops)
     mixed = call(
-        other_kernel,
+        join_kernel,
         jax.ShapeDtypeStruct((ROWS, width), BF16),
-        [core, rows, other, first],
-        [place, place],
-        flops=flops,
+        [lax.rem(index, 2)[None], mine, lax.ppermute(theirs, "seq", swap)],
+        [pltpu.VMEM(half, F32)] * 2,
         smem=1,
     )
     return mixed[:, None, :]
@@ -255,9 +256,7 @@
 
 
 def gather_line(shard):
-    twice = jnp.concatenate([shard, shard], axis=0)
-    got = lax.all_gather(twice, "seq", axis=0, axis_index_groups=lines("y"))
-    return got[:, : shard.shape[0]].reshape(-1, shard.shape[1])
+    return lax.all_gather(shard, "seq", axis=0, axis_index_groups=lines("y"), tiled=True)
 
 
 def solution(mesh):

time: 151 us -> 140 us (0.927)
  waiting for transfers between devices: 50 us -> 2.67 us
  blocking collectives: 34.5 us -> 81.8 us
  starting transfers between devices: 28.4 us -> 23.9 us
  Pallas kernels: 14.1 us -> 10.8 us
  other arithmetic: 2.52 us -> 0.28 us
    all_gather x0 -> x1, blocking collectives: none -> 25.5 us  [gather_line(): lax.all_gather(shard, 'seq', axis=0, axis_index_groups=lines('y'), tiled=...]
    all_to_all x0 -> x1, blocking collectives: none -> 21.6 us  [local(): lax.all_to_all(copies, 'chan', split_axis=0, concat_axis=0, tiled=True)]
    all_gather x1 -> x0, waiting for transfers between devices: 21.3 us -> none  [gather_line(): got = lax.all_gather(twice, 'seq', axis=0, axis_index_groups=lines('y'))]
    all_to_all x1 -> x0, waiting for transfers between devices: 17.7 us -> none  [local(): lax.all_to_all(copies, 'chan', split_axis=0, concat_axis=0, tiled=True)]
    all_gather x1, waiting for transfers between devices: 10.9 us -> 0.01 us  [local(): lax.all_gather(line, 'seq', axis=0, axis_index_groups=lines('z'), tiled=T...]
    all_to_all x1 -> x0, starting transfers between devices: 3.94 us -> none  [local(): lax.all_to_all(copies, 'chan', split_axis=0, concat_axis=0, tiled=True)]
    pallas_call x6 -> x7, Pallas kernels: 14.1 us -> 10.8 us  [call(): pl.pallas_call(kernel, out_shape=out, in_specs=in_specs, out_specs=full(o...]
    ppermute x1 -> x2, waiting for transfers between devices: 0.01 us -> 2.64 us  [the longest x1 2.64 us: local(): twin_rows = lax.ppermute(rows, 'seq', swap)]
  transfers between devices with their start and end apart: 5 -> 4, of which waited for: 3 -> 1; matrix products, arithmetic and copies ran while one was open for 3% -> 1% of each run, Pallas kernels for 6% -> 5%
where the time goes in v3:
time: 140 us; the launch traced here: 139 us
  blocking collectives  81.8 us (58%)
  starting transfers between devices  23.9 us (17%)
  between operations  13.5 us (10%)
  Pallas kernels  10.8 us (8%)
  local copies, waits for them, and re-layouts  6.3 us (4%)
  waiting for transfers between devices  2.67 us (2%)
    all_to_all x1, blocking collectives, exchange(): got = lax.all_to_all(sent, SEQ, split_axis=0, concat_axis=0, tiled=True)  34.7 us
    all_gather x1, blocking collectives, gather_line(): lax.all_gather(shard, 'seq', axis=0, axis_index_groups=lines('y'), tiled=...  25.5 us
    all_to_all x1, blocking collectives, local(): lax.all_to_all(copies, 'chan', split_axis=0, concat_axis=0, tiled=True)  21.6 us
    all_to_all x1, starting transfers between devices, exchange(): got = lax.all_to_all(sent, SEQ, split_axis=0, concat_axis=0, tiled=True)  18.6 us
    pallas_call x7, Pallas kernels, call(): pl.pallas_call(kernel, out_shape=out, in_specs=in_specs, out_specs=full(o...  10.8 us
    unnamed x14, local copies, waits for them, and re-layouts  5.42 us
    ppermute x1, starting transfers between devices, local(): twin_rows = lax.ppermute(rows, 'seq', swap)  3.01 us
  transfers between devices with their start and end apart: 4, of which 1 were waited for; matrix products, arithmetic and copies ran while one was open for 1% of the time, Pallas kernels for 5%

profile of v3, /device:TPU:1, one launch (start us, length us, event | category | flops | bytes accessed | tf_op | source)
XLA Modules:
  0.0 139.2 jit_solution(3916464995811133305)
XLA Ops:
  6.5 0.0 copy-start.2
  6.5 0.0 copy-start.3
  6.5 1.0 copy-done.3
  7.6 0.0 copy-start.5
  7.6 1.1 shard_map.64
  8.7 0.0 copy-start.6
  8.7 18.6 %all-to-all-start = ((bf16[128,5,2,128]{3,2,1,0:T(2,128)(2,1)}), bf16[128,5,2,128]{3,2,1,0:T(2,128)(2,1)S(1)}, u32[]{:S(2)}, u32[]{:S(2)}) async-start(bf16[128,5,2,128]{3,2,1,0:T(2,128)(2,1)} %bitcast.3), calls=%async_computation | async-start | bytes 655360 | tf_op jit(solution)/shard_map/all_to_all | solution.py:182
  27.3 0.0 all-gather.2.cloned.1.call-start
  27.3 0.0 copy-done.5
  27.3 0.1 copy.8
  27.4 0.2 reduce-window.9
  27.6 0.1 reduce
  27.7 0.8 dynamic_slice.3.skip_ref
  28.5 0.0 copy-done.2
  28.5 0.4 shard_map.65.toep_ref
  28.9 0.0 copy-done.6
  28.9 25.5 %all_gather.6 = bf16[64,4096]{1,0:T(8,128)(2,1)} all-gather(bf16[8,4096]{1,0:T(8,128)(2,1)S(1)} %bitcast.17), channel_id=1, replica_groups={{0,8,16,24,32,40,48,56},{64,72,80,88,96,104,112,120},{128,136,144,152,1..., dimensions={0}, use_global_device_ids=true | all-gather | bytes 589824 | tf_op jit(solution)/shard_map/all_gather | solution.py:259
  54.4 0.0 all-to-all-done
  54.4 0.0 all-gather.2.cloned.1.call-update
  54.4 0.0 copy-start.4
  54.4 5.4 %shard_map.66 = bf16[1280,128]{1,0:T(8,128)(2,1)S(1)} custom-call(s32[128]{0:T(128)S(1)} %sub.3.start_ref, s32[128]{0:T(128)S(1)} %copy-done.5, f32[8]{0:T(128)S(1)} %dynamic_slice.3.skip_ref, bf16[1280,128]{1,0:T(8,128)(2,1)S(1)} %bitcast.11, bf16[8,256,256]{2,1,0:T(8,128)(2,1)S(1)} %shard_map.65.toep_ref), custom_call_target="tpu_custom_call" | custom-call | flops 134217728 | bytes 1704992 | tf_op jit(solution)/shard_map/pallas_call | solution.py:35
  59.8 34.7 %all_to_all.15 = bf16[128,5,2,128]{3,2,1,0:T(2,128)(2,1)S(1)} all-to-all(bf16[128,5,2,128]{3,2,1,0:T(2,128)(2,1)S(1)} %bitcast.12), channel_id=1, replica_groups=mesh['seq'=128,'chan'=4] {'seq'}, dimensions={0} | all-to-all | bytes 655360 | tf_op jit(solution)/shard_map/all_to_all | solution.py:182
  94.5 0.0 copy-done.4
  94.5 0.4 shard_map.67
  94.9 21.6 %all_to_all.16.rows_ref = bf16[4,160,1024]{2,1,0:T(8,128)(2,1)S(1)} all-to-all(bf16[4,160,1024]{2,1,0:T(8,128)(2,1)S(1)} %shard_map.67), channel_id=1, replica_groups=mesh['seq'=128,'chan'=4] {'chan'}, dimensions={0} | all-to-all | bytes 2621440 | tf_op jit(solution)/shard_map/all_to_all | solution.py:232
  116.5 3.0 %collective-permute-start = (bf16[4,160,1024]{2,1,0:T(8,128)(2,1)S(1)}, bf16[4,160,1024]{2,1,0:T(8,128)(2,1)S(1)}, u32[]{:S(2)}, u32[]{:S(2)}) collective-permute-start(bf16[4,160,1024]{2,1,0:T(8,128)(2,1)S(1)} %all_to_all.16.rows_ref), channel_id=1, source_target_pairs={{0,4},{4,0},{8,12},{12,8},{16,20},{20,16},{24,28},{28,24},{32,36},... | collective-permute-start | bytes 3932168 | tf_op jit(solution)/shard_map/ppermute | solution.py:236
  119.5 2.6 %collective-permute-done.rows_ref = bf16[4,160,1024]{2,1,0:T(8,128)(2,1)S(1)} collective-permute-done((bf16[4,160,1024]{2,1,0:T(8,128)(2,1)S(1)}, bf16[4,160,1024]{2,1,0:T(8,128)(2,1)S(1)}, u32[]{:S(2)}, u32[]{:S(2)}) %collective-permute-start) | collective-permute-done | bytes 1310752 | tf_op jit(solution)/shard_map/ppermute | solution.py:236
  122.2 0.0 all-gather.2.cloned.1.call-done.w_ref
  122.2 0.0 copy-start
  122.2 2.2 %copy-done = bf16[512,4096]{1,0:T(8,128)(2,1)S(1)} copy-done((bf16[512,4096]{1,0:T(8,128)(2,1)S(1)}, bf16[512,4096]{1,0:T(8,128)(2,1)}, u32[]{:S(2)}) %copy-start) | copy-done | bytes 4194328
  124.4 1.3 shard_map.69
  125.6 2.3 %collective-permute-start.1 = (bf16[512,160]{1,0:T(8,128)(2,1)S(1)}, bf16[512,160]{1,0:T(8,128)(2,1)S(1)}, u32[]{:S(2)}, u32[]{:S(2)}) collective-permute-start(bf16[512,160]{1,0:T(8,128)(2,1)S(1)} %shard_map.69), channel_id=1, source_target_pairs={{0,4},{4,0},{8,12},{12,8},{16,20},{20,16},{24,28},{28,24},{32,36},... | collective-permute-start | bytes 491528 | tf_op jit(solution)/shard_map/ppermute | solution.py:242
  127.9 0.0 copy-start.1
  127.9 2.2 %copy-done.1 = bf16[512,4096]{1,0:T(8,128)(2,1)S(1)} copy-done((bf16[512,4096]{1,0:T(8,128)(2,1)S(1)}, bf16[512,4096]{1,0:T(8,128)(2,1)}, u32[]{:S(2)}) %copy-start.1) | copy-done | bytes 4194328
  130.1 1.3 shard_map.68.own_ref
  131.4 0.0 collective-permute-done.1.other_ref
  131.4 1.0 shard_map.70
  (1 shorter events, 0.0 us)
Async XLA Ops:
  6.5 22.0 %copy-start.2 = (bf16[256,1024]{1,0:T(8,128)(2,1)S(1)}, bf16[256,1024]{1,0:T(8,128)(2,1)}, u32[]{:S(2)}) copy-start(bf16[256,1024]{1,0:T(8,128)(2,1)} %f_ref) | copy-start | bytes 1572868
  6.5 1.0 copy-start.3
  7.6 19.8 %copy-start.5 = (s32[128]{0:T(128)S(1)}, s32[128]{0:T(128)}, u32[]{:S(2)}) copy-start(s32[128]{0:T(128)} %length_ref) | copy-start | bytes 1540
  8.7 20.2 %copy-start.6 = (bf16[4096,8]{0,1:T(8,128)(2,1)S(1)}, bf16[4096,8]{0,1:T(8,128)(2,1)}, u32[]{:S(2)}) copy-start(bf16[4096,8]{0,1:T(8,128)(2,1)} %param.10) | copy-start | bytes 196612
  8.7 45.7 %all-to-all-start = ((bf16[128,5,2,128]{3,2,1,0:T(2,128)(2,1)}), bf16[128,5,2,128]{3,2,1,0:T(2,128)(2,1)S(1)}, u32[]{:S(2)}, u32[]{:S(2)}) async-start(bf16[128,5,2,128]{3,2,1,0:T(2,128)(2,1)} %bitcast.3), calls=%async_computation | async-start | bytes 655360 | tf_op jit(solution)/shard_map/all_to_all | solution.py:182
  27.3 94.9 %all-gather.2.cloned.1.call-start = ((), (), s32[]{:S(2)}) async-start(), calls=%async_computation.3 | async-start | bytes 4718592 | tf_op jit(solution)/shard_map/all_gather | solution.py:209
  54.4 40.1 %copy-start.4 = (bf16[160,1,1024]{2,0,1:T(8,128)(2,1)S(1)}, bf16[160,1,1024]{2,0,1:T(8,128)(2,1)}, u32[]{:S(2)}) copy-start(bf16[160,1,1024]{2,0,1:T(8,128)(2,1)} %param.7) | copy-start | bytes 983044
  116.5 5.7 %collective-permute-start = (bf16[4,160,1024]{2,1,0:T(8,128)(2,1)S(1)}, bf16[4,160,1024]{2,1,0:T(8,128)(2,1)S(1)}, u32[]{:S(2)}, u32[]{:S(2)}) collective-permute-start(bf16[4,160,1024]{2,1,0:T(8,128)(2,1)S(1)} %all_to_all.16.rows_ref), channel_id=1, source_target_pairs={{0,4},{4,0},{8,12},{12,8},{16,20},{20,16},{24,28},{28,24},{32,36},... | collective-permute-start | bytes 3932168 | tf_op jit(solution)/shard_map/ppermute | solution.py:236
  122.2 2.2 %copy-start = (bf16[512,4096]{1,0:T(8,128)(2,1)S(1)}, bf16[512,4096]{1,0:T(8,128)(2,1)}, u32[]{:S(2)}) copy-start(bf16[512,4096]{1,0:T(8,128)(2,1)} %all-gather.2.cloned.1.call-done.w_ref) | copy-start | bytes 12582916
  125.6 5.7 %collective-permute-start.1 = (bf16[512,160]{1,0:T(8,128)(2,1)S(1)}, bf16[512,160]{1,0:T(8,128)(2,1)S(1)}, u32[]{:S(2)}, u32[]{:S(2)}) collective-permute-start(bf16[512,160]{1,0:T(8,128)(2,1)S(1)} %shard_map.69), channel_id=1, source_target_pairs={{0,4},{4,0},{8,12},{12,8},{16,20},{20,16},{24,28},{28,24},{32,36},... | collective-permute-start | bytes 491528 | tf_op jit(solution)/shard_map/ppermute | solution.py:242
  127.9 2.2 %copy-start.1 = (bf16[512,4096]{1,0:T(8,128)(2,1)S(1)}, bf16[512,4096]{1,0:T(8,128)(2,1)}, u32[]{:S(2)}) copy-start(bf16[512,4096]{1,0:T(8,128)(2,1)} %all-gather.2.cloned.1.call-done.w_ref) | copy-start | bytes 12582916
Sparse Core Ops, SparseCore 0:
  54.5 50.9 all-gather.1

commit v4 on v0

--- a/solution.py
+++ b/solution.py
@@ -20,7 +20,8 @@
 PEERS = 128
 MSG = PEERS * PER
 VMEM_LIMIT = 48 * 1024 * 1024
-SEQ = ("z", "y", "core")
+SEQ = ("z", "y_far", "y_near", "core")
+NEAR = 1
 
 
 def full(shape):
@@ -142,9 +143,48 @@
         cols = slice(j * LANES, (j + 1) * LANES)
         head = [msg[pl.ds((16 * j + g) * PER, CH), :] for g in range(16)]
         head = jnp.concatenate(head, axis=0).T
-        out_ref[:HEAD, cols] = (head * g_ref[:HEAD, cols].astype(F32)).astype(BF16)
+        head = (head * g_ref[:HEAD, cols].astype(F32)).astype(BF16)
         tail = low[cols, :].T[:TAIL]
-        out_ref[HEAD:, cols] = (tail * g_ref[HEAD:, cols].astype(F32)).astype(BF16)
+        tail = (tail * g_ref[HEAD:, cols].astype(F32)).astype(BF16)
+        for q in range(out_ref.shape[0]):
+            out_ref[q, :HEAD, cols] = head
+            out_ref[q, HEAD:, cols] = tail
+
+
+def product_kernel(near, rows_ref, w_ref, out_ref):
+    groups, _, width = rows_ref.shape
+    total = jnp.zeros((w_ref.shape[0], ROWS), F32)
+    for q in range(groups):
+        part = w_ref[:, q * width : (q + 1) * width]
+        total += lax.dot_general(part, rows_ref[q], (((1,), (1,)), ((), ())), preferred_element_type=F32)
+    for j in range(w_ref.shape[0] // LANES):
+        parts = []
+        for y in range(8):
+            for core in range(2):
+                group = 16 * j + y // near * 2 * near + core * near + y % near
+                parts.append(total[group * CH : (group + 1) * CH])
+        block = jnp.concatenate(parts, axis=0)
+        out_ref[:, j * LANES : (j + 1) * LANES] = block.T.astype(BF16)
+
+
+def product(rows, table, near):
+    block = 256
+    return pl.pallas_call(
+        functools.partial(product_kernel, near),
+        out_shape=jax.ShapeDtypeStruct((ROWS, table.shape[0]), BF16),
+        grid=(table.shape[0] // block,),
+        in_specs=[
+            pl.BlockSpec(rows.shape, lambda j: (0, 0, 0)),
+            pl.BlockSpec((block, table.shape[1]), lambda j: (j, 0)),
+        ],
+        out_specs=pl.BlockSpec((ROWS, block), lambda j: (0, j)),
+        compiler_params=pltpu.CompilerParams(vmem_limit_bytes=VMEM_LIMIT),
+        cost_estimate=pl.CostEstimate(
+            flops=2 * ROWS * table.size,
+            bytes_accessed=2 * (table.size + rows.size + ROWS * table.shape[0]),
+            transcendentals=0,
+        ),
+    )(rows, table)
 
 
 def exchange(message):
@@ -160,6 +200,8 @@
     buf = pltpu.VMEM((MSG, LANES), F32)
     low = pltpu.VMEM((width, LANES), F32)
     packed = call(pack_kernel, msg, [values.reshape(ROWS, width)], [buf, low])
+    table = gather_columns(weights.T)
+    packed, filters, doc_lengths, skip = lax.optimization_barrier((packed, filters, doc_lengths, skip))
     toep = call(
         toeplitz_kernel,
         jax.ShapeDtypeStruct((CH, 2 * LANES, 2 * LANES), BF16),
@@ -169,7 +211,7 @@
     )
     starts = jnp.cumsum(doc_lengths) - doc_lengths
     own_skip = lax.dynamic_slice(skip, (index * CH,), (CH,))
-    got = exchange(packed)
+    got, toep, starts, own_skip = lax.optimization_barrier((exchange(packed), toep, starts, own_skip))
     convolved = call(
         conv_kernel,
         msg,
@@ -185,27 +227,24 @@
         smem=3,
     )
     back = exchange(convolved)
-    gated = call(
+    groups = lax.axis_size("chan")
+    copies = call(
         gate_kernel,
-        jax.ShapeDtypeStruct((ROWS, width), BF16),
+        jax.ShapeDtypeStruct((groups, ROWS, width), BF16),
         [back, gates.reshape(ROWS, width)],
         [buf, low],
     )
-    return project(gated, weights, index)
-
-
-def project(gated, weights, index):
-    half = gated.shape[1] // 2
-    parts = [lax.all_gather(gated[:, a : a + half], "chan", axis=0) for a in (0, half)]
-    rows = jnp.concatenate(parts, axis=2)
-    rows = jnp.swapaxes(rows, 0, 1).reshape(ROWS, -1)
-    table = lax.all_gather(weights.T, SEQ, axis=0, tiled=True)
-    mixed = lax.dot_general(rows, table, (((1,), (1,)), ((), ())), preferred_element_type=F32)
-    return mixed.astype(BF16)[:, None, :]
+    rows = lax.all_to_all(copies, "chan", split_axis=0, concat_axis=0, tiled=True)
+    mixed = product(rows, table, NEAR)
+    return mixed[:, None, :]
+
+
+def gather_columns(shard):
+    return lax.all_gather(shard, ("z", "y_far", "core"), axis=0, tiled=True)
 
 
 def solution(mesh):
-    shape = dict(z=8, y=8, core=2, chan=4)
+    shape = dict(z=8, y_far=8 // NEAR, y_near=NEAR, core=2, chan=4)
     fine = Mesh(mesh.devices.reshape(tuple(shape.values())), tuple(shape))
     placed = (
         P(None, SEQ, "chan"),

time: 124 us -> 124 us (level)
  matrix products: 7.01 us -> 0 us
  Pallas kernels: 7.28 us -> 13.7 us
  waiting for transfers between devices: 29.1 us -> 32.7 us
  local copies, waits for them, and re-layouts: 3.41 us -> 1.86 us
  blocking collectives: 44.2 us -> 42.8 us
    all_gather x2 -> x0, blocking collectives: 22.6 us -> none  [project(): lax.all_gather(gated[:, a:a + half], 'chan', axis=0)]
    all_to_all x0 -> x1, blocking collectives: none -> 21.2 us  [local(): lax.all_to_all(copies, 'chan', split_axis=0, concat_axis=0, tiled=True)]
    dot_general x1 -> x0, matrix products: 7.01 us -> none  [project(): lax.dot_general(rows, table, (((1,), (1,)), ((), ())), preferred_element_...]
    pallas_call x0 -> x1, Pallas kernels: none -> 6.39 us  [product(): pl.pallas_call(functools.partial(product_kernel, near), out_shape=jax.Sha...]
    all_gather x1, waiting for transfers between devices: 13.1 us -> 16.6 us  [gather_columns(): return lax.all_gather(shard, ('z', 'y_far', 'core'), axis=0, tiled=True)]
  transfers between devices with their start and end apart: 2 -> 2, of which waited for: 2 -> 2; matrix products, arithmetic and copies ran while one was open for 3% -> 1% of each run, Pallas kernels for 6% -> 6%
where the time goes in v4:
time: 124 us; the launch traced here: 123 us
  blocking collectives  42.8 us (35%)
  waiting for transfers between devices  32.7 us (26%)
  starting transfers between devices  18.4 us (15%)
  Pallas kernels  13.7 us (11%)
  between operations  13.5 us (11%)
  local copies, waits for them, and re-layouts  1.86 us (2%)
    all_to_all x1, blocking collectives, exchange(): got = lax.all_to_all(sent, SEQ, split_axis=0, concat_axis=0, tiled=True)  21.6 us
    all_to_all x1, blocking collectives, local(): lax.all_to_all(copies, 'chan', split_axis=0, concat_axis=0, tiled=True)  21.2 us
    all_to_all x1, starting transfers between devices, exchange(): got = lax.all_to_all(sent, SEQ, split_axis=0, concat_axis=0, tiled=True)  18.4 us
    all_gather x1, waiting for transfers between devices, gather_columns(): return lax.all_gather(shard, ('z', 'y_far', 'core'), axis=0, tiled=True)  16.6 us
    all_to_all x1, waiting for transfers between devices, exchange(): got = lax.all_to_all(sent, SEQ, split_axis=0, concat_axis=0, tiled=True)  15.4 us
    pallas_call x4, Pallas kernels, call(): pl.pallas_call(kernel, out_shape=out, in_specs=in_specs, out_specs=full(o...  7.3 us
    pallas_call x1, Pallas kernels, product(): pl.pallas_call(functools.partial(product_kernel, near), out_shape=jax.Sha...  6.39 us
  transfers between devices with their start and end apart: 2, of which 2 were waited for; matrix products, arithmetic and copies ran while one was open for 1% of the time, Pallas kernels for 6%

profile of v4, /device:TPU:1, one launch (start us, length us, event | category | flops | bytes accessed | tf_op | source)
XLA Modules:
  0.0 123.2 jit_solution(641564804570688283)
XLA Ops:
  6.5 0.0 copy-start
  6.5 0.0 all-gather.2.cloned.1.call-start
  6.5 0.7 all-gather.2.cloned.1.call-update
  7.3 0.0 copy-start.1
  7.3 1.0 copy-done.1
  8.2 0.0 copy-start.3
  8.2 1.1 shard_map.64
  9.4 18.4 %all-to-all-start = ((bf16[128,5,2,128]{3,2,1,0:T(2,128)(2,1)}), bf16[128,5,2,128]{3,2,1,0:T(2,128)(2,1)S(1)}, u32[]{:S(2)}, u32[]{:S(2)}) async-start(bf16[128,5,2,128]{3,2,1,0:T(2,128)(2,1)} %bitcast.1), calls=%async_computation | async-start | bytes 655360 | tf_op jit(solution)/shard_map/all_to_all | solution.py:192
  27.8 0.0 copy-done.3
  27.8 0.1 copy.8
  27.9 0.2 reduce-window.9
  28.1 0.1 reduce
  28.2 0.8 dynamic_slice.3.skip_ref
  29.0 0.0 copy-done
  29.0 0.4 shard_map.65.toep_ref
  29.4 0.0 copy-start.2
  29.4 15.4 %all-to-all-done = bf16[128,5,2,128]{3,2,1,0:T(2,128)(2,1)S(1)} async-done(((bf16[128,5,2,128]{3,2,1,0:T(2,128)(2,1)}), bf16[128,5,2,128]{3,2,1,0:T(2,128)(2,1)S(1)}, u32[]{:S(2)}, u32[]{:S(2)}) %all-to-all-start) | async-done | bytes 327712 | tf_op jit(solution)/shard_map/all_to_all | solution.py:192
  44.7 5.4 %shard_map.66 = bf16[1280,128]{1,0:T(8,128)(2,1)S(1)} custom-call(s32[128]{0:T(128)S(1)} %sub.3.start_ref, s32[128]{0:T(128)S(1)} %copy-done.3, f32[8]{0:T(128)S(1)} %dynamic_slice.3.skip_ref, bf16[1280,128]{1,0:T(8,128)(2,1)S(1)} %bitcast.10, bf16[8,256,256]{2,1,0:T(8,128)(2,1)S(1)} %shard_map.65.toep_ref), custom_call_target="tpu_custom_call" | custom-call | flops 134217728 | bytes 1704992 | tf_op jit(solution)/shard_map/pallas_call | solution.py:37
  50.1 21.6 %all_to_all.15 = bf16[128,5,2,128]{3,2,1,0:T(2,128)(2,1)S(1)} all-to-all(bf16[128,5,2,128]{3,2,1,0:T(2,128)(2,1)S(1)} %bitcast.11), channel_id=1, replica_groups=mesh['z'=8,'y_far'=8,'y_near'=1,'core'=2,'chan'=4] {'z','y_far','y_near'..., dimensions={0} | all-to-all | bytes 655360 | tf_op jit(solution)/shard_map/all_to_all | solution.py:192
  71.7 0.0 copy-done.2
  71.7 0.4 shard_map.67
  72.1 21.2 %all_to_all.16.rows_ref = bf16[4,160,1024]{2,1,0:T(8,128)(2,1)S(1)} all-to-all(bf16[4,160,1024]{2,1,0:T(8,128)(2,1)S(1)} %shard_map.67), channel_id=1, replica_groups=mesh['z'=8,'y_far'=8,'y_near'=1,'core'=2,'chan'=4] {'chan'}, dimensions={0} | all-to-all | bytes 2621440 | tf_op jit(solution)/shard_map/all_to_all | solution.py:237
  93.4 16.6 %all-gather.2.cloned.1.call-done.w_ref = bf16[1024,4096]{1,0:T(8,128)(2,1)} async-done(((bf16[8,4096]{1,0:T(8,128)(2,1)}), bf16[1024,4096]{1,0:T(8,128)(2,1)}) %all-gather.2.cloned.1.call-update) | async-done | bytes 8388624 | tf_op jit(solution)/shard_map/all_gather | solution.py:243
  109.9 6.4 %shard_map.68 = bf16[160,1024]{1,0:T(8,128)(2,1)} custom-call(bf16[4,160,1024]{2,1,0:T(8,128)(2,1)S(1)} %all_to_all.16.rows_ref, bf16[1024,4096]{1,0:T(8,128)(2,1)} %all-gather.2.cloned.1.call-done.w_ref), custom_call_target="tpu_custom_call" | custom-call | flops 1342177280 | bytes 10027008 | tf_op jit(solution)/shard_map/pallas_call | solution.py:172
  (1 shorter events, 0.0 us)
Async XLA Ops:
  6.5 22.5 %copy-start = (bf16[256,1024]{1,0:T(8,128)(2,1)S(1)}, bf16[256,1024]{1,0:T(8,128)(2,1)}, u32[]{:S(2)}) copy-start(bf16[256,1024]{1,0:T(8,128)(2,1)} %f_ref) | copy-start | bytes 1572868
  6.5 103.4 %all-gather.2.cloned.1.call-start = ((), (), s32[]{:S(2)}) async-start(), calls=%async_computation.3 | async-start | bytes 8454144 | tf_op jit(solution)/shard_map/all_gather | solution.py:243
  7.3 1.0 copy-start.1
  8.2 19.6 %copy-start.3 = (s32[128]{0:T(128)S(1)}, s32[128]{0:T(128)}, u32[]{:S(2)}) copy-start(s32[128]{0:T(128)} %length_ref) | copy-start | bytes 1540
  9.4 35.4 %all-to-all-start = ((bf16[128,5,2,128]{3,2,1,0:T(2,128)(2,1)}), bf16[128,5,2,128]{3,2,1,0:T(2,128)(2,1)S(1)}, u32[]{:S(2)}, u32[]{:S(2)}) async-start(bf16[128,5,2,128]{3,2,1,0:T(2,128)(2,1)} %bitcast.1), calls=%async_computation | async-start | bytes 655360 | tf_op jit(solution)/shard_map/all_to_all | solution.py:192
  29.4 42.3 %copy-start.2 = (bf16[160,1,1024]{2,0,1:T(8,128)(2,1)S(1)}, bf16[160,1,1024]{2,0,1:T(8,128)(2,1)}, u32[]{:S(2)}) copy-start(bf16[160,1,1024]{2,0,1:T(8,128)(2,1)} %param.7) | copy-start | bytes 983044
Sparse Core Ops, SparseCore 0:
  10.5 99.4 all-gather.1

commit v5 on v4

--- a/solution.py
+++ b/solution.py
@@ -21,7 +21,7 @@
 MSG = PEERS * PER
 VMEM_LIMIT = 48 * 1024 * 1024
 SEQ = ("z", "y_far", "y_near", "core")
-NEAR = 1
+NEAR = 4
 
 
 def full(shape):
@@ -240,6 +240,7 @@
 
 
 def gather_columns(shard):
+    shard = lax.all_gather(shard, "y_near", axis=0, tiled=True)
     return lax.all_gather(shard, ("z", "y_far", "core"), axis=0, tiled=True)
 
 

time: 124 us -> 185 us (1.49)
  waiting for transfers between devices: 32.7 us -> 77.2 us
  blocking collectives: 42.8 us -> 59.4 us
    all_gather x1, waiting for transfers between devices: 16.6 us -> 58.5 us  [gather_columns(): return lax.all_gather(shard, ('z', 'y_far', 'core'), axis=0, tiled=True)]
    all_gather x0 -> x1, blocking collectives: none -> 14.6 us  [gather_columns(): shard = lax.all_gather(shard, 'y_near', axis=0, tiled=True)]
    all_to_all x1, waiting for transfers between devices: 15.4 us -> 18.7 us  [exchange(): got = lax.all_to_all(sent, SEQ, split_axis=0, concat_axis=0, tiled=True)]
    all_to_all x1, blocking collectives: 21.6 us -> 23.4 us  [exchange(): got = lax.all_to_all(sent, SEQ, split_axis=0, concat_axis=0, tiled=True)]
  transfers between devices with their start and end apart: 2 -> 2, of which waited for: 2 -> 2; matrix products, arithmetic and copies ran while one was open for 1% -> 1% of each run, Pallas kernels for 6% -> 4%
where the time goes in v5:
time: 185 us
  waiting for transfers between devices  77.2 us (42%)
  blocking collectives  59.4 us (32%)
  starting transfers between devices  18.7 us (10%)
  Pallas kernels  13.7 us (7%)
  between operations  13.5 us (7%)
  local copies, waits for them, and re-layouts  1.86 us (1%)
    all_gather x1, waiting for transfers between devices, gather_columns(): return lax.all_gather(shard, ('z', 'y_far', 'core'), axis=0, tiled=True)  58.5 us
    all_to_all x1, blocking collectives, exchange(): got = lax.all_to_all(sent, SEQ, split_axis=0, concat_axis=0, tiled=True)  23.4 us
    all_to_all x1, blocking collectives, local(): lax.all_to_all(copies, 'chan', split_axis=0, concat_axis=0, tiled=True)  21.3 us
    all_to_all x1, starting transfers between devices, exchange(): got = lax.all_to_all(sent, SEQ, split_axis=0, concat_axis=0, tiled=True)  18.7 us
    all_to_all x1, waiting for transfers between devices, exchange(): got = lax.all_to_all(sent, SEQ, split_axis=0, concat_axis=0, tiled=True)  18.7 us
    all_gather x1, blocking collectives, gather_columns(): shard = lax.all_gather(shard, 'y_near', axis=0, tiled=True)  14.6 us
    pallas_call x4, Pallas kernels, call(): pl.pallas_call(kernel, out_shape=out, in_specs=in_specs, out_specs=full(o...  7.3 us
    pallas_call x1, Pallas kernels, product(): pl.pallas_call(functools.partial(product_kernel, near), out_shape=jax.Sha...  6.41 us
  transfers between devices with their start and end apart: 2, of which 2 were waited for; matrix products, arithmetic and copies ran while one was open for 1% of the time, Pallas kernels for 4%

profile of v5, /device:TPU:1, one launch (start us, length us, event | category | flops | bytes accessed | tf_op | source)
XLA Modules:
  0.0 184.6 jit_solution(17101381841771703426)
XLA Ops:
  6.5 0.0 copy-start.3
  6.5 0.0 copy-start
  6.5 0.0 all-gather.2.cloned.1.call-start
  6.5 14.6 %all_gather.6 = bf16[32,4096]{1,0:T(8,128)(2,1)} all-gather(bf16[8,4096]{1,0:T(8,128)(2,1)} %bitcast.16), channel_id=1, replica_groups=mesh['z'=8,'y_far'=2,'y_near'=4,'core'=2,'chan'=4] {'y_near'}, dimensions={0}, use_global_device_ids=true | all-gather | bytes 327680 | tf_op jit(solution)/shard_map/all_gather | solution.py:243
  21.1 0.0 all-gather.2.cloned.1.call-update
  21.2 0.0 copy-start.1
  21.2 1.0 copy-done.1
  22.1 1.1 shard_map.64
  23.3 18.7 %all-to-all-start = ((bf16[128,5,2,128]{3,2,1,0:T(2,128)(2,1)}), bf16[128,5,2,128]{3,2,1,0:T(2,128)(2,1)S(1)}, u32[]{:S(2)}, u32[]{:S(2)}) async-start(bf16[128,5,2,128]{3,2,1,0:T(2,128)(2,1)} %bitcast.1), calls=%async_computation | async-start | bytes 655360 | tf_op jit(solution)/shard_map/all_to_all | solution.py:192
  42.0 0.0 copy-done.3
  42.0 0.1 copy.8
  42.1 0.2 reduce-window.9
  42.3 0.1 reduce
  42.4 0.8 dynamic_slice.3.skip_ref
  43.2 0.0 copy-done
  43.2 0.4 shard_map.65.toep_ref
  43.5 0.0 copy-start.2
  43.5 18.7 %all-to-all-done = bf16[128,5,2,128]{3,2,1,0:T(2,128)(2,1)S(1)} async-done(((bf16[128,5,2,128]{3,2,1,0:T(2,128)(2,1)}), bf16[128,5,2,128]{3,2,1,0:T(2,128)(2,1)S(1)}, u32[]{:S(2)}, u32[]{:S(2)}) %all-to-all-start) | async-done | bytes 327712 | tf_op jit(solution)/shard_map/all_to_all | solution.py:192
  62.2 5.4 %shard_map.66 = bf16[1280,128]{1,0:T(8,128)(2,1)S(1)} custom-call(s32[128]{0:T(128)S(1)} %sub.3.start_ref, s32[128]{0:T(128)S(1)} %copy-done.3, f32[8]{0:T(128)S(1)} %dynamic_slice.3.skip_ref, bf16[1280,128]{1,0:T(8,128)(2,1)S(1)} %bitcast.10, bf16[8,256,256]{2,1,0:T(8,128)(2,1)S(1)} %shard_map.65.toep_ref), custom_call_target="tpu_custom_call" | custom-call | flops 134217728 | bytes 1704992 | tf_op jit(solution)/shard_map/pallas_call | solution.py:37
  67.6 23.4 %all_to_all.15 = bf16[128,5,2,128]{3,2,1,0:T(2,128)(2,1)S(1)} all-to-all(bf16[128,5,2,128]{3,2,1,0:T(2,128)(2,1)S(1)} %bitcast.11), channel_id=1, replica_groups=mesh['z'=8,'y_far'=2,'y_near'=4,'core'=2,'chan'=4] {'z','y_far','y_near'..., dimensions={0} | all-to-all | bytes 655360 | tf_op jit(solution)/shard_map/all_to_all | solution.py:192
  91.0 0.0 copy-done.2
  91.0 0.4 shard_map.67
  91.5 21.3 %all_to_all.16.rows_ref = bf16[4,160,1024]{2,1,0:T(8,128)(2,1)S(1)} all-to-all(bf16[4,160,1024]{2,1,0:T(8,128)(2,1)S(1)} %shard_map.67), channel_id=1, replica_groups=mesh['z'=8,'y_far'=2,'y_near'=4,'core'=2,'chan'=4] {'chan'}, dimensions={0} | all-to-all | bytes 2621440 | tf_op jit(solution)/shard_map/all_to_all | solution.py:237
  112.8 58.5 %all-gather.2.cloned.1.call-done.w_ref = bf16[1024,4096]{1,0:T(8,128)(2,1)} async-done(((bf16[32,4096]{1,0:T(8,128)(2,1)}), bf16[1024,4096]{1,0:T(8,128)(2,1)}) %all-gather.2.cloned.1.call-update) | async-done | bytes 8388624 | tf_op jit(solution)/shard_map/all_gather | solution.py:244
  171.3 6.4 %shard_map.68 = bf16[160,1024]{1,0:T(8,128)(2,1)} custom-call(bf16[4,160,1024]{2,1,0:T(8,128)(2,1)S(1)} %all_to_all.16.rows_ref, bf16[1024,4096]{1,0:T(8,128)(2,1)} %all-gather.2.cloned.1.call-done.w_ref), custom_call_target="tpu_custom_call" | custom-call | flops 1342177280 | bytes 10027008 | tf_op jit(solution)/shard_map/pallas_call | solution.py:172
  (1 shorter events, 0.0 us)
Async XLA Ops:
  6.5 35.4 %copy-start.3 = (s32[128]{0:T(128)S(1)}, s32[128]{0:T(128)}, u32[]{:S(2)}) copy-start(s32[128]{0:T(128)} %length_ref) | copy-start | bytes 1540
  6.5 36.6 %copy-start = (bf16[256,1024]{1,0:T(8,128)(2,1)S(1)}, bf16[256,1024]{1,0:T(8,128)(2,1)}, u32[]{:S(2)}) copy-start(bf16[256,1024]{1,0:T(8,128)(2,1)} %f_ref) | copy-start | bytes 1572868
  6.5 164.8 %all-gather.2.cloned.1.call-start = ((), (), s32[]{:S(2)}) async-start(), calls=%async_computation.3 | async-start | bytes 8650752 | tf_op jit(solution)/shard_map/all_gather | solution.py:244
  21.2 1.0 copy-start.1
  23.3 38.9 %all-to-all-start = ((bf16[128,5,2,128]{3,2,1,0:T(2,128)(2,1)}), bf16[128,5,2,128]{3,2,1,0:T(2,128)(2,1)S(1)}, u32[]{:S(2)}, u32[]{:S(2)}) async-start(bf16[128,5,2,128]{3,2,1,0:T(2,128)(2,1)} %bitcast.1), calls=%async_computation | async-start | bytes 655360 | tf_op jit(solution)/shard_map/all_to_all | solution.py:192
  43.5 47.5 %copy-start.2 = (bf16[160,1,1024]{2,0,1:T(8,128)(2,1)S(1)}, bf16[160,1,1024]{2,0,1:T(8,128)(2,1)}, u32[]{:S(2)}) copy-start(bf16[160,1,1024]{2,0,1:T(8,128)(2,1)} %param.7) | copy-start | bytes 983044
Sparse Core Ops, SparseCore 0:
  21.3 149.9 all-gather.1

commit v6 on v4

--- a/solution.py
+++ b/solution.py
@@ -20,8 +20,7 @@
 PEERS = 128
 MSG = PEERS * PER
 VMEM_LIMIT = 48 * 1024 * 1024
-SEQ = ("z", "y_far", "y_near", "core")
-NEAR = 1
+SEQ = ("z", "y_half", "y_rest", "core")
 
 
 def full(shape):
@@ -151,32 +150,30 @@
             out_ref[q, HEAD:, cols] = tail
 
 
-def product_kernel(near, rows_ref, w_ref, out_ref):
-    groups, _, width = rows_ref.shape
-    total = jnp.zeros((w_ref.shape[0], ROWS), F32)
-    for q in range(groups):
-        part = w_ref[:, q * width : (q + 1) * width]
-        total += lax.dot_general(part, rows_ref[q], (((1,), (1,)), ((), ())), preferred_element_type=F32)
-    for j in range(w_ref.shape[0] // LANES):
+def product_kernel(rows_ref, *refs):
+    *w_refs, out_ref = refs
+    total = jnp.zeros((w_refs[0].shape[0], ROWS), F32)
+    for q, w_ref in enumerate(w_refs):
+        total += lax.dot_general(w_ref[...], rows_ref[q], (((1,), (1,)), ((), ())), preferred_element_type=F32)
+    for j in range(w_refs[0].shape[0] // LANES):
         parts = []
         for y in range(8):
             for core in range(2):
-                group = 16 * j + y // near * 2 * near + core * near + y % near
+                group = 16 * j + 4 * (y % 4) + 2 * core + y // 4
                 parts.append(total[group * CH : (group + 1) * CH])
         block = jnp.concatenate(parts, axis=0)
         out_ref[:, j * LANES : (j + 1) * LANES] = block.T.astype(BF16)
 
 
-def product(rows, table, near):
+def product(rows, table):
     block = 256
+    groups, _, width = rows.shape
+    streams = [pl.BlockSpec((block, width), functools.partial(lambda q, j: (j, q), q)) for q in range(groups)]
     return pl.pallas_call(
-        functools.partial(product_kernel, near),
+        product_kernel,
         out_shape=jax.ShapeDtypeStruct((ROWS, table.shape[0]), BF16),
         grid=(table.shape[0] // block,),
-        in_specs=[
-            pl.BlockSpec(rows.shape, lambda j: (0, 0, 0)),
-            pl.BlockSpec((block, table.shape[1]), lambda j: (j, 0)),
-        ],
+        in_specs=[pl.BlockSpec(rows.shape, lambda j: (0, 0, 0)), *streams],
         out_specs=pl.BlockSpec((ROWS, block), lambda j: (0, j)),
         compiler_params=pltpu.CompilerParams(vmem_limit_bytes=VMEM_LIMIT),
         cost_estimate=pl.CostEstimate(
@@ -184,7 +181,7 @@
             bytes_accessed=2 * (table.size + rows.size + ROWS * table.shape[0]),
             transcendentals=0,
         ),
-    )(rows, table)
+    )(rows, *[table] * groups)
 
 
 def exchange(message):
@@ -235,16 +232,17 @@
         [buf, low],
     )
     rows = lax.all_to_all(copies, "chan", split_axis=0, concat_axis=0, tiled=True)
-    mixed = product(rows, table, NEAR)
+    mixed = product(rows, table)
     return mixed[:, None, :]
 
 
 def gather_columns(shard):
-    return lax.all_gather(shard, ("z", "y_far", "core"), axis=0, tiled=True)
+    pair = lax.all_gather(shard, "y_half", axis=0, tiled=True)
+    return lax.all_gather(pair, ("z", "y_rest", "core"), axis=0, tiled=True)
 
 
 def solution(mesh):
-    shape = dict(z=8, y_far=8 // NEAR, y_near=NEAR, core=2, chan=4)
+    shape = dict(z=8, y_half=2, y_rest=4, core=2, chan=4)
     fine = Mesh(mesh.devices.reshape(tuple(shape.values())), tuple(shape))
     placed = (
         P(None, SEQ, "chan"),

time: 124 us -> 169 us (1.36)
  the two profiles are of different devices: /device:TPU:1 before, /device:TPU:53 now
where the time goes in v6:
time: 169 us; the launch traced here: 168 us
  waiting for transfers between devices  69 us (41%)
  blocking collectives  51.3 us (30%)
  starting transfers between devices  18.7 us (11%)
  Pallas kernels  13.6 us (8%)
  between operations  13.5 us (8%)
  local copies, waits for them, and re-layouts  1.86 us (1%)
    all_gather x1, waiting for transfers between devices, gather_columns(): return lax.all_gather(pair, ('z', 'y_rest', 'core'), axis=0, tiled=True)  55.2 us
    all_to_all x1, blocking collectives, exchange(): got = lax.all_to_all(sent, SEQ, split_axis=0, concat_axis=0, tiled=True)  24.5 us
    all_to_all x1, starting transfers between devices, exchange(): got = lax.all_to_all(sent, SEQ, split_axis=0, concat_axis=0, tiled=True)  18.7 us
    all_to_all x1, blocking collectives, local(): lax.all_to_all(copies, 'chan', split_axis=0, concat_axis=0, tiled=True)  18.7 us
    all_to_all x1, waiting for transfers between devices, exchange(): got = lax.all_to_all(sent, SEQ, split_axis=0, concat_axis=0, tiled=True)  13.8 us
    all_gather x1, blocking collectives, gather_columns(): pair = lax.all_gather(shard, 'y_half', axis=0, tiled=True)  8.13 us
    pallas_call x4, Pallas kernels, call(): pl.pallas_call(kernel, out_shape=out, in_specs=in_specs, out_specs=full(o...  7.3 us
    pallas_call x1, Pallas kernels, product(): pl.pallas_call(product_kernel, out_shape=jax.ShapeDtypeStruct((ROWS, tabl...  6.33 us
  transfers between devices with their start and end apart: 2, of which 2 were waited for; matrix products, arithmetic and copies ran while one was open for 1% of the time, Pallas kernels for 4%

profile of v6, /device:TPU:53, one launch (start us, length us, event | category | flops | bytes accessed | tf_op | source)
XLA Modules:
  0.0 168.3 jit_solution(13825993643241864248)
XLA Ops:
  6.5 0.0 copy-start
  6.5 0.0 all-gather.2.cloned.1.call-start
  6.5 8.1 %all_gather.6 = bf16[16,4096]{1,0:T(8,128)(2,1)} all-gather(bf16[8,4096]{1,0:T(8,128)(2,1)} %bitcast.16), channel_id=1, replica_groups=mesh['z'=8,'y_half'=2,'y_rest'=4,'core'=2,'chan'=4] {'y_half'}, dimensions={0}, use_global_device_ids=true | all-gather | bytes 196608 | tf_op jit(solution)/shard_map/all_gather | solution.py:240
  14.7 0.0 all-gather.2.cloned.1.call-update
  14.7 0.0 copy-start.1
  14.7 1.0 copy-done.1
  15.7 0.0 copy-start.3
  15.7 1.1 shard_map.64
  16.8 18.7 %all-to-all-start = ((bf16[128,5,2,128]{3,2,1,0:T(2,128)(2,1)}), bf16[128,5,2,128]{3,2,1,0:T(2,128)(2,1)S(1)}, u32[]{:S(2)}, u32[]{:S(2)}) async-start(bf16[128,5,2,128]{3,2,1,0:T(2,128)(2,1)} %bitcast.1), calls=%async_computation | async-start | bytes 655360 | tf_op jit(solution)/shard_map/all_to_all | solution.py:189
  35.5 0.0 copy-done.3
  35.5 0.1 copy.8
  35.7 0.2 reduce-window.9
  35.8 0.1 reduce
  35.9 0.8 dynamic_slice.3.skip_ref
  36.7 0.0 copy-done
  36.7 0.4 shard_map.65.toep_ref
  37.1 0.0 copy-start.2
  37.1 13.8 %all-to-all-done = bf16[128,5,2,128]{3,2,1,0:T(2,128)(2,1)S(1)} async-done(((bf16[128,5,2,128]{3,2,1,0:T(2,128)(2,1)}), bf16[128,5,2,128]{3,2,1,0:T(2,128)(2,1)S(1)}, u32[]{:S(2)}, u32[]{:S(2)}) %all-to-all-start) | async-done | bytes 327712 | tf_op jit(solution)/shard_map/all_to_all | solution.py:189
  50.9 5.4 %shard_map.66 = bf16[1280,128]{1,0:T(8,128)(2,1)S(1)} custom-call(s32[128]{0:T(128)S(1)} %sub.3.start_ref, s32[128]{0:T(128)S(1)} %copy-done.3, f32[8]{0:T(128)S(1)} %dynamic_slice.3.skip_ref, bf16[1280,128]{1,0:T(8,128)(2,1)S(1)} %bitcast.10, bf16[8,256,256]{2,1,0:T(8,128)(2,1)S(1)} %shard_map.65.toep_ref), custom_call_target="tpu_custom_call" | custom-call | flops 134217728 | bytes 1704992 | tf_op jit(solution)/shard_map/pallas_call | solution.py:36
  56.3 24.5 %all_to_all.15 = bf16[128,5,2,128]{3,2,1,0:T(2,128)(2,1)S(1)} all-to-all(bf16[128,5,2,128]{3,2,1,0:T(2,128)(2,1)S(1)} %bitcast.11), channel_id=1, replica_groups=mesh['z'=8,'y_half'=2,'y_rest'=4,'core'=2,'chan'=4] {'z','y_half','y_res..., dimensions={0} | all-to-all | bytes 655360 | tf_op jit(solution)/shard_map/all_to_all | solution.py:189
  80.8 0.0 copy-done.2
  80.8 0.4 shard_map.67
  81.2 18.7 %all_to_all.16.rows_ref = bf16[4,160,1024]{2,1,0:T(8,128)(2,1)S(1)} all-to-all(bf16[4,160,1024]{2,1,0:T(8,128)(2,1)S(1)} %shard_map.67), channel_id=1, replica_groups=mesh['z'=8,'y_half'=2,'y_rest'=4,'core'=2,'chan'=4] {'chan'}, dimensions={0} | all-to-all | bytes 2621440 | tf_op jit(solution)/shard_map/all_to_all | solution.py:234
  99.9 55.2 %all-gather.2.cloned.1.call-done.refs_0_.refs_1_.refs_2_.refs_3_ = bf16[1024,4096]{1,0:T(8,128)(2,1)} async-done(((bf16[16,4096]{1,0:T(8,128)(2,1)}), bf16[1024,4096]{1,0:T(8,128)(2,1)}) %all-gather.2.cloned.1.call-update) | async-done | bytes 8388624 | tf_op jit(solution)/shard_map/all_gather | solution.py:241
  155.1 6.3 %shard_map.68 = bf16[160,1024]{1,0:T(8,128)(2,1)} custom-call(bf16[4,160,1024]{2,1,0:T(8,128)(2,1)S(1)} %all_to_all.16.rows_ref, bf16[1024,4096]{1,0:T(8,128)(2,1)} %all-gather.2.cloned.1.call-done.refs_0_.refs_1_.refs_2_.refs_3_, bf16[1024,4096]{1,0:T(8,128)(2,1)} %all-gather.2.cloned.1.call-done.refs_0_.refs_1_.refs_2_.refs_3_, ...), custom_call_target="tpu_custom_call" | custom-call | flops 1342177280 | bytes 10027008 | tf_op jit(solution)/shard_map/pallas_call | solution.py:172
  (1 shorter events, 0.0 us)
Async XLA Ops:
  6.5 30.2 %copy-start = (bf16[256,1024]{1,0:T(8,128)(2,1)S(1)}, bf16[256,1024]{1,0:T(8,128)(2,1)}, u32[]{:S(2)}) copy-start(bf16[256,1024]{1,0:T(8,128)(2,1)} %f_ref) | copy-start | bytes 1572868
  6.5 148.6 %all-gather.2.cloned.1.call-start = ((), (), s32[]{:S(2)}) async-start(), calls=%async_computation.3 | async-start | bytes 8519680 | tf_op jit(solution)/shard_map/all_gather | solution.py:241
  14.7 1.0 copy-start.1
  15.7 19.9 %copy-start.3 = (s32[128]{0:T(128)S(1)}, s32[128]{0:T(128)}, u32[]{:S(2)}) copy-start(s32[128]{0:T(128)} %length_ref) | copy-start | bytes 1540
  16.8 34.1 %all-to-all-start = ((bf16[128,5,2,128]{3,2,1,0:T(2,128)(2,1)}), bf16[128,5,2,128]{3,2,1,0:T(2,128)(2,1)S(1)}, u32[]{:S(2)}, u32[]{:S(2)}) async-start(bf16[128,5,2,128]{3,2,1,0:T(2,128)(2,1)} %bitcast.1), calls=%async_computation | async-start | bytes 655360 | tf_op jit(solution)/shard_map/all_to_all | solution.py:189
  37.1 43.7 %copy-start.2 = (bf16[160,1,1024]{2,0,1:T(8,128)(2,1)S(1)}, bf16[160,1,1024]{2,0,1:T(8,128)(2,1)}, u32[]{:S(2)}) copy-start(bf16[160,1,1024]{2,0,1:T(8,128)(2,1)} %param.7) | copy-start | bytes 983044
Sparse Core Ops, SparseCore 0:
  14.8 140.2 all-gather.1

commit v7 on v0

--- a/solution.py
+++ b/solution.py
@@ -1,5 +1,3 @@
-import functools
-
 import jax
 import jax.numpy as jnp
 from jax import lax
@@ -142,9 +140,69 @@
         cols = slice(j * LANES, (j + 1) * LANES)
         head = [msg[pl.ds((16 * j + g) * PER, CH), :] for g in range(16)]
         head = jnp.concatenate(head, axis=0).T
-        out_ref[:HEAD, cols] = (head * g_ref[:HEAD, cols].astype(F32)).astype(BF16)
+        head = (head * g_ref[:HEAD, cols].astype(F32)).astype(BF16)
         tail = low[cols, :].T[:TAIL]
-        out_ref[HEAD:, cols] = (tail * g_ref[HEAD:, cols].astype(F32)).astype(BF16)
+        tail = (tail * g_ref[HEAD:, cols].astype(F32)).astype(BF16)
+        for q in range(out_ref.shape[0]):
+            out_ref[q, :HEAD, cols] = head
+            out_ref[q, HEAD:, cols] = tail
+
+
+def product_kernel(rows_ref, twin_ref, w_ref, mine_ref, twins_ref, total):
+    step = pl.program_id(0)
+
+    def term(ref):
+        return lax.dot_general(w_ref[...], ref[0], (((1,), (1,)), ((), ())), preferred_element_type=F32)
+
+    @pl.when(step == 0)
+    def _():
+        mine_ref[...] = term(rows_ref)
+        total[...] = term(twin_ref)
+
+    @pl.when(step > 0)
+    def _():
+        mine_ref[...] += term(rows_ref)
+        total[...] += term(twin_ref)
+
+    @pl.when(step == pl.num_programs(0) - 1)
+    def _():
+        twins_ref[...] = total[...].astype(BF16)
+
+
+def product(rows, twin_rows, columns):
+    groups, count, width = rows.shape
+    wide = columns.shape[0]
+    part = pl.BlockSpec((1, count, width), lambda q: (q, 0, 0))
+    result = pl.BlockSpec((wide, count), lambda q: (0, 0))
+    return pl.pallas_call(
+        product_kernel,
+        out_shape=[jax.ShapeDtypeStruct((wide, count), F32), jax.ShapeDtypeStruct((wide, count), BF16)],
+        grid=(groups,),
+        in_specs=[part, part, pl.BlockSpec((wide, width), lambda q: (0, q))],
+        out_specs=[result, result],
+        scratch_shapes=[pltpu.VMEM((wide, count), F32)],
+        compiler_params=pltpu.CompilerParams(vmem_limit_bytes=VMEM_LIMIT),
+        cost_estimate=pl.CostEstimate(
+            flops=4 * count * columns.size,
+            bytes_accessed=2 * (columns.size + 2 * rows.size + 3 * wide * count),
+            transcendentals=0,
+        ),
+    )(rows, twin_rows, columns)
+
+
+def join_kernel(core_ref, mine_ref, other_ref, out_ref, zero, one):
+    other = other_ref[...].astype(F32)
+    first = core_ref[0] == 0
+    mine = mine_ref[...]
+    zero[...] = jnp.where(first, mine, other)
+    one[...] = jnp.where(first, other, mine)
+    for z in range(8):
+        parts = []
+        for y in range(8):
+            rows = slice((8 * z + y) * CH, (8 * z + y + 1) * CH)
+            parts += [zero[rows, :], one[rows, :]]
+        block = jnp.concatenate(parts, axis=0)
+        out_ref[:, z * LANES : (z + 1) * LANES] = block.T.astype(BF16)
 
 
 def exchange(message):
@@ -160,6 +218,8 @@
     buf = pltpu.VMEM((MSG, LANES), F32)
     low = pltpu.VMEM((width, LANES), F32)
     packed = call(pack_kernel, msg, [values.reshape(ROWS, width)], [buf, low])
+    table = gather_columns(weights.T)
+    packed, filters, doc_lengths, skip = lax.optimization_barrier((packed, filters, doc_lengths, skip))
     toep = call(
         toeplitz_kernel,
         jax.ShapeDtypeStruct((CH, 2 * LANES, 2 * LANES), BF16),
@@ -169,7 +229,7 @@
     )
     starts = jnp.cumsum(doc_lengths) - doc_lengths
     own_skip = lax.dynamic_slice(skip, (index * CH,), (CH,))
-    got = exchange(packed)
+    got, toep, starts, own_skip = lax.optimization_barrier((exchange(packed), toep, starts, own_skip))
     convolved = call(
         conv_kernel,
         msg,
@@ -185,23 +245,29 @@
         smem=3,
     )
     back = exchange(convolved)
-    gated = call(
+    groups = lax.axis_size("chan")
+    copies = call(
         gate_kernel,
-        jax.ShapeDtypeStruct((ROWS, width), BF16),
+        jax.ShapeDtypeStruct((groups, ROWS, width), BF16),
         [back, gates.reshape(ROWS, width)],
         [buf, low],
     )
-    return project(gated, weights, index)
-
-
-def project(gated, weights, index):
-    half = gated.shape[1] // 2
-    parts = [lax.all_gather(gated[:, a : a + half], "chan", axis=0) for a in (0, half)]
-    rows = jnp.concatenate(parts, axis=2)
-    rows = jnp.swapaxes(rows, 0, 1).reshape(ROWS, -1)
-    table = lax.all_gather(weights.T, SEQ, axis=0, tiled=True)
-    mixed = lax.dot_general(rows, table, (((1,), (1,)), ((), ())), preferred_element_type=F32)
-    return mixed.astype(BF16)[:, None, :]
+    rows = lax.all_to_all(copies, "chan", split_axis=0, concat_axis=0, tiled=True)
+    swap = [(0, 1), (1, 0)]
+    mine, twins = product(rows, lax.ppermute(rows, "core", swap), table)
+    place = pltpu.VMEM(mine.shape, F32)
+    mixed = call(
+        join_kernel,
+        jax.ShapeDtypeStruct((ROWS, width), BF16),
+        [lax.rem(index, 2)[None], mine, lax.ppermute(twins, "core", swap)],
+        [place, place],
+        smem=1,
+    )
+    return mixed[:, None, :]
+
+
+def gather_columns(shard):
+    return lax.all_gather(shard, ("z", "y"), axis=0, tiled=True)
 
 
 def solution(mesh):

time: 124 us -> 124 us (level)
  starting transfers between devices: 18.4 us -> 28.5 us
  matrix products: 7.01 us -> 0 us
  Pallas kernels: 7.28 us -> 13 us
  waiting for transfers between devices: 29.1 us -> 24.4 us
  blocking collectives: 44.2 us -> 42.5 us
  local copies, waits for them, and re-layouts: 3.41 us -> 1.86 us
    all_gather x2 -> x0, blocking collectives: 22.6 us -> none  [project(): lax.all_gather(gated[:, a:a + half], 'chan', axis=0)]
    all_to_all x0 -> x1, blocking collectives: none -> 20.9 us  [local(): lax.all_to_all(copies, 'chan', split_axis=0, concat_axis=0, tiled=True)]
    ppermute x0 -> x2, starting transfers between devices: none -> 10.1 us  [the longest x1 6.47 us: local(): lax.ppermute(twins, 'core', swap)]
    all_gather x1, waiting for transfers between devices: 13.1 us -> 4.58 us  [gather_columns(): return lax.all_gather(shard, ('z', 'y'), axis=0, tiled=True)]
    dot_general x1 -> x0, matrix products: 7.01 us -> none  [project(): lax.dot_general(rows, table, (((1,), (1,)), ((), ())), preferred_element_...]
    pallas_call x0 -> x1, Pallas kernels: none -> 4.76 us  [product(): pl.pallas_call(product_kernel, out_shape=[jax.ShapeDtypeStruct((wide, cou...]
    ppermute x0 -> x2, waiting for transfers between devices: none -> 3.78 us  [the longest x1 2.64 us: local(): mine, twins = product(rows, lax.ppermute(rows, 'core', swap), table)]
    pallas_call x4 -> x5, Pallas kernels: 7.28 us -> 8.24 us  [call(): pl.pallas_call(kernel, out_shape=out, in_specs=in_specs, out_specs=full(o...]
  transfers between devices with their start and end apart: 2 -> 4, of which waited for: 2 -> 4; matrix products, arithmetic and copies ran while one was open for 3% -> 1% of each run, Pallas kernels for 6% -> 6%
where the time goes in v7:
time: 124 us
  blocking collectives  42.5 us (34%)
  starting transfers between devices  28.5 us (23%)
  waiting for transfers between devices  24.4 us (20%)
  between operations  13.5 us (11%)
  Pallas kernels  13 us (10%)
  local copies, waits for them, and re-layouts  1.86 us (2%)
    all_to_all x1, blocking collectives, exchange(): got = lax.all_to_all(sent, SEQ, split_axis=0, concat_axis=0, tiled=True)  21.6 us
    all_to_all x1, blocking collectives, local(): lax.all_to_all(copies, 'chan', split_axis=0, concat_axis=0, tiled=True)  20.9 us
    all_to_all x1, starting transfers between devices, exchange(): got = lax.all_to_all(sent, SEQ, split_axis=0, concat_axis=0, tiled=True)  18.4 us
    all_to_all x1, waiting for transfers between devices, exchange(): got = lax.all_to_all(sent, SEQ, split_axis=0, concat_axis=0, tiled=True)  15.3 us
    pallas_call x5, Pallas kernels, call(): pl.pallas_call(kernel, out_shape=out, in_specs=in_specs, out_specs=full(o...  8.24 us
    ppermute x1, starting transfers between devices, local(): lax.ppermute(twins, 'core', swap)  6.47 us
    pallas_call x1, Pallas kernels, product(): pl.pallas_call(product_kernel, out_shape=[jax.ShapeDtypeStruct((wide, cou...  4.76 us
    all_gather x1, waiting for transfers between devices, gather_columns(): return lax.all_gather(shard, ('z', 'y'), axis=0, tiled=True)  4.58 us
  transfers between devices with their start and end apart: 4, of which 4 were waited for; matrix products, arithmetic and copies ran while one was open for 1% of the time, Pallas kernels for 6%

profile of v7, /device:TPU:1, one launch (start us, length us, event | category | flops | bytes accessed | tf_op | source)
XLA Modules:
  0.0 124.1 jit_solution(9552312696653255189)
XLA Ops:
  6.5 0.0 copy-start
  6.5 0.0 all-gather.2.cloned.1.call-start
  6.5 0.7 all-gather.2.cloned.1.call-update
  7.3 0.0 copy-start.1
  7.3 1.0 copy-done.1
  8.2 0.0 copy-start.3
  8.2 1.1 shard_map.64
  9.4 18.4 %all-to-all-start = ((bf16[128,5,2,128]{3,2,1,0:T(2,128)(2,1)}), bf16[128,5,2,128]{3,2,1,0:T(2,128)(2,1)S(1)}, u32[]{:S(2)}, u32[]{:S(2)}) async-start(bf16[128,5,2,128]{3,2,1,0:T(2,128)(2,1)} %bitcast.2), calls=%async_computation | async-start | bytes 655360 | tf_op jit(solution)/shard_map/all_to_all | solution.py:210
  27.8 0.0 copy-done.3
  27.8 0.1 copy.8
  27.9 0.2 reduce-window.9
  28.1 0.1 reduce
  28.2 0.8 dynamic_slice.3.skip_ref
  29.0 0.0 copy-done
  29.0 0.4 shard_map.65.toep_ref
  29.4 0.0 copy-start.2
  29.4 15.3 %all-to-all-done = bf16[128,5,2,128]{3,2,1,0:T(2,128)(2,1)S(1)} async-done(((bf16[128,5,2,128]{3,2,1,0:T(2,128)(2,1)}), bf16[128,5,2,128]{3,2,1,0:T(2,128)(2,1)S(1)}, u32[]{:S(2)}, u32[]{:S(2)}) %all-to-all-start) | async-done | bytes 327712 | tf_op jit(solution)/shard_map/all_to_all | solution.py:210
  44.7 5.4 %shard_map.66 = bf16[1280,128]{1,0:T(8,128)(2,1)S(1)} custom-call(s32[128]{0:T(128)S(1)} %sub.3.start_ref, s32[128]{0:T(128)S(1)} %copy-done.3, f32[8]{0:T(128)S(1)} %dynamic_slice.3.skip_ref, bf16[1280,128]{1,0:T(8,128)(2,1)S(1)} %bitcast.11, bf16[8,256,256]{2,1,0:T(8,128)(2,1)S(1)} %shard_map.65.toep_ref), custom_call_target="tpu_custom_call" | custom-call | flops 134217728 | bytes 1704992 | tf_op jit(solution)/shard_map/pallas_call | solution.py:34
  50.1 21.6 %all_to_all.15 = bf16[128,5,2,128]{3,2,1,0:T(2,128)(2,1)S(1)} all-to-all(bf16[128,5,2,128]{3,2,1,0:T(2,128)(2,1)S(1)} %bitcast.12), channel_id=1, replica_groups=mesh['z'=8,'y'=8,'core'=2,'chan'=4] {'z','y','core'}, dimensions={0} | all-to-all | bytes 655360 | tf_op jit(solution)/shard_map/all_to_all | solution.py:210
  71.7 0.0 copy-done.2
  71.7 0.4 shard_map.67
  72.1 20.9 %all_to_all.16.rows_ref = bf16[4,160,1024]{2,1,0:T(8,128)(2,1)S(1)} all-to-all(bf16[4,160,1024]{2,1,0:T(8,128)(2,1)S(1)} %shard_map.67), channel_id=1, replica_groups=mesh['z'=8,'y'=8,'core'=2,'chan'=4] {'chan'}, dimensions={0} | all-to-all | bytes 2621440 | tf_op jit(solution)/shard_map/all_to_all | solution.py:255
  93.0 3.7 %collective-permute-start = (bf16[4,160,1024]{2,1,0:T(8,128)(2,1)S(1)}, bf16[4,160,1024]{2,1,0:T(8,128)(2,1)S(1)}, u32[]{:S(2)}, u32[]{:S(2)}) collective-permute-start(bf16[4,160,1024]{2,1,0:T(8,128)(2,1)S(1)} %all_to_all.16.rows_ref), channel_id=1, source_target_pairs={{0,4},{4,0},{1,5},{5,1},{2,6},{6,2},{3,7},{7,3},{8,12},{12,8},{9,1... | collective-permute-start | bytes 3932168 | tf_op jit(solution)/shard_map/ppermute | solution.py:257
  96.7 2.6 %collective-permute-done.twin_ref = bf16[4,160,1024]{2,1,0:T(8,128)(2,1)S(1)} collective-permute-done((bf16[4,160,1024]{2,1,0:T(8,128)(2,1)S(1)}, bf16[4,160,1024]{2,1,0:T(8,128)(2,1)S(1)}, u32[]{:S(2)}, u32[]{:S(2)}) %collective-permute-start) | collective-permute-done | bytes 1310752 | tf_op jit(solution)/shard_map/ppermute | solution.py:257
  99.3 4.6 %all-gather.2.cloned.1.call-done.w_ref = bf16[512,4096]{1,0:T(8,128)(2,1)} async-done(((bf16[8,4096]{1,0:T(8,128)(2,1)}), bf16[512,4096]{1,0:T(8,128)(2,1)}) %all-gather.2.cloned.1.call-update) | async-done | bytes 4194320 | tf_op jit(solution)/shard_map/all_gather | solution.py:270
  103.9 4.8 %shard_map.68 = (f32[512,160]{1,0:T(8,128)S(1)}, bf16[512,160]{1,0:T(8,128)(2,1)S(1)}) custom-call(bf16[4,160,1024]{2,1,0:T(8,128)(2,1)S(1)} %all_to_all.16.rows_ref, bf16[4,160,1024]{2,1,0:T(8,128)(2,1)S(1)} %collective-permute-done.twin_ref, bf16[512,4096]{1,0:T(8,128)(2,1)} %all-gather.2.cloned.1.call-done.w_ref), custom_call_target="tpu_custom_call" | custom-call | flops 1342177280 | bytes 7307264 | tf_op jit(solution)/shard_map/pallas_call | solution.py:177
  108.7 6.5 %collective-permute-start.1 = (bf16[512,160]{1,0:T(8,128)(2,1)S(1)}, bf16[512,160]{1,0:T(8,128)(2,1)S(1)}, u32[]{:S(2)}, u32[]{:S(2)}) collective-permute-start(bf16[512,160]{1,0:T(8,128)(2,1)S(1)} %get-tuple-element.24), channel_id=1, source_target_pairs={{0,4},{4,0},{1,5},{5,1},{2,6},{6,2},{3,7},{7,3},{8,12},{12,8},{9,1... | collective-permute-start | bytes 491528 | tf_op jit(solution)/shard_map/ppermute | solution.py:262
  115.2 1.1 collective-permute-done.1.other_ref
  116.3 0.9 shard_map.69
  (1 shorter events, 0.0 us)
Async XLA Ops:
  6.5 22.5 %copy-start = (bf16[256,1024]{1,0:T(8,128)(2,1)S(1)}, bf16[256,1024]{1,0:T(8,128)(2,1)}, u32[]{:S(2)}) copy-start(bf16[256,1024]{1,0:T(8,128)(2,1)} %f_ref) | copy-start | bytes 1572868
  6.5 97.4 %all-gather.2.cloned.1.call-start = ((), (), s32[]{:S(2)}) async-start(), calls=%async_computation.3 | async-start | bytes 4259840 | tf_op jit(solution)/shard_map/all_gather | solution.py:270
  7.3 1.0 copy-start.1
  8.2 19.6 %copy-start.3 = (s32[128]{0:T(128)S(1)}, s32[128]{0:T(128)}, u32[]{:S(2)}) copy-start(s32[128]{0:T(128)} %length_ref) | copy-start | bytes 1540
  9.4 35.3 %all-to-all-start = ((bf16[128,5,2,128]{3,2,1,0:T(2,128)(2,1)}), bf16[128,5,2,128]{3,2,1,0:T(2,128)(2,1)S(1)}, u32[]{:S(2)}, u32[]{:S(2)}) async-start(bf16[128,5,2,128]{3,2,1,0:T(2,128)(2,1)} %bitcast.2), calls=%async_computation | async-start | bytes 655360 | tf_op jit(solution)/shard_map/all_to_all | solution.py:210
  29.4 42.4 %copy-start.2 = (bf16[160,1,1024]{2,0,1:T(8,128)(2,1)S(1)}, bf16[160,1,1024]{2,0,1:T(8,128)(2,1)}, u32[]{:S(2)}) copy-start(bf16[160,1,1024]{2,0,1:T(8,128)(2,1)} %param.7) | copy-start | bytes 983044
  93.0 6.3 %collective-permute-start = (bf16[4,160,1024]{2,1,0:T(8,128)(2,1)S(1)}, bf16[4,160,1024]{2,1,0:T(8,128)(2,1)S(1)}, u32[]{:S(2)}, u32[]{:S(2)}) collective-permute-start(bf16[4,160,1024]{2,1,0:T(8,128)(2,1)S(1)} %all_to_all.16.rows_ref), channel_id=1, source_target_pairs={{0,4},{4,0},{1,5},{5,1},{2,6},{6,2},{3,7},{7,3},{8,12},{12,8},{9,1... | collective-permute-start | bytes 3932168 | tf_op jit(solution)/shard_map/ppermute | solution.py:257
  108.7 7.6 %collective-permute-start.1 = (bf16[512,160]{1,0:T(8,128)(2,1)S(1)}, bf16[512,160]{1,0:T(8,128)(2,1)S(1)}, u32[]{:S(2)}, u32[]{:S(2)}) collective-permute-start(bf16[512,160]{1,0:T(8,128)(2,1)S(1)} %get-tuple-element.24), channel_id=1, source_target_pairs={{0,4},{4,0},{1,5},{5,1},{2,6},{6,2},{3,7},{7,3},{8,12},{12,8},{9,1... | collective-permute-start | bytes 491528 | tf_op jit(solution)/shard_map/ppermute | solution.py:262
Sparse Core Ops, SparseCore 0:
  10.4 93.4 all-gather.1

commit v8 on v2

--- a/solution.py
+++ b/solution.py
@@ -233,9 +233,8 @@
     )
     block, four, two, back_two, _ = lax.optimization_barrier((line, *fars, convolved))
     near = jnp.concatenate([block, four, two, back_two], axis=0)
-    back, *sides = lax.optimization_barrier((exchange(convolved), *handed(block, two, back_two, "z")))
-    own = near, jnp.concatenate(sides, axis=0)
-    other = tuple(lax.ppermute(part, "seq", [(i, i ^ 1) for i in range(PEERS)]) for part in own)
+    back = exchange(convolved)
+    sides = handed(block, two, back_two, "z")
     groups = lax.axis_size("chan")
     copies = call(
         gate_kernel,
@@ -244,6 +243,9 @@
         [buf, low],
     )
     rows = lax.all_to_all(copies, "chan", split_axis=0, concat_axis=0, tiled=True)
+    rows, *sides = lax.optimization_barrier((rows, *sides))
+    own = near, jnp.concatenate(sides, axis=0)
+    other = tuple(lax.ppermute(part, "seq", [(i, i ^ 1) for i in range(PEERS)]) for part in own)
     wide = own[0].shape[0] + own[1].shape[0]
     half = jax.ShapeDtypeStruct((wide, ROWS), F32)
     flops = 2 * ROWS * wide * own[0].shape[1]

time: 145 us -> 132 us (0.910)
  blocking collectives: 21.6 us -> 0 us
  waiting for transfers between devices: 14.6 us -> 24.3 us
  starting transfers between devices: 82.6 us -> 78.6 us
    all_to_all x1 -> x0, blocking collectives: 21.6 us -> none  [local(): lax.all_to_all(copies, 'chan', split_axis=0, concat_axis=0, tiled=True)]
    all_to_all x0 -> x1, waiting for transfers between devices: none -> 13.6 us  [local(): lax.all_to_all(copies, 'chan', split_axis=0, concat_axis=0, tiled=True)]
    ppermute x2, starting transfers between devices: 17.4 us -> 4.89 us  [local(): lax.ppermute(part, 'seq', [(i, i ^ 1) for i in range(PEERS)])]
    ppermute x10, waiting for transfers between devices: 14.6 us -> 2.51 us  [move(): return lax.ppermute(array, 'seq', pairs)]
    all_to_all x2, waiting for transfers between devices: 0.01 us -> 5.7 us  [exchange(): got = lax.all_to_all(sent, SEQ, split_axis=0, concat_axis=0, tiled=True)]
    ppermute x10, starting transfers between devices: 43 us -> 48.5 us  [move(): return lax.ppermute(array, 'seq', pairs)]
    all_to_all x0 -> x1, starting transfers between devices: none -> 4.02 us  [local(): lax.all_to_all(copies, 'chan', split_axis=0, concat_axis=0, tiled=True)]
    ppermute x2, waiting for transfers between devices: 0.01 us -> 2.5 us  [local(): lax.ppermute(part, 'seq', [(i, i ^ 1) for i in range(PEERS)])]
  transfers between devices with their start and end apart: 14 -> 15, of which waited for: 5 -> 5; matrix products, arithmetic and copies ran while one was open for 7% -> 9% of each run, Pallas kernels for 6% -> 7%
where the time goes in v8:
time: 132 us; the launch traced here: 131 us
  starting transfers between devices  78.6 us (60%)
  waiting for transfers between devices  24.3 us (18%)
  Pallas kernels  14.2 us (11%)
  local copies, waits for them, and re-layouts  9.35 us (7%)
  other arithmetic  3.86 us (3%)
    ppermute x10, starting transfers between devices, move(): return lax.ppermute(array, 'seq', pairs)  48.5 us
    all_to_all x2, starting transfers between devices, exchange(): got = lax.all_to_all(sent, SEQ, split_axis=0, concat_axis=0, tiled=True)  21.2 us
    pallas_call x6, Pallas kernels, call(): pl.pallas_call(kernel, out_shape=out, in_specs=in_specs, out_specs=full(o...  14.2 us
    all_to_all x1, waiting for transfers between devices, local(): lax.all_to_all(copies, 'chan', split_axis=0, concat_axis=0, tiled=True)  13.6 us
    unnamed x23, local copies, waits for them, and re-layouts  6.47 us
    all_to_all x2, waiting for transfers between devices, exchange(): got = lax.all_to_all(sent, SEQ, split_axis=0, concat_axis=0, tiled=True)  5.7 us
    ppermute x2, starting transfers between devices, local(): lax.ppermute(part, 'seq', [(i, i ^ 1) for i in range(PEERS)])  4.89 us
    all_to_all x1, starting transfers between devices, local(): lax.all_to_all(copies, 'chan', split_axis=0, concat_axis=0, tiled=True)  4.02 us
  transfers between devices with their start and end apart: 15, of which 5 were waited for; matrix products, arithmetic and copies ran while one was open for 9% of the time, Pallas kernels for 7%

profile of v8, /device:TPU:1, one launch (start us, length us, event | category | flops | bytes accessed | tf_op | source)
XLA Modules:
  0.0 130.7 jit_solution(7405254676173730504)
XLA Ops:
  0.0 0.0 copy-start.1
  0.0 1.0 copy-done.1
  1.0 0.0 copy-start.6
  1.0 1.1 shard_map.64
  2.1 0.0 copy-start.3
  2.1 6.8 %collective-permute-start.2 = (bf16[8,4096]{1,0:T(8,128)(2,1)}, bf16[8,4096]{1,0:T(8,128)(2,1)S(1)}, u32[]{:S(2)}, u32[]{:S(2)}) collective-permute-start(bf16[8,4096]{1,0:T(8,128)(2,1)} %bitcast.15), channel_id=1, source_target_pairs={{48,0},{56,8},{0,16},{8,24},{16,32},{24,40},{32,48},{40,56},{112,6... | collective-permute-start | bytes 196616 | tf_op jit(solution)/shard_map/ppermute | solution.py:275
  8.9 6.8 %collective-permute-start.1 = (bf16[8,4096]{1,0:T(8,128)(2,1)}, bf16[8,4096]{1,0:T(8,128)(2,1)S(1)}, u32[]{:S(2)}, u32[]{:S(2)}) collective-permute-start(bf16[8,4096]{1,0:T(8,128)(2,1)} %bitcast.16), channel_id=1, source_target_pairs={{16,0},{24,8},{32,16},{40,24},{48,32},{56,40},{0,48},{8,56},{80,64... | collective-permute-start | bytes 196616 | tf_op jit(solution)/shard_map/ppermute | solution.py:275
  15.7 5.5 %collective-permute-start = (bf16[8,4096]{1,0:T(8,128)(2,1)}, bf16[8,4096]{1,0:T(8,128)(2,1)S(1)}, u32[]{:S(2)}, u32[]{:S(2)}) collective-permute-start(bf16[8,4096]{1,0:T(8,128)(2,1)} %bitcast.17), channel_id=1, source_target_pairs={{32,0},{40,8},{48,16},{56,24},{0,32},{8,40},{16,48},{24,56},{96,64... | collective-permute-start | bytes 196616 | tf_op jit(solution)/shard_map/ppermute | solution.py:275
  21.1 10.1 %all-to-all-start = ((bf16[128,5,2,128]{3,2,1,0:T(2,128)(2,1)}), bf16[128,5,2,128]{3,2,1,0:T(2,128)(2,1)S(1)}, u32[]{:S(2)}, u32[]{:S(2)}) async-start(bf16[128,5,2,128]{3,2,1,0:T(2,128)(2,1)} %bitcast.4), calls=%async_computation | async-start | bytes 655360 | tf_op jit(solution)/shard_map/all_to_all | solution.py:193
  31.3 0.8 constant_dynamic-update-slice_fusion.5
  32.1 0.8 copy.8
  32.9 0.2 reduce-window.9
  33.0 0.1 reduce
  33.1 0.7 sub.3.start_ref
  33.8 0.8 dynamic_slice.3.skip_ref
  34.6 0.0 copy-start
  34.6 1.0 copy-done
  35.6 0.4 shard_map.65.toep_ref
  36.0 0.0 collective-permute-done.2
  36.0 0.0 collective-permute-done.1
  36.0 0.0 copy-done.6
  36.0 3.3 %collective-permute-start.4 = (bf16[16,4096]{1,0:T(8,128)(2,1)S(1)}, bf16[16,4096]{1,0:T(8,128)(2,1)S(1)}, u32[]{:S(2)}, u32[]{:S(2)}) collective-permute-start(bf16[16,4096]{1,0:T(8,128)(2,1)S(1)} %get-tuple-element.39), channel_id=1, source_target_pairs={{56,0},{0,8},{8,16},{16,24},{24,32},{32,40},{40,48},{48,56},{120,6... | collective-permute-start | bytes 393224 | tf_op jit(solution)/shard_map/ppermute | solution.py:275
  39.3 3.8 %collective-permute-start.3 = (bf16[16,4096]{1,0:T(8,128)(2,1)S(1)}, bf16[16,4096]{1,0:T(8,128)(2,1)S(1)}, u32[]{:S(2)}, u32[]{:S(2)}) collective-permute-start(bf16[16,4096]{1,0:T(8,128)(2,1)S(1)} %get-tuple-element.40), channel_id=1, source_target_pairs={{8,0},{16,8},{24,16},{32,24},{40,32},{48,40},{56,48},{0,56},{72,64... | collective-permute-start | bytes 393224 | tf_op jit(solution)/shard_map/ppermute | solution.py:275
  43.1 0.0 collective-permute-done
  43.2 2.3 %collective-permute-done.3 = bf16[16,4096]{1,0:T(8,128)(2,1)S(1)} collective-permute-done((bf16[16,4096]{1,0:T(8,128)(2,1)S(1)}, bf16[16,4096]{1,0:T(8,128)(2,1)S(1)}, u32[]{:S(2)}, u32[]{:S(2)}) %collective-permute-start.3) | collective-permute-done | bytes 131104 | tf_op jit(solution)/shard_map/ppermute | solution.py:275
  45.5 0.1 collective-permute-done.4
  45.7 3.8 %collective-permute-start.7 = (bf16[64,4096]{1,0:T(8,128)(2,1)S(1)}, bf16[64,4096]{1,0:T(8,128)(2,1)S(1)}, u32[]{:S(2)}, u32[]{:S(2)}) collective-permute-start(bf16[64,4096]{1,0:T(8,128)(2,1)S(1)} %constant_dynamic-update-slice_fusion), channel_id=1, source_target_pairs={{52,4},{60,12},{4,20},{12,28},{20,36},{28,44},{36,52},{44,60},{116... | collective-permute-start | bytes 1572872 | tf_op jit(solution)/shard_map/ppermute | solution.py:275
  49.5 3.6 %collective-permute-start.6 = (bf16[64,4096]{1,0:T(8,128)(2,1)S(1)}, bf16[64,4096]{1,0:T(8,128)(2,1)}, u32[]{:S(2)}, u32[]{:S(2)}) collective-permute-start(bf16[64,4096]{1,0:T(8,128)(2,1)S(1)} %constant_dynamic-update-slice_fusion), channel_id=1, source_target_pairs={{20,4},{28,12},{36,20},{44,28},{52,36},{60,44},{4,52},{12,60},{84,... | collective-permute-start | bytes 1572872 | tf_op jit(solution)/shard_map/ppermute | solution.py:275
  53.1 6.7 %collective-permute-start.5 = (bf16[64,4096]{1,0:T(8,128)(2,1)S(1)}, bf16[64,4096]{1,0:T(8,128)(2,1)}, u32[]{:S(2)}, u32[]{:S(2)}) collective-permute-start(bf16[64,4096]{1,0:T(8,128)(2,1)S(1)} %constant_dynamic-update-slice_fusion), channel_id=1, source_target_pairs={{36,4},{44,12},{52,20},{60,28},{4,36},{12,44},{20,52},{28,60},{100... | collective-permute-start | bytes 1572872 | tf_op jit(solution)/shard_map/ppermute | solution.py:275
  59.9 0.0 all-to-all-done
  59.9 0.0 copy-done.3
  59.9 6.1 %shard_map.66 = bf16[1280,128]{1,0:T(8,128)(2,1)} custom-call(s32[128]{0:T(128)S(1)} %sub.3.start_ref, s32[128]{0:T(128)S(1)} %copy-done.3, f32[8]{0:T(128)S(1)} %dynamic_slice.3.skip_ref, bf16[1280,128]{1,0:T(8,128)(2,1)S(1)} %bitcast.10, bf16[8,256,256]{2,1,0:T(8,128)(2,1)S(1)} %shard_map.65.toep_ref), custom_call_target="tpu_custom_call" | custom-call | flops 134217728 | bytes 1704992 | tf_op jit(solution)/shard_map/pallas_call | solution.py:37
  66.0 11.1 %all-to-all-start.1 = ((bf16[128,5,2,128]{3,2,1,0:T(2,128)(2,1)}), bf16[128,5,2,128]{3,2,1,0:T(2,128)(2,1)S(1)}, u32[]{:S(2)}, u32[]{:S(2)}) async-start(bf16[128,5,2,128]{3,2,1,0:T(2,128)(2,1)} %bitcast.6), calls=%async_computation.1 | async-start | bytes 655360 | tf_op jit(solution)/shard_map/all_to_all | solution.py:193
  77.1 0.0 copy-start.2
  77.1 0.0 collective-permute-done.7
  77.1 0.0 copy-start.4
  77.1 0.0 collective-permute-done.6
  77.1 0.0 collective-permute-done.5
  77.1 2.9 %pad_maximum_fusion = (bf16[128,4096]{1,0:T(8,128)(2,1)}, bf16[128,4096]{1,0:T(8,128)(2,1)}) fusion(bf16[64,4096]{1,0:T(8,128)(2,1)S(1)} %constant_dynamic-update-slice_fusion, bf16[64,4096]{1,0:T(8,128)(2,1)S(1)} %collective-permute-done.7, bf16[64,4096]{1,0:T(8,128)(2,1)} %collective-permute-done.6), kind=kLoop, calls=%fused_computation | loop fusion | flops 3670016 | bytes 3670016 | tf_op jit(solution)/shard_map/concatenate | solution.py:284
  80.0 6.4 %collective-permute-start.9 = (bf16[128,4096]{1,0:T(8,128)(2,1)}, bf16[128,4096]{1,0:T(8,128)(2,1)}, u32[]{:S(2)}, u32[]{:S(2)}) collective-permute-start(bf16[128,4096]{1,0:T(8,128)(2,1)} %get-tuple-element.37), channel_id=1, source_target_pairs={{60,4},{4,12},{12,20},{20,28},{28,36},{36,44},{44,52},{52,60},{124... | collective-permute-start | bytes 3145736 | tf_op jit(solution)/shard_map/ppermute | solution.py:275
  86.4 0.0 copy-done.4
  86.5 1.9 %collective-permute-start.8 = (bf16[128,4096]{1,0:T(8,128)(2,1)}, bf16[128,4096]{1,0:T(8,128)(2,1)}, u32[]{:S(2)}, u32[]{:S(2)}) collective-permute-start(bf16[128,4096]{1,0:T(8,128)(2,1)} %get-tuple-element.38), channel_id=1, source_target_pairs={{12,4},{20,12},{28,20},{36,28},{44,36},{52,44},{60,52},{4,60},{76,... | collective-permute-start | bytes 3145736 | tf_op jit(solution)/shard_map/ppermute | solution.py:275
  88.4 5.7 %all-to-all-done.1 = bf16[128,5,2,128]{3,2,1,0:T(2,128)(2,1)S(1)} async-done(((bf16[128,5,2,128]{3,2,1,0:T(2,128)(2,1)}), bf16[128,5,2,128]{3,2,1,0:T(2,128)(2,1)S(1)}, u32[]{:S(2)}, u32[]{:S(2)}) %all-to-all-start.1) | async-done | bytes 327712 | tf_op jit(solution)/shard_map/all_to_all | solution.py:193
  94.1 0.0 copy-done.2
  94.1 1.5 %shard_map.67 = bf16[4,160,1024]{2,1,0:T(8,128)(2,1)} custom-call(bf16[1280,128]{1,0:T(8,128)(2,1)S(1)} %bitcast.11, bf16[160,1024]{1,0:T(8,128)(2,1)S(1)} %bitcast.13), custom_call_target="tpu_custom_call" | custom-call | bytes 1966080 | tf_op jit(solution)/shard_map/pallas_call | solution.py:37
  95.6 4.0 %all-to-all-start.2 = ((bf16[4,160,1024]{2,1,0:T(8,128)(2,1)}), bf16[4,160,1024]{2,1,0:T(8,128)(2,1)S(1)}, u32[]{:S(2)}, u32[]{:S(2)}) async-start(bf16[4,160,1024]{2,1,0:T(8,128)(2,1)} %shard_map.67), calls=%async_computation.2 | async-start | bytes 2621440 | tf_op jit(solution)/shard_map/all_to_all | solution.py:245
  99.6 0.0 copy-start.5
  99.6 1.1 constant_dynamic-update-slice_fusion.8
  100.8 1.1 constant_dynamic-update-slice_fusion.7
  101.9 0.0 copy-done.5
  101.9 2.0 %collective-permute-start.10 = (bf16[256,4096]{1,0:T(8,128)(2,1)S(1)}, bf16[256,4096]{1,0:T(8,128)(2,1)}, u32[]{:S(2)}, u32[]{:S(2)}) collective-permute-start(bf16[256,4096]{1,0:T(8,128)(2,1)S(1)} %constant_dynamic-update-slice_fusion.6.near_ref), channel_id=1, source_target_pairs={{0,4},{4,0},{8,12},{12,8},{16,20},{20,16},{24,28},{28,24},{32,36},... | collective-permute-start | bytes 6291464 | tf_op jit(solution)/shard_map/ppermute | solution.py:248
  104.0 0.0 collective-permute-done.9
  104.0 0.0 collective-permute-done.8
  104.0 13.6 %all-to-all-done.2.rows_ref = bf16[4,160,1024]{2,1,0:T(8,128)(2,1)S(1)} async-done(((bf16[4,160,1024]{2,1,0:T(8,128)(2,1)}), bf16[4,160,1024]{2,1,0:T(8,128)(2,1)S(1)}, u32[]{:S(2)}, u32[]{:S(2)}) %all-to-all-start.2) | async-done | bytes 1310752 | tf_op jit(solution)/shard_map/all_to_all | solution.py:245
  117.6 1.3 %constant_dynamic-update-slice_fusion.11 = bf16[256,4096]{1,0:T(8,128)(2,1)S(1)} fusion(bf16[128,4096]{1,0:T(8,128)(2,1)} %collective-permute-done.8), kind=kLoop, calls=%fused_computation.15 | loop fusion | bytes 2097152
  118.9 1.3 %constant_dynamic-update-slice_fusion.10.far_ref = bf16[256,4096]{1,0:T(8,128)(2,1)S(1)} fusion(bf16[256,4096]{1,0:T(8,128)(2,1)S(1)} %constant_dynamic-update-slice_fusion.11, bf16[128,4096]{1,0:T(8,128)(2,1)} %collective-permute-done.9), kind=kLoop, calls=%fused_computation.14 | loop fusion | bytes 2097152 | tf_op jit(solution)/shard_map/concatenate | solution.py:247
  120.2 2.9 %collective-permute-start.11 = (bf16[256,4096]{1,0:T(8,128)(2,1)S(1)}, bf16[256,4096]{1,0:T(8,128)(2,1)S(1)}, u32[]{:S(2)}, u32[]{:S(2)}) collective-permute-start(bf16[256,4096]{1,0:T(8,128)(2,1)S(1)} %constant_dynamic-update-slice_fusion.10.far_ref), channel_id=1, source_target_pairs={{0,4},{4,0},{8,12},{12,8},{16,20},{20,16},{24,28},{28,24},{32,36},... | collective-permute-start | bytes 6291464 | tf_op jit(solution)/shard_map/ppermute | solution.py:248
  123.1 1.2 shard_map.68.own_ref
  124.3 0.0 collective-permute-done.10.near_ref
  124.3 2.5 %collective-permute-done.11.far_ref = bf16[256,4096]{1,0:T(8,128)(2,1)S(1)} collective-permute-done((bf16[256,4096]{1,0:T(8,128)(2,1)S(1)}, bf16[256,4096]{1,0:T(8,128)(2,1)S(1)}, u32[]{:S(2)}, u32[]{:S(2)}) %collective-permute-start.11) | collective-permute-done | bytes 2097184 | tf_op jit(solution)/shard_map/ppermute | solution.py:248
  126.8 3.8 %shard_map.69 = bf16[160,1024]{1,0:T(8,128)(2,1)} custom-call(s32[1]{0:T(128)} %bitcast.index_ref, bf16[4,160,1024]{2,1,0:T(8,128)(2,1)S(1)} %all-to-all-done.2.rows_ref, bf16[256,4096]{1,0:T(8,128)(2,1)} %collective-permute-done.10.near_ref, bf16[256,4096]{1,0:T(8,128)(2,1)S(1)} %collective-permute-done.11.far_ref, f32[512,160]{1,0:T(8,128)S(1)} %shard_map.68.own_ref), custom_call_target="tpu_custom_call" | custom-call | flops 671088640 | bytes 6160388 | tf_op jit(solution)/shard_map/pallas_call | solution.py:37
  (8 shorter events, 0.1 us)
Async XLA Ops:
  0.0 1.0 copy-start.1
  1.0 35.0 %copy-start.6 = (bf16[4096,8]{0,1:T(8,128)(2,1)S(1)}, bf16[4096,8]{0,1:T(8,128)(2,1)}, u32[]{:S(2)}) copy-start(bf16[4096,8]{0,1:T(8,128)(2,1)} %param.10) | copy-start | bytes 196612
  2.1 57.8 %copy-start.3 = (s32[128]{0:T(128)S(1)}, s32[128]{0:T(128)}, u32[]{:S(2)}) copy-start(s32[128]{0:T(128)} %length_ref) | copy-start | bytes 1540
  2.1 33.9 %collective-permute-start.2 = (bf16[8,4096]{1,0:T(8,128)(2,1)}, bf16[8,4096]{1,0:T(8,128)(2,1)S(1)}, u32[]{:S(2)}, u32[]{:S(2)}) collective-permute-start(bf16[8,4096]{1,0:T(8,128)(2,1)} %bitcast.15), channel_id=1, source_target_pairs={{48,0},{56,8},{0,16},{8,24},{16,32},{24,40},{32,48},{40,56},{112,6... | collective-permute-start | bytes 196616 | tf_op jit(solution)/shard_map/ppermute | solution.py:275
  8.9 27.1 %collective-permute-start.1 = (bf16[8,4096]{1,0:T(8,128)(2,1)}, bf16[8,4096]{1,0:T(8,128)(2,1)S(1)}, u32[]{:S(2)}, u32[]{:S(2)}) collective-permute-start(bf16[8,4096]{1,0:T(8,128)(2,1)} %bitcast.16), channel_id=1, source_target_pairs={{16,0},{24,8},{32,16},{40,24},{48,32},{56,40},{0,48},{8,56},{80,64... | collective-permute-start | bytes 196616 | tf_op jit(solution)/shard_map/ppermute | solution.py:275
  15.7 27.5 %collective-permute-start = (bf16[8,4096]{1,0:T(8,128)(2,1)}, bf16[8,4096]{1,0:T(8,128)(2,1)S(1)}, u32[]{:S(2)}, u32[]{:S(2)}) collective-permute-start(bf16[8,4096]{1,0:T(8,128)(2,1)} %bitcast.17), channel_id=1, source_target_pairs={{32,0},{40,8},{48,16},{56,24},{0,32},{8,40},{16,48},{24,56},{96,64... | collective-permute-start | bytes 196616 | tf_op jit(solution)/shard_map/ppermute | solution.py:275
  21.1 38.7 %all-to-all-start = ((bf16[128,5,2,128]{3,2,1,0:T(2,128)(2,1)}), bf16[128,5,2,128]{3,2,1,0:T(2,128)(2,1)S(1)}, u32[]{:S(2)}, u32[]{:S(2)}) async-start(bf16[128,5,2,128]{3,2,1,0:T(2,128)(2,1)} %bitcast.4), calls=%async_computation | async-start | bytes 655360 | tf_op jit(solution)/shard_map/all_to_all | solution.py:193
  34.6 1.0 copy-start
  36.0 9.6 %collective-permute-start.4 = (bf16[16,4096]{1,0:T(8,128)(2,1)S(1)}, bf16[16,4096]{1,0:T(8,128)(2,1)S(1)}, u32[]{:S(2)}, u32[]{:S(2)}) collective-permute-start(bf16[16,4096]{1,0:T(8,128)(2,1)S(1)} %get-tuple-element.39), channel_id=1, source_target_pairs={{56,0},{0,8},{8,16},{16,24},{24,32},{32,40},{40,48},{48,56},{120,6... | collective-permute-start | bytes 393224 | tf_op jit(solution)/shard_map/ppermute | solution.py:275
  39.3 6.2 %collective-permute-start.3 = (bf16[16,4096]{1,0:T(8,128)(2,1)S(1)}, bf16[16,4096]{1,0:T(8,128)(2,1)S(1)}, u32[]{:S(2)}, u32[]{:S(2)}) collective-permute-start(bf16[16,4096]{1,0:T(8,128)(2,1)S(1)} %get-tuple-element.40), channel_id=1, source_target_pairs={{8,0},{16,8},{24,16},{32,24},{40,32},{48,40},{56,48},{0,56},{72,64... | collective-permute-start | bytes 393224 | tf_op jit(solution)/shard_map/ppermute | solution.py:275
  45.7 31.4 %collective-permute-start.7 = (bf16[64,4096]{1,0:T(8,128)(2,1)S(1)}, bf16[64,4096]{1,0:T(8,128)(2,1)S(1)}, u32[]{:S(2)}, u32[]{:S(2)}) collective-permute-start(bf16[64,4096]{1,0:T(8,128)(2,1)S(1)} %constant_dynamic-update-slice_fusion), channel_id=1, source_target_pairs={{52,4},{60,12},{4,20},{12,28},{20,36},{28,44},{36,52},{44,60},{116... | collective-permute-start | bytes 1572872 | tf_op jit(solution)/shard_map/ppermute | solution.py:275
  49.5 27.7 %collective-permute-start.6 = (bf16[64,4096]{1,0:T(8,128)(2,1)S(1)}, bf16[64,4096]{1,0:T(8,128)(2,1)}, u32[]{:S(2)}, u32[]{:S(2)}) collective-permute-start(bf16[64,4096]{1,0:T(8,128)(2,1)S(1)} %constant_dynamic-update-slice_fusion), channel_id=1, source_target_pairs={{20,4},{28,12},{36,20},{44,28},{52,36},{60,44},{4,52},{12,60},{84,... | collective-permute-start | bytes 1572872 | tf_op jit(solution)/shard_map/ppermute | solution.py:275
  53.1 24.0 %collective-permute-start.5 = (bf16[64,4096]{1,0:T(8,128)(2,1)S(1)}, bf16[64,4096]{1,0:T(8,128)(2,1)}, u32[]{:S(2)}, u32[]{:S(2)}) collective-permute-start(bf16[64,4096]{1,0:T(8,128)(2,1)S(1)} %constant_dynamic-update-slice_fusion), channel_id=1, source_target_pairs={{36,4},{44,12},{52,20},{60,28},{4,36},{12,44},{20,52},{28,60},{100... | collective-permute-start | bytes 1572872 | tf_op jit(solution)/shard_map/ppermute | solution.py:275
  66.0 28.1 %all-to-all-start.1 = ((bf16[128,5,2,128]{3,2,1,0:T(2,128)(2,1)}), bf16[128,5,2,128]{3,2,1,0:T(2,128)(2,1)S(1)}, u32[]{:S(2)}, u32[]{:S(2)}) async-start(bf16[128,5,2,128]{3,2,1,0:T(2,128)(2,1)} %bitcast.6), calls=%async_computation.1 | async-start | bytes 655360 | tf_op jit(solution)/shard_map/all_to_all | solution.py:193
  77.1 17.0 %copy-start.2 = (bf16[160,1,1024]{2,0,1:T(8,128)(2,1)S(1)}, bf16[160,1,1024]{2,0,1:T(8,128)(2,1)}, u32[]{:S(2)}) copy-start(bf16[160,1,1024]{2,0,1:T(8,128)(2,1)} %param.7) | copy-start | bytes 983044
  77.1 9.3 %copy-start.4 = (bf16[64,4096]{1,0:T(8,128)(2,1)}, bf16[64,4096]{1,0:T(8,128)(2,1)S(1)}, u32[]{:S(2)}) copy-start(bf16[64,4096]{1,0:T(8,128)(2,1)S(1)} %collective-permute-done.7) | copy-start | bytes 1572868
  80.0 23.9 %collective-permute-start.9 = (bf16[128,4096]{1,0:T(8,128)(2,1)}, bf16[128,4096]{1,0:T(8,128)(2,1)}, u32[]{:S(2)}, u32[]{:S(2)}) collective-permute-start(bf16[128,4096]{1,0:T(8,128)(2,1)} %get-tuple-element.37), channel_id=1, source_target_pairs={{60,4},{4,12},{12,20},{20,28},{28,36},{36,44},{44,52},{52,60},{124... | collective-permute-start | bytes 3145736 | tf_op jit(solution)/shard_map/ppermute | solution.py:275
  86.5 17.5 %collective-permute-start.8 = (bf16[128,4096]{1,0:T(8,128)(2,1)}, bf16[128,4096]{1,0:T(8,128)(2,1)}, u32[]{:S(2)}, u32[]{:S(2)}) collective-permute-start(bf16[128,4096]{1,0:T(8,128)(2,1)} %get-tuple-element.38), channel_id=1, source_target_pairs={{12,4},{20,12},{28,20},{36,28},{44,36},{52,44},{60,52},{4,60},{76,... | collective-permute-start | bytes 3145736 | tf_op jit(solution)/shard_map/ppermute | solution.py:275
  95.6 21.9 %all-to-all-start.2 = ((bf16[4,160,1024]{2,1,0:T(8,128)(2,1)}), bf16[4,160,1024]{2,1,0:T(8,128)(2,1)S(1)}, u32[]{:S(2)}, u32[]{:S(2)}) async-start(bf16[4,160,1024]{2,1,0:T(8,128)(2,1)} %shard_map.67), calls=%async_computation.2 | async-start | bytes 2621440 | tf_op jit(solution)/shard_map/all_to_all | solution.py:245
  99.6 2.2 %copy-start.5 = (bf16[64,4096]{1,0:T(8,128)(2,1)S(1)}, bf16[64,4096]{1,0:T(8,128)(2,1)}, u32[]{:S(2)}) copy-start(bf16[64,4096]{1,0:T(8,128)(2,1)} %copy-done.4) | copy-start | bytes 1572868
  101.9 22.4 %collective-permute-start.10 = (bf16[256,4096]{1,0:T(8,128)(2,1)S(1)}, bf16[256,4096]{1,0:T(8,128)(2,1)}, u32[]{:S(2)}, u32[]{:S(2)}) collective-permute-start(bf16[256,4096]{1,0:T(8,128)(2,1)S(1)} %constant_dynamic-update-slice_fusion.6.near_ref), channel_id=1, source_target_pairs={{0,4},{4,0},{8,12},{12,8},{16,20},{20,16},{24,28},{28,24},{32,36},... | collective-permute-start | bytes 6291464 | tf_op jit(solution)/shard_map/ppermute | solution.py:248
  120.2 6.6 %collective-permute-start.11 = (bf16[256,4096]{1,0:T(8,128)(2,1)S(1)}, bf16[256,4096]{1,0:T(8,128)(2,1)S(1)}, u32[]{:S(2)}, u32[]{:S(2)}) collective-permute-start(bf16[256,4096]{1,0:T(8,128)(2,1)S(1)} %constant_dynamic-update-slice_fusion.10.far_ref), channel_id=1, source_target_pairs={{0,4},{4,0},{8,12},{12,8},{16,20},{20,16},{24,28},{28,24},{32,36},... | collective-permute-start | bytes 6291464 | tf_op jit(solution)/shard_map/ppermute | solution.py:248

commit v9 on v6

--- a/solution.py
+++ b/solution.py
@@ -1,5 +1,3 @@
-import functools
-
 import jax
 import jax.numpy as jnp
 from jax import lax
@@ -20,7 +18,7 @@
 PEERS = 128
 MSG = PEERS * PER
 VMEM_LIMIT = 48 * 1024 * 1024
-SEQ = ("z", "y_half", "y_rest", "core")
+SEQ = ("z", "y", "core")
 
 
 def full(shape):
@@ -150,38 +148,46 @@
             out_ref[q, HEAD:, cols] = tail
 
 
-def product_kernel(rows_ref, *refs):
-    *w_refs, out_ref = refs
-    total = jnp.zeros((w_refs[0].shape[0], ROWS), F32)
-    for q, w_ref in enumerate(w_refs):
-        total += lax.dot_general(w_ref[...], rows_ref[q], (((1,), (1,)), ((), ())), preferred_element_type=F32)
-    for j in range(w_refs[0].shape[0] // LANES):
-        parts = []
-        for y in range(8):
-            for core in range(2):
-                group = 16 * j + 4 * (y % 4) + 2 * core + y // 4
-                parts.append(total[group * CH : (group + 1) * CH])
-        block = jnp.concatenate(parts, axis=0)
-        out_ref[:, j * LANES : (j + 1) * LANES] = block.T.astype(BF16)
+def product_kernel(rows_ref, w_ref, out_ref, total):
+    step = pl.program_id(0)
+    term = lax.dot_general(w_ref[...], rows_ref[0], (((1,), (1,)), ((), ())), preferred_element_type=F32)
+
+    @pl.when(step == 0)
+    def _():
+        total[...] = term
+
+    @pl.when(step > 0)
+    def _():
+        total[...] += term
+
+    @pl.when(step == pl.num_programs(0) - 1)
+    def _():
+        for j in range(total.shape[0] // LANES):
+            cols = slice(j * LANES, (j + 1) * LANES)
+            out_ref[:, cols] = total[cols, :].T.astype(BF16)
 
 
 def product(rows, table):
-    block = 256
-    groups, _, width = rows.shape
-    streams = [pl.BlockSpec((block, width), functools.partial(lambda q, j: (j, q), q)) for q in range(groups)]
+    block = 512
+    count, wide = rows.shape[1], table.shape[0]
+    parts = rows.shape[2] // block
     return pl.pallas_call(
         product_kernel,
-        out_shape=jax.ShapeDtypeStruct((ROWS, table.shape[0]), BF16),
-        grid=(table.shape[0] // block,),
-        in_specs=[pl.BlockSpec(rows.shape, lambda j: (0, 0, 0)), *streams],
-        out_specs=pl.BlockSpec((ROWS, block), lambda j: (0, j)),
+        out_shape=jax.ShapeDtypeStruct((count, wide), BF16),
+        grid=(table.shape[1] // block,),
+        in_specs=[
+            pl.BlockSpec((1, count, block), lambda k: (k // parts, 0, k % parts)),
+            pl.BlockSpec((wide, block), lambda k: (0, k)),
+        ],
+        out_specs=pl.BlockSpec((count, wide), lambda k: (0, 0)),
+        scratch_shapes=[pltpu.VMEM((wide, count), F32)],
         compiler_params=pltpu.CompilerParams(vmem_limit_bytes=VMEM_LIMIT),
         cost_estimate=pl.CostEstimate(
-            flops=2 * ROWS * table.size,
-            bytes_accessed=2 * (table.size + rows.size + ROWS * table.shape[0]),
+            flops=2 * count * table.size,
+            bytes_accessed=2 * (table.size + rows.size + count * wide),
             transcendentals=0,
         ),
-    )(rows, *[table] * groups)
+    )(rows, table)
 
 
 def exchange(message):
@@ -237,12 +243,11 @@
 
 
 def gather_columns(shard):
-    pair = lax.all_gather(shard, "y_half", axis=0, tiled=True)
-    return lax.all_gather(pair, ("z", "y_rest", "core"), axis=0, tiled=True)
+    return lax.all_gather(shard, SEQ, axis=0, tiled=True)
 
 
 def solution(mesh):
-    shape = dict(z=8, y_half=2, y_rest=4, core=2, chan=4)
+    shape = dict(z=8, y=8, core=2, chan=4)
     fine = Mesh(mesh.devices.reshape(tuple(shape.values())), tuple(shape))
     placed = (
         P(None, SEQ, "chan"),

time: 169 us -> 126 us (0.75)
  the two profiles are of different devices: /device:TPU:53 before, /device:TPU:1 now
where the time goes in v9:
time: 126 us
  blocking collectives  42.8 us (34%)
  waiting for transfers between devices  32.7 us (26%)
  starting transfers between devices  18.4 us (15%)
  Pallas kernels  16.2 us (13%)
  between operations  13.5 us (11%)
  local copies, waits for them, and re-layouts  1.86 us (1%)
    all_to_all x1, blocking collectives, exchange(): got = lax.all_to_all(sent, SEQ, split_axis=0, concat_axis=0, tiled=True)  21.6 us
    all_to_all x1, blocking collectives, local(): lax.all_to_all(copies, 'chan', split_axis=0, concat_axis=0, tiled=True)  21.2 us
    all_to_all x1, starting transfers between devices, exchange(): got = lax.all_to_all(sent, SEQ, split_axis=0, concat_axis=0, tiled=True)  18.4 us
    all_gather x1, waiting for transfers between devices, gather_columns(): return lax.all_gather(shard, SEQ, axis=0, tiled=True)  16.6 us
    all_to_all x1, waiting for transfers between devices, exchange(): got = lax.all_to_all(sent, SEQ, split_axis=0, concat_axis=0, tiled=True)  15.4 us
    pallas_call x1, Pallas kernels, product(): pl.pallas_call(product_kernel, out_shape=jax.ShapeDtypeStruct((count, wid...  8.92 us
    pallas_call x4, Pallas kernels, call(): pl.pallas_call(kernel, out_shape=out, in_specs=in_specs, out_specs=full(o...  7.3 us
  transfers between devices with their start and end apart: 2, of which 2 were waited for; matrix products, arithmetic and copies ran while one was open for 1% of the time, Pallas kernels for 6%

profile of v9, /device:TPU:1, one launch (start us, length us, event | category | flops | bytes accessed | tf_op | source)
XLA Modules:
  0.0 125.7 jit_solution(3941155704010093365)
XLA Ops:
  6.5 0.0 copy-start
  6.5 0.0 all-gather.2.cloned.1.call-start
  6.5 0.7 all-gather.2.cloned.1.call-update
  7.3 0.0 copy-start.1
  7.3 1.0 copy-done.1
  8.2 0.0 copy-start.3
  8.2 1.1 shard_map.64
  9.4 18.4 %all-to-all-start = ((bf16[128,5,2,128]{3,2,1,0:T(2,128)(2,1)}), bf16[128,5,2,128]{3,2,1,0:T(2,128)(2,1)S(1)}, u32[]{:S(2)}, u32[]{:S(2)}) async-start(bf16[128,5,2,128]{3,2,1,0:T(2,128)(2,1)} %bitcast.1), calls=%async_computation | async-start | bytes 655360 | tf_op jit(solution)/shard_map/all_to_all | solution.py:195
  27.8 0.0 copy-done.3
  27.8 0.1 copy.8
  27.9 0.2 reduce-window.9
  28.1 0.1 reduce
  28.2 0.8 dynamic_slice.3.skip_ref
  29.0 0.0 copy-done
  29.0 0.4 shard_map.65.toep_ref
  29.4 0.0 copy-start.2
  29.4 15.4 %all-to-all-done = bf16[128,5,2,128]{3,2,1,0:T(2,128)(2,1)S(1)} async-done(((bf16[128,5,2,128]{3,2,1,0:T(2,128)(2,1)}), bf16[128,5,2,128]{3,2,1,0:T(2,128)(2,1)S(1)}, u32[]{:S(2)}, u32[]{:S(2)}) %all-to-all-start) | async-done | bytes 327712 | tf_op jit(solution)/shard_map/all_to_all | solution.py:195
  44.7 5.4 %shard_map.66 = bf16[1280,128]{1,0:T(8,128)(2,1)S(1)} custom-call(s32[128]{0:T(128)S(1)} %sub.3.start_ref, s32[128]{0:T(128)S(1)} %copy-done.3, f32[8]{0:T(128)S(1)} %dynamic_slice.3.skip_ref, bf16[1280,128]{1,0:T(8,128)(2,1)S(1)} %bitcast.10, bf16[8,256,256]{2,1,0:T(8,128)(2,1)S(1)} %shard_map.65.toep_ref), custom_call_target="tpu_custom_call" | custom-call | flops 134217728 | bytes 1704992 | tf_op jit(solution)/shard_map/pallas_call | solution.py:34
  50.1 21.6 %all_to_all.15 = bf16[128,5,2,128]{3,2,1,0:T(2,128)(2,1)S(1)} all-to-all(bf16[128,5,2,128]{3,2,1,0:T(2,128)(2,1)S(1)} %bitcast.11), channel_id=1, replica_groups=mesh['z'=8,'y'=8,'core'=2,'chan'=4] {'z','y','core'}, dimensions={0} | all-to-all | bytes 655360 | tf_op jit(solution)/shard_map/all_to_all | solution.py:195
  71.7 0.0 copy-done.2
  71.7 0.4 shard_map.67
  72.1 21.2 %all_to_all.16.rows_ref = bf16[4,160,1024]{2,1,0:T(8,128)(2,1)S(1)} all-to-all(bf16[4,160,1024]{2,1,0:T(8,128)(2,1)S(1)} %shard_map.67), channel_id=1, replica_groups=mesh['z'=8,'y'=8,'core'=2,'chan'=4] {'chan'}, dimensions={0} | all-to-all | bytes 2621440 | tf_op jit(solution)/shard_map/all_to_all | solution.py:240
  93.4 16.6 %all-gather.2.cloned.1.call-done.w_ref = bf16[1024,4096]{1,0:T(8,128)(2,1)} async-done(((bf16[8,4096]{1,0:T(8,128)(2,1)}), bf16[1024,4096]{1,0:T(8,128)(2,1)}) %all-gather.2.cloned.1.call-update) | async-done | bytes 8388624 | tf_op jit(solution)/shard_map/all_gather | solution.py:246
  109.9 8.9 %shard_map.68 = bf16[160,1024]{1,0:T(8,128)(2,1)} custom-call(bf16[4,160,1024]{2,1,0:T(8,128)(2,1)S(1)} %all_to_all.16.rows_ref, bf16[1024,4096]{1,0:T(8,128)(2,1)} %all-gather.2.cloned.1.call-done.w_ref), custom_call_target="tpu_custom_call" | custom-call | flops 1342177280 | bytes 10027008 | tf_op jit(solution)/shard_map/pallas_call | solution.py:174
  (1 shorter events, 0.0 us)
Async XLA Ops:
  6.5 22.5 %copy-start = (bf16[256,1024]{1,0:T(8,128)(2,1)S(1)}, bf16[256,1024]{1,0:T(8,128)(2,1)}, u32[]{:S(2)}) copy-start(bf16[256,1024]{1,0:T(8,128)(2,1)} %f_ref) | copy-start | bytes 1572868
  6.5 103.4 %all-gather.2.cloned.1.call-start = ((), (), s32[]{:S(2)}) async-start(), calls=%async_computation.3 | async-start | bytes 8454144 | tf_op jit(solution)/shard_map/all_gather | solution.py:246
  7.3 1.0 copy-start.1
  8.2 19.6 %copy-start.3 = (s32[128]{0:T(128)S(1)}, s32[128]{0:T(128)}, u32[]{:S(2)}) copy-start(s32[128]{0:T(128)} %length_ref) | copy-start | bytes 1540
  9.4 35.4 %all-to-all-start = ((bf16[128,5,2,128]{3,2,1,0:T(2,128)(2,1)}), bf16[128,5,2,128]{3,2,1,0:T(2,128)(2,1)S(1)}, u32[]{:S(2)}, u32[]{:S(2)}) async-start(bf16[128,5,2,128]{3,2,1,0:T(2,128)(2,1)} %bitcast.1), calls=%async_computation | async-start | bytes 655360 | tf_op jit(solution)/shard_map/all_to_all | solution.py:195
  29.4 42.4 %copy-start.2 = (bf16[160,1,1024]{2,0,1:T(8,128)(2,1)S(1)}, bf16[160,1,1024]{2,0,1:T(8,128)(2,1)}, u32[]{:S(2)}) copy-start(bf16[160,1,1024]{2,0,1:T(8,128)(2,1)} %param.7) | copy-start | bytes 983044
Sparse Core Ops, SparseCore 0:
  10.5 99.4 all-gather.1

commit v10 on v9

--- a/solution.py
+++ b/solution.py
@@ -148,39 +148,35 @@
             out_ref[q, HEAD:, cols] = tail
 
 
-def product_kernel(rows_ref, w_ref, out_ref, total):
-    step = pl.program_id(0)
-    term = lax.dot_general(w_ref[...], rows_ref[0], (((1,), (1,)), ((), ())), preferred_element_type=F32)
-
-    @pl.when(step == 0)
-    def _():
-        total[...] = term
-
-    @pl.when(step > 0)
-    def _():
-        total[...] += term
-
-    @pl.when(step == pl.num_programs(0) - 1)
-    def _():
-        for j in range(total.shape[0] // LANES):
-            cols = slice(j * LANES, (j + 1) * LANES)
-            out_ref[:, cols] = total[cols, :].T.astype(BF16)
+def product_kernel(rows_ref, table_ref, out_ref, held, sems):
+    blocks, size, _ = held.shape
+    groups, _, width = rows_ref.shape
+    copies = [
+        pltpu.make_async_copy(table_ref.at[pl.ds(j * size, size)], held.at[j], sems.at[j]) for j in range(blocks)
+    ]
+    for copy in copies:
+        copy.start()
+    for j in range(blocks):
+        copies[j].wait()
+        total = jnp.zeros((size, ROWS), F32)
+        for q in range(groups):
+            part = held[j, :, q * width : (q + 1) * width]
+            total += lax.dot_general(part, rows_ref[q], (((1,), (1,)), ((), ())), preferred_element_type=F32)
+        out_ref[:, j * size : (j + 1) * size] = total.T.astype(BF16)
 
 
 def product(rows, table):
-    block = 512
-    count, wide = rows.shape[1], table.shape[0]
-    parts = rows.shape[2] // block
+    blocks = 4
+    count, (wide, depth) = rows.shape[1], table.shape
     return pl.pallas_call(
         product_kernel,
         out_shape=jax.ShapeDtypeStruct((count, wide), BF16),
-        grid=(table.shape[1] // block,),
-        in_specs=[
-            pl.BlockSpec((1, count, block), lambda k: (k // parts, 0, k % parts)),
-            pl.BlockSpec((wide, block), lambda k: (0, k)),
+        in_specs=[full(rows.shape), pl.BlockSpec(memory_space=pltpu.HBM)],
+        out_specs=full((count, wide)),
+        scratch_shapes=[
+            pltpu.VMEM((blocks, wide // blocks, depth), BF16),
+            pltpu.SemaphoreType.DMA((blocks,)),
         ],
-        out_specs=pl.BlockSpec((count, wide), lambda k: (0, 0)),
-        scratch_shapes=[pltpu.VMEM((wide, count), F32)],
         compiler_params=pltpu.CompilerParams(vmem_limit_bytes=VMEM_LIMIT),
         cost_estimate=pl.CostEstimate(
             flops=2 * count * table.size,

time: 126 us -> 125 us (level)
  Pallas kernels: 16.2 us -> 14.9 us
    pallas_call x1, Pallas kernels: 8.92 us -> 7.58 us  [product(): pl.pallas_call(product_kernel, out_shape=jax.ShapeDtypeStruct((count, wid...]
where the time goes in v10:
time: 125 us; the launch traced here: 124 us
  blocking collectives  42.8 us (34%)
  waiting for transfers between devices  32.6 us (26%)
  starting transfers between devices  18.4 us (15%)
  Pallas kernels  14.9 us (12%)
  between operations  13.5 us (11%)
  local copies, waits for them, and re-layouts  1.86 us (1%)
    all_to_all x1, blocking collectives, exchange(): got = lax.all_to_all(sent, SEQ, split_axis=0, concat_axis=0, tiled=True)  21.6 us
    all_to_all x1, blocking collectives, local(): lax.all_to_all(copies, 'chan', split_axis=0, concat_axis=0, tiled=True)  21.2 us
    all_to_all x1, starting transfers between devices, exchange(): got = lax.all_to_all(sent, SEQ, split_axis=0, concat_axis=0, tiled=True)  18.4 us
    all_gather x1, waiting for transfers between devices, gather_columns(): return lax.all_gather(shard, SEQ, axis=0, tiled=True)  16.6 us
    all_to_all x1, waiting for transfers between devices, exchange(): got = lax.all_to_all(sent, SEQ, split_axis=0, concat_axis=0, tiled=True)  15.4 us
    pallas_call x1, Pallas kernels, product(): pl.pallas_call(product_kernel, out_shape=jax.ShapeDtypeStruct((count, wid...  7.58 us
    pallas_call x4, Pallas kernels, call(): pl.pallas_call(kernel, out_shape=out, in_specs=in_specs, out_specs=full(o...  7.3 us
  transfers between devices with their start and end apart: 2, of which 2 were waited for; matrix products, arithmetic and copies ran while one was open for 1% of the time, Pallas kernels for 6%

profile of v10, /device:TPU:1, one launch (start us, length us, event | category | flops | bytes accessed | tf_op | source)
XLA Modules:
  0.0 124.4 jit_solution(13033931491949218224)
XLA Ops:
  6.5 0.0 copy-start
  6.5 0.0 all-gather.2.cloned.1.call-start
  6.5 0.7 all-gather.2.cloned.1.call-update
  7.3 0.0 copy-start.1
  7.3 1.0 copy-done.1
  8.2 0.0 copy-start.3
  8.2 1.1 shard_map.64
  9.4 18.4 %all-to-all-start = ((bf16[128,5,2,128]{3,2,1,0:T(2,128)(2,1)}), bf16[128,5,2,128]{3,2,1,0:T(2,128)(2,1)S(1)}, u32[]{:S(2)}, u32[]{:S(2)}) async-start(bf16[128,5,2,128]{3,2,1,0:T(2,128)(2,1)} %bitcast.1), calls=%async_computation | async-start | bytes 655360 | tf_op jit(solution)/shard_map/all_to_all | solution.py:191
  27.8 0.0 copy-done.3
  27.8 0.1 copy.8
  27.9 0.2 reduce-window.9
  28.1 0.1 reduce
  28.2 0.8 dynamic_slice.3.skip_ref
  29.0 0.0 copy-done
  29.0 0.4 shard_map.65.toep_ref
  29.4 0.0 copy-start.2
  29.4 15.4 %all-to-all-done = bf16[128,5,2,128]{3,2,1,0:T(2,128)(2,1)S(1)} async-done(((bf16[128,5,2,128]{3,2,1,0:T(2,128)(2,1)}), bf16[128,5,2,128]{3,2,1,0:T(2,128)(2,1)S(1)}, u32[]{:S(2)}, u32[]{:S(2)}) %all-to-all-start) | async-done | bytes 327712 | tf_op jit(solution)/shard_map/all_to_all | solution.py:191
  44.7 5.4 %shard_map.66 = bf16[1280,128]{1,0:T(8,128)(2,1)S(1)} custom-call(s32[128]{0:T(128)S(1)} %sub.3.start_ref, s32[128]{0:T(128)S(1)} %copy-done.3, f32[8]{0:T(128)S(1)} %dynamic_slice.3.skip_ref, bf16[1280,128]{1,0:T(8,128)(2,1)S(1)} %bitcast.10, bf16[8,256,256]{2,1,0:T(8,128)(2,1)S(1)} %shard_map.65.toep_ref), custom_call_target="tpu_custom_call" | custom-call | flops 134217728 | bytes 1704992 | tf_op jit(solution)/shard_map/pallas_call | solution.py:34
  50.1 21.6 %all_to_all.15 = bf16[128,5,2,128]{3,2,1,0:T(2,128)(2,1)S(1)} all-to-all(bf16[128,5,2,128]{3,2,1,0:T(2,128)(2,1)S(1)} %bitcast.11), channel_id=1, replica_groups=mesh['z'=8,'y'=8,'core'=2,'chan'=4] {'z','y','core'}, dimensions={0} | all-to-all | bytes 655360 | tf_op jit(solution)/shard_map/all_to_all | solution.py:191
  71.7 0.0 copy-done.2
  71.7 0.4 shard_map.67
  72.1 21.2 %all_to_all.16.rows_ref = bf16[4,160,1024]{2,1,0:T(8,128)(2,1)S(1)} all-to-all(bf16[4,160,1024]{2,1,0:T(8,128)(2,1)S(1)} %shard_map.67), channel_id=1, replica_groups=mesh['z'=8,'y'=8,'core'=2,'chan'=4] {'chan'}, dimensions={0} | all-to-all | bytes 2621440 | tf_op jit(solution)/shard_map/all_to_all | solution.py:236
  93.3 16.6 %all-gather.2.cloned.1.call-done.table_ref = bf16[1024,4096]{1,0:T(8,128)(2,1)} async-done(((bf16[8,4096]{1,0:T(8,128)(2,1)}), bf16[1024,4096]{1,0:T(8,128)(2,1)}) %all-gather.2.cloned.1.call-update) | async-done | bytes 8388624 | tf_op jit(solution)/shard_map/all_gather | solution.py:242
  109.9 7.6 %shard_map.68 = bf16[160,1024]{1,0:T(8,128)(2,1)} custom-call(bf16[4,160,1024]{2,1,0:T(8,128)(2,1)S(1)} %all_to_all.16.rows_ref, bf16[1024,4096]{1,0:T(8,128)(2,1)} %all-gather.2.cloned.1.call-done.table_ref), custom_call_target="tpu_custom_call" | custom-call | flops 1342177280 | bytes 10027008 | tf_op jit(solution)/shard_map/pallas_call | solution.py:171
  (1 shorter events, 0.0 us)
Async XLA Ops:
  6.5 22.5 %copy-start = (bf16[256,1024]{1,0:T(8,128)(2,1)S(1)}, bf16[256,1024]{1,0:T(8,128)(2,1)}, u32[]{:S(2)}) copy-start(bf16[256,1024]{1,0:T(8,128)(2,1)} %f_ref) | copy-start | bytes 1572868
  6.5 103.4 %all-gather.2.cloned.1.call-start = ((), (), s32[]{:S(2)}) async-start(), calls=%async_computation.3 | async-start | bytes 8454144 | tf_op jit(solution)/shard_map/all_gather | solution.py:242
  7.3 1.0 copy-start.1
  8.2 19.6 %copy-start.3 = (s32[128]{0:T(128)S(1)}, s32[128]{0:T(128)}, u32[]{:S(2)}) copy-start(s32[128]{0:T(128)} %length_ref) | copy-start | bytes 1540
  9.4 35.4 %all-to-all-start = ((bf16[128,5,2,128]{3,2,1,0:T(2,128)(2,1)}), bf16[128,5,2,128]{3,2,1,0:T(2,128)(2,1)S(1)}, u32[]{:S(2)}, u32[]{:S(2)}) async-start(bf16[128,5,2,128]{3,2,1,0:T(2,128)(2,1)} %bitcast.1), calls=%async_computation | async-start | bytes 655360 | tf_op jit(solution)/shard_map/all_to_all | solution.py:191
  29.4 42.3 %copy-start.2 = (bf16[160,1,1024]{2,0,1:T(8,128)(2,1)S(1)}, bf16[160,1,1024]{2,0,1:T(8,128)(2,1)}, u32[]{:S(2)}) copy-start(bf16[160,1,1024]{2,0,1:T(8,128)(2,1)} %param.7) | copy-start | bytes 983044
Sparse Core Ops, SparseCore 0:
  10.5 99.3 all-gather.1

commit v11 on v4

--- a/solution.py
+++ b/solution.py
@@ -168,7 +168,7 @@
 
 
 def product(rows, table, near):
-    block = 256
+    block = 512
     return pl.pallas_call(
         functools.partial(product_kernel, near),
         out_shape=jax.ShapeDtypeStruct((ROWS, table.shape[0]), BF16),

time: 124 us -> 123 us (level)
  no operation moved by 1% of the time
where the time goes in v11:
time: 123 us; the launch traced here: 122 us
  blocking collectives  42.8 us (35%)
  waiting for transfers between devices  32.7 us (27%)
  starting transfers between devices  18.4 us (15%)
  between operations  13.5 us (11%)
  Pallas kernels  12.8 us (10%)
  local copies, waits for them, and re-layouts  1.86 us (2%)
    all_to_all x1, blocking collectives, exchange(): got = lax.all_to_all(sent, SEQ, split_axis=0, concat_axis=0, tiled=True)  21.6 us
    all_to_all x1, blocking collectives, local(): lax.all_to_all(copies, 'chan', split_axis=0, concat_axis=0, tiled=True)  21.2 us
    all_to_all x1, starting transfers between devices, exchange(): got = lax.all_to_all(sent, SEQ, split_axis=0, concat_axis=0, tiled=True)  18.4 us
    all_gather x1, waiting for transfers between devices, gather_columns(): return lax.all_gather(shard, ('z', 'y_far', 'core'), axis=0, tiled=True)  16.6 us
    all_to_all x1, waiting for transfers between devices, exchange(): got = lax.all_to_all(sent, SEQ, split_axis=0, concat_axis=0, tiled=True)  15.4 us
    pallas_call x4, Pallas kernels, call(): pl.pallas_call(kernel, out_shape=out, in_specs=in_specs, out_specs=full(o...  7.3 us
    pallas_call x1, Pallas kernels, product(): pl.pallas_call(functools.partial(product_kernel, near), out_shape=jax.Sha...  5.52 us
  transfers between devices with their start and end apart: 2, of which 2 were waited for; matrix products, arithmetic and copies ran while one was open for 1% of the time, Pallas kernels for 6%

profile of v11, /device:TPU:1, one launch (start us, length us, event | category | flops | bytes accessed | tf_op | source)
XLA Modules:
  0.0 122.3 jit_solution(11063228716385769511)
XLA Ops:
  6.5 0.0 copy-start
  6.5 0.0 all-gather.2.cloned.1.call-start
  6.5 0.7 all-gather.2.cloned.1.call-update
  7.3 0.0 copy-start.1
  7.3 1.0 copy-done.1
  8.2 0.0 copy-start.3
  8.2 1.1 shard_map.64
  9.4 18.4 %all-to-all-start = ((bf16[128,5,2,128]{3,2,1,0:T(2,128)(2,1)}), bf16[128,5,2,128]{3,2,1,0:T(2,128)(2,1)S(1)}, u32[]{:S(2)}, u32[]{:S(2)}) async-start(bf16[128,5,2,128]{3,2,1,0:T(2,128)(2,1)} %bitcast.1), calls=%async_computation | async-start | bytes 655360 | tf_op jit(solution)/shard_map/all_to_all | solution.py:192
  27.8 0.0 copy-done.3
  27.8 0.1 copy.8
  27.9 0.2 reduce-window.9
  28.1 0.1 reduce
  28.2 0.8 dynamic_slice.3.skip_ref
  29.0 0.0 copy-done
  29.0 0.4 shard_map.65.toep_ref
  29.4 0.0 copy-start.2
  29.4 15.4 %all-to-all-done = bf16[128,5,2,128]{3,2,1,0:T(2,128)(2,1)S(1)} async-done(((bf16[128,5,2,128]{3,2,1,0:T(2,128)(2,1)}), bf16[128,5,2,128]{3,2,1,0:T(2,128)(2,1)S(1)}, u32[]{:S(2)}, u32[]{:S(2)}) %all-to-all-start) | async-done | bytes 327712 | tf_op jit(solution)/shard_map/all_to_all | solution.py:192
  44.7 5.4 %shard_map.66 = bf16[1280,128]{1,0:T(8,128)(2,1)S(1)} custom-call(s32[128]{0:T(128)S(1)} %sub.3.start_ref, s32[128]{0:T(128)S(1)} %copy-done.3, f32[8]{0:T(128)S(1)} %dynamic_slice.3.skip_ref, bf16[1280,128]{1,0:T(8,128)(2,1)S(1)} %bitcast.10, bf16[8,256,256]{2,1,0:T(8,128)(2,1)S(1)} %shard_map.65.toep_ref), custom_call_target="tpu_custom_call" | custom-call | flops 134217728 | bytes 1704992 | tf_op jit(solution)/shard_map/pallas_call | solution.py:37
  50.1 21.6 %all_to_all.15 = bf16[128,5,2,128]{3,2,1,0:T(2,128)(2,1)S(1)} all-to-all(bf16[128,5,2,128]{3,2,1,0:T(2,128)(2,1)S(1)} %bitcast.11), channel_id=1, replica_groups=mesh['z'=8,'y_far'=8,'y_near'=1,'core'=2,'chan'=4] {'z','y_far','y_near'..., dimensions={0} | all-to-all | bytes 655360 | tf_op jit(solution)/shard_map/all_to_all | solution.py:192
  71.7 0.0 copy-done.2
  71.7 0.4 shard_map.67
  72.1 21.2 %all_to_all.16.rows_ref = bf16[4,160,1024]{2,1,0:T(8,128)(2,1)S(1)} all-to-all(bf16[4,160,1024]{2,1,0:T(8,128)(2,1)S(1)} %shard_map.67), channel_id=1, replica_groups=mesh['z'=8,'y_far'=8,'y_near'=1,'core'=2,'chan'=4] {'chan'}, dimensions={0} | all-to-all | bytes 2621440 | tf_op jit(solution)/shard_map/all_to_all | solution.py:237
  93.4 16.6 %all-gather.2.cloned.1.call-done.w_ref = bf16[1024,4096]{1,0:T(8,128)(2,1)} async-done(((bf16[8,4096]{1,0:T(8,128)(2,1)}), bf16[1024,4096]{1,0:T(8,128)(2,1)}) %all-gather.2.cloned.1.call-update) | async-done | bytes 8388624 | tf_op jit(solution)/shard_map/all_gather | solution.py:243
  109.9 5.5 %shard_map.68 = bf16[160,1024]{1,0:T(8,128)(2,1)} custom-call(bf16[4,160,1024]{2,1,0:T(8,128)(2,1)S(1)} %all_to_all.16.rows_ref, bf16[1024,4096]{1,0:T(8,128)(2,1)} %all-gather.2.cloned.1.call-done.w_ref), custom_call_target="tpu_custom_call" | custom-call | flops 1342177280 | bytes 10027008 | tf_op jit(solution)/shard_map/pallas_call | solution.py:172
  (1 shorter events, 0.0 us)
Async XLA Ops:
  6.5 22.5 %copy-start = (bf16[256,1024]{1,0:T(8,128)(2,1)S(1)}, bf16[256,1024]{1,0:T(8,128)(2,1)}, u32[]{:S(2)}) copy-start(bf16[256,1024]{1,0:T(8,128)(2,1)} %f_ref) | copy-start | bytes 1572868
  6.5 103.4 %all-gather.2.cloned.1.call-start = ((), (), s32[]{:S(2)}) async-start(), calls=%async_computation.3 | async-start | bytes 8454144 | tf_op jit(solution)/shard_map/all_gather | solution.py:243
  7.3 1.0 copy-start.1
  8.2 19.6 %copy-start.3 = (s32[128]{0:T(128)S(1)}, s32[128]{0:T(128)}, u32[]{:S(2)}) copy-start(s32[128]{0:T(128)} %length_ref) | copy-start | bytes 1540
  9.4 35.4 %all-to-all-start = ((bf16[128,5,2,128]{3,2,1,0:T(2,128)(2,1)}), bf16[128,5,2,128]{3,2,1,0:T(2,128)(2,1)S(1)}, u32[]{:S(2)}, u32[]{:S(2)}) async-start(bf16[128,5,2,128]{3,2,1,0:T(2,128)(2,1)} %bitcast.1), calls=%async_computation | async-start | bytes 655360 | tf_op jit(solution)/shard_map/all_to_all | solution.py:192
  29.4 42.3 %copy-start.2 = (bf16[160,1,1024]{2,0,1:T(8,128)(2,1)S(1)}, bf16[160,1,1024]{2,0,1:T(8,128)(2,1)}, u32[]{:S(2)}) copy-start(bf16[160,1,1024]{2,0,1:T(8,128)(2,1)} %param.7) | copy-start | bytes 983044
Sparse Core Ops, SparseCore 0:
  10.5 99.4 all-gather.1
